TPU v7x, 32 devices: a whole 2x2x4 slice. The times are simulated.
32 devices in a mesh: blk: 8 (over z, x), ma: 4 (over y, core).
Axes of the slice: x: 2, y: 2, z: 4, core: 2. Of those that a mesh axis runs over, the one named last changes fastest.
Arguments:
- weights: bfloat16 [32, 32, 8, 4, 128], P(('blk', 'ma')), may hold values from 0.099609375 to 0.3984375
- offsets: int32 [32, 32, 8, 128], P(('blk', 'ma')), may hold values from 0 to 127
- counts: int32 [32, 32], P(('blk', 'ma')), may hold values from 1 to 8, 144 in all within a row
- block_ids: int32 [32, 32, 8], P(('blk', 'ma')), may hold values from 0 to 127
- m_table: int32 [384], replicated, may hold values from 0 to 383, as said below
- legendre: bfloat16 [384, 1664, 128], P(('blk', 'ma')), as said below
Outputs:
- kappa_band: float32 [4, 128, 4096], P(None, ('blk', 'ma'))
- potential: float32 [4, 128, 4096], P(None, ('blk', 'ma'))
Inputs may be any that keep to these rules, and one draw needn't show every extreme that they name: Groups with index below counts[d, e] are live, the others hold no particles; each row sums to (8 + 1) * 32 // 2 and reaches 8. `m_table`: a permutation of 0 to 383. legendre[j, l, q] is zero for every l below m_table[j].
All inputs are finite; a program needn't handle non-finite values.
Results may differ from a plain program's by a relative error of at most 0.0058.
Values may be sent and summed in bfloat16 or wider, within the bound.
No kernel may reach another device: no remote copies, remote signals or barrier semaphores. Data moves between devices by JAX's collectives and lax.ppermute only.
A program may use at most 128 MiB of HBM per device.

v0:
```python
import math

import jax
import jax.numpy as jnp
from jax import lax
from jax.sharding import PartitionSpec as P

NPHI = 4096


highest = lax.Precision.HIGHEST


def split_length(length):
    factor = 1
    for candidate in range(1, math.isqrt(length) + 1):
        if length % candidate == 0:
            factor = candidate
    return (factor, length // factor)


def phase_table(row_count, col_count, period):
    row_index = lax.broadcasted_iota(jnp.int32, (row_count, col_count), 0)
    col_index = lax.broadcasted_iota(jnp.int32, (row_count, col_count), 1)
    angles = (row_index * col_index % period).astype(jnp.float32) * (2.0 * jnp.pi / period)
    return (jnp.cos(angles), jnp.sin(angles))


def forward_dft(signal, length):
    first, second = split_length(length)
    row_count = signal.shape[0]
    cube = signal.reshape(row_count, first, second)
    cos_first, sin_first = phase_table(first, first, first)
    section_real = jnp.einsum("rks,km->rms", cube, cos_first, precision=highest)
    section_imag = -jnp.einsum("rks,km->rms", cube, sin_first, precision=highest)
    twist_c, twist_s = phase_table(first, second, length)
    turned_real = section_real * twist_c + section_imag * twist_s
    turned_imag = section_imag * twist_c - section_real * twist_s
    cos_second, sin_second = phase_table(second, second, second)
    out_real = jnp.einsum("rms,sn->rnm", turned_real, cos_second, precision=highest) + jnp.einsum(
        "rms,sn->rnm", turned_imag, sin_second, precision=highest
    )
    out_imag = jnp.einsum("rms,sn->rnm", turned_imag, cos_second, precision=highest) - jnp.einsum(
        "rms,sn->rnm", turned_real, sin_second, precision=highest
    )
    return (out_real.reshape(row_count, length), out_imag.reshape(row_count, length))


def inverse_real(spec_real, spec_imag, length):
    first, second = split_length(length)
    row_count = spec_real.shape[0]
    grid_real = spec_real.reshape(row_count, second, first)
    grid_imag = spec_imag.reshape(row_count, second, first)
    cos_second, sin_second = phase_table(second, second, second)
    section_real = jnp.einsum("rnm,ns->rms", grid_real, cos_second, precision=highest) - jnp.einsum(
        "rnm,ns->rms", grid_imag, sin_second, precision=highest
    )
    section_imag = jnp.einsum("rnm,ns->rms", grid_imag, cos_second, precision=highest) + jnp.einsum(
        "rnm,ns->rms", grid_real, sin_second, precision=highest
    )
    twist_c, twist_s = phase_table(first, second, length)
    turned_real = section_real * twist_c - section_imag * twist_s
    turned_imag = section_real * twist_s + section_imag * twist_c
    cos_first, sin_first = phase_table(first, first, first)
    result = jnp.einsum("rms,mk->rks", turned_real, cos_first, precision=highest) - jnp.einsum(
        "rms,mk->rks", turned_imag, sin_first, precision=highest
    )
    return result.reshape(row_count, length)


def per_device(weights, offsets, counts, block_ids, m_table, legendre):
    band_count = lax.axis_size("blk")
    mode_groups = lax.axis_size("ma")
    devices = band_count * mode_groups
    device = lax.axis_index("blk") * mode_groups + lax.axis_index("ma")
    groups = weights[0]
    capacity = groups.shape[1]
    bin_count = groups.shape[2]
    cycle_length = NPHI
    cycles_here = legendre.shape[2] // devices
    blocks_here = cycles_here * cycle_length // 128
    slots_here = legendre.shape[0]
    live_mask = lax.broadcasted_iota(jnp.int32, (devices, capacity), 1) < counts[0][:, None]
    columns = lax.broadcasted_iota(jnp.int32, (1, 1, 1, 128), 3)
    onehot = (offsets[0][:, :, :, None] == columns).astype(jnp.bfloat16)
    partial_value = jnp.einsum(
        "dcbs,dcsp->dcbp", groups, onehot, preferred_element_type=jnp.float32
    )
    partial_value = jnp.where(live_mask[:, :, None, None], partial_value, 0.0)
    sent_ids = block_ids[0].astype(jnp.float32)
    arrived, arrived_ids = (
        lax.all_to_all(partial_value, ("blk", "ma"), split_axis=0, concat_axis=0, tiled=True),
        lax.all_to_all(sent_ids, ("blk", "ma"), split_axis=0, concat_axis=0, tiled=True),
    )
    received = arrived.reshape(devices * capacity, bin_count * 128)
    slot_ids = arrived_ids.reshape(devices * capacity, 1)
    selector = (slot_ids == lax.broadcasted_iota(jnp.float32, (1, blocks_here), 1)).astype(
        jnp.float32
    )
    counted = jnp.einsum("gl,gq->lq", selector, received, precision=highest)
    convergence = (
        counted.reshape(blocks_here, bin_count, 128)
        .transpose(1, 0, 2)
        .reshape(bin_count * cycles_here, cycle_length)
    )
    mode_count = m_table.shape[0]
    spectrum_real, spectrum_imag = forward_dft(convergence, cycle_length)
    real_part = jnp.take(spectrum_real, m_table, axis=1)
    imag_part = jnp.take(spectrum_imag, m_table, axis=1)
    parity = (device * cycles_here + lax.broadcasted_iota(jnp.int32, (cycles_here, 1), 0)) % 2
    twists = (m_table[None, :] * parity).astype(jnp.float32) * (jnp.pi / cycle_length)
    twist_cos = jnp.cos(twists)
    twist_sin = jnp.sin(twists)
    real_part = (real_part / cycle_length).reshape(bin_count, cycles_here, mode_count)
    imag_part = (imag_part / cycle_length).reshape(bin_count, cycles_here, mode_count)
    real_turned = real_part * twist_cos + imag_part * twist_sin
    imag_turned = imag_part * twist_cos - real_part * twist_sin
    coefficients = jnp.stack([real_turned, imag_turned], axis=2).astype(jnp.bfloat16)
    by_owner = coefficients.reshape(bin_count, cycles_here, 2, devices, slots_here)
    outgoing = by_owner.transpose(3, 4, 0, 2, 1)
    mode_rows = lax.all_to_all(outgoing, ("blk", "ma"), split_axis=0, concat_axis=4, tiled=True)[0]
    harmonic = jnp.einsum("jlr,jbcr->jbcl", legendre, mode_rows, preferred_element_type=jnp.float32)
    degrees = lax.broadcasted_iota(jnp.float32, (1, 1, 1, legendre.shape[1]), 3)
    filter_gain = jnp.where(
        degrees > 0.5, -20000.0 / jnp.maximum(degrees * (degrees + 1.0), 1.0), 0.0
    )
    filtered = jnp.stack([harmonic, harmonic * filter_gain], axis=1).astype(jnp.bfloat16)
    synthesis = jnp.einsum(
        "jlr,jfbcl->jfbcr", legendre, filtered, preferred_element_type=jnp.float32
    ).astype(jnp.bfloat16)
    outgoing_maps = synthesis.reshape(slots_here, 2, bin_count, 2, devices, cycles_here)
    mode_weight = jnp.where(m_table == 0, 1.0, 2.0).astype(jnp.float32)
    turn_cos = jnp.transpose(twist_cos)[:, None, None, :]
    turn_sin = jnp.transpose(twist_sin)[:, None, None, :]
    mode_scale = mode_weight[:, None, None, None]
    values = lax.all_to_all(outgoing_maps, ("blk", "ma"), split_axis=4, concat_axis=0, tiled=True)[
        :, :, :, :, 0, :
    ].astype(jnp.float32)
    real_in = values[:, :, :, 0, :]
    imag_in = values[:, :, :, 1, :]
    real_out = (real_in * turn_cos - imag_in * turn_sin) * mode_scale
    imag_out = (real_in * turn_sin + imag_in * turn_cos) * mode_scale
    item_count = values.shape[1]
    flat_real = jnp.transpose(real_out.reshape(mode_count, -1))
    flat_imag = jnp.transpose(imag_out.reshape(mode_count, -1))
    row_total = flat_real.shape[0]
    full_real = jnp.zeros((row_total, cycle_length), jnp.float32).at[:, m_table].set(flat_real)
    full_imag = jnp.zeros((row_total, cycle_length), jnp.float32).at[:, m_table].set(flat_imag)
    maps_out = inverse_real(full_real, full_imag, cycle_length)
    sky_maps = maps_out.reshape(item_count, bin_count, cycles_here, cycle_length)
    return (sky_maps[0], sky_maps[1])


def solution(mesh):
    placed = (
        P(("blk", "ma"), None, None, None, None),
        P(("blk", "ma"), None, None, None),
        P(("blk", "ma"), None),
        P(("blk", "ma"), None, None),
        P(),
        P(("blk", "ma"), None, None),
    )
    return jax.shard_map(
        per_device,
        mesh=mesh,
        in_specs=placed,
        out_specs=(P(None, ("blk", "ma"), None), P(None, ("blk", "ma"), None)),
        check_vma=False,
    )
```

profile of v0, /device:TPU:0, one launch (start us, length us, event | category | flops | bytes accessed | tf_op | source)
XLA Modules:
  0.0 108.4 jit_solution(14818198983309111806)
XLA Ops:
  0.6 0.8 copy.109
  1.4 0.6 convert_element_type.110
  2.1 7.3 %all-to-all-start = ((f32[32,1,8]{2,1,0:T(1,128)}), f32[32,1,8]{2,1,0:T(1,128)S(1)}, u32[]{:S(2)}, u32[]{:S(2)}) async-start(f32[32,1,8]{2,1,0:T(1,128)} %bitcast.1), calls=%async_computation | async-start | bytes 32768 | tf_op jit(solution)/shard_map/all_to_all | solution.py:93
  9.5 0.7 iota_compare_fusion.8
  10.2 8.7 %fusion.13 = f32[32,8,4,128]{3,2,1,0:T(4,128)} fusion(s32[32,8,128]{2,1,0:T(8,128)} %bitcast.150, bf16[1,32,8,4,128]{4,3,2,1,0:T(4,128)(2,1)S(1)} %copy-done, pred[32,8]{1,0:T(8,128)(4,1)S(1)} %iota_compare_fusion.8), kind=kOutput, calls=%fused_computation.23 | convolution fusion | flops 37879808 | bytes 917760 | tf_op jit(solution)/shard_map/dcbs,dcsp->dcbp/dot_general | solution.py:86
  19.1 5.8 %all-to-all-start.1 = ((f32[32,8,4,128]{3,2,1,0:T(4,128)}), f32[32,8,4,128]{3,2,1,0:T(4,128)S(1)}, u32[]{:S(2)}, u32[]{:S(2)}) async-start(f32[32,8,4,128]{3,2,1,0:T(4,128)} %fusion.13), calls=%async_computation.1 | async-start | bytes 1048576 | tf_op jit(solution)/shard_map/all_to_all | solution.py:92
  25.2 0.6 copy-done.4
  25.8 0.6 compare_and_fusion
  26.4 0.7 fusion.88
  27.1 0.9 fusion.41
  28.1 0.5 broadcast.433
  28.5 0.6 reduce.3
  29.2 11.2 %all-to-all-done.1 = f32[32,8,4,128]{3,2,1,0:T(4,128)S(1)} async-done(((f32[32,8,4,128]{3,2,1,0:T(4,128)}), f32[32,8,4,128]{3,2,1,0:T(4,128)S(1)}, u32[]{:S(2)}, u32[]{:S(2)}) %all-to-all-start.1) | async-done | bytes 524320 | tf_op jit(solution)/shard_map/all_to_all | solution.py:92
  40.7 0.4 convolution_bitcast_fusion
  41.3 0.7 convolution_negate_fusion
  42.0 0.7 fusion.60
  42.7 1.7 %fusion.26 = f32[64,16,64]{2,0,1:T(8,128)S(1)} fusion(f32[64,16,64]{2,0,1:T(8,128)S(1)} %fusion.60, f32[64,16,64]{2,0,1:T(8,128)S(1)} %convolution_negate_fusion, f32[64,64]{1,0:T(8,128)S(1)} %copy.112, f32[64,64]{1,0:T(8,128)S(1)} %copy.111), kind=kOutput, calls=%fused_computation.40 | convolution fusion | flops 50585600 | bytes 819200 | tf_op jit(solution)/shard_map/rms,sn->rnm/dot_general | solution.py:43
  44.5 1.7 %fusion.30 = f32[64,16,64]{2,0,1:T(8,128)S(1)} fusion(f32[64,16,64]{2,0,1:T(8,128)S(1)} %convolution_negate_fusion, f32[64,16,64]{2,0,1:T(8,128)S(1)} %fusion.60, f32[64,64]{1,0:T(8,128)S(1)} %copy.112, f32[64,64]{1,0:T(8,128)S(1)} %copy.111), kind=kOutput, calls=%fused_computation.44 | convolution fusion | flops 50585600 | bytes 819200 | tf_op jit(solution)/shard_map/rms,sn->rnm/dot_general | solution.py:40
  46.2 1.7 %fusion.7 = f32[16,64,64]{2,1,0:T(8,128)S(1)} fusion(f32[64,16,64]{2,0,1:T(8,128)S(1)} %fusion.26, f32[64,16,64]{2,0,1:T(8,128)S(1)} %convolution_negate_fusion, f32[64,16,64]{2,0,1:T(8,128)S(1)} %fusion.60, f32[64,64]{1,0:T(8,128)S(1)} %copy.112, f32[64,64]{1,0:T(8,128)S(1)} %copy.111), kind=kOutput, calls=%fused_computation.17 | convolution fusion | flops 50651136 | bytes 1081344 | tf_op jit(solution)/shard_map/rms,sn->rnm/dot_general | solution.py:43
  47.9 1.7 %fusion.8 = f32[16,64,64]{2,1,0:T(8,128)S(1)} fusion(f32[64,16,64]{2,0,1:T(8,128)S(1)} %fusion.30, f32[64,16,64]{2,0,1:T(8,128)S(1)} %fusion.60, f32[64,16,64]{2,0,1:T(8,128)S(1)} %convolution_negate_fusion, f32[64,64]{1,0:T(8,128)S(1)} %copy.112, f32[64,64]{1,0:T(8,128)S(1)} %copy.111), kind=kOutput, calls=%fused_computation.19 | convolution fusion | flops 50651136 | bytes 1081344 | tf_op jit(solution)/shard_map/rms,sn->rnm/dot_general | solution.py:40
  49.6 0.6 copy.142
  50.3 1.1 %gather_fusion = f32[384,16]{1,0:T(8,128)S(1)} fusion(f32[16,4096]{0,1:T(8,128)S(1)} %bitcast.142, s32[1024]{0:T(1024)S(1)} %pad_clamp_fusion), kind=kCustom, calls=%fused_computation.clone | custom fusion | bytes 50688 | tf_op jit(solution)/shard_map/jit(_take)/gather | solution.py:108
  51.5 0.7 copy.143
  52.2 1.1 %gather_fusion.1 = f32[384,16]{1,0:T(8,128)S(1)} fusion(f32[16,4096]{0,1:T(8,128)S(1)} %bitcast.141, s32[1024]{0:T(1024)S(1)} %pad_clamp_fusion), kind=kCustom, calls=%fused_computation.1.clone | custom fusion | bytes 50688 | tf_op jit(solution)/shard_map/jit(_take)/gather | solution.py:109
  54.3 0.9 reshape.411
  55.2 3.3 %all-to-all-start.2 = ((bf16[32,2,192]{2,1,0:T(2,128)(2,1)}), bf16[32,2,192]{2,1,0:T(2,128)(2,1)S(1)}, u32[]{:S(2)}, u32[]{:S(2)}) async-start(bf16[32,2,192]{2,1,0:T(2,128)(2,1)} %reshape.411), calls=%async_computation.2 | async-start | bytes 65536 | tf_op jit(solution)/shard_map/all_to_all | solution.py:121
  58.5 7.1 %all-to-all-done.2 = bf16[32,2,192]{2,1,0:T(2,128)(2,1)S(1)} async-done(((bf16[32,2,192]{2,1,0:T(2,128)(2,1)}), bf16[32,2,192]{2,1,0:T(2,128)(2,1)S(1)}, u32[]{:S(2)}, u32[]{:S(2)}) %all-to-all-start.2) | async-done | bytes 24608 | tf_op jit(solution)/shard_map/all_to_all | solution.py:121
  66.3 4.0 %convert_bitcast_fusion.1 = (bf16[12,1,4,2,1664]{4,2,3,0,1:T(4,128)(2,1)S(1)}, bf16[12,1,4,2,1664]{4,2,3,0,1:T(4,128)(2,1)S(1)}) fusion(f32[1664]{0:T(1024)S(1)} %fusion.87, bf16[12,4,2,128]{3,1,2,0:T(4,128)(2,1)S(1)} %copy.119, bf16[12,1664,128]{2,1,0:T(8,128)(2,1)} %param.13), kind=kOutput, calls=%fused_computation.53 | convolution fusion | flops 41373696 | bytes 5782016 | tf_op jit(solution)/shard_map/jlr,jbcr->jbcl/dot_general | solution.py:122
  70.3 3.6 %fusion.9 = bf16[12,2,4,2,128]{4,2,3,1,0:T(4,128)(2,1)S(1)} fusion(bf16[12,1664,128]{2,1,0:T(8,128)(2,1)} %param.13, bf16[12,1,4,2,1664]{4,2,3,0,1:T(4,128)(2,1)S(1)} %get-tuple-element.8, bf16[12,1,4,2,1664]{4,2,3,0,1:T(4,128)(2,1)S(1)} %get-tuple-element.7), kind=kOutput, calls=%fused_computation.21 | convolution fusion | flops 82132992 | bytes 5799936 | tf_op jit(solution)/shard_map/jlr,jfbcl->jfbcr/dot_general | solution.py:128
  74.5 1.6 %reshape.413 = bf16[32,2,384]{2,1,0:T(2,128)(2,1)} reshape(bf16[32,2,4,2,4,12]{5,4,3,2,1,0:T(4,128)(2,1)S(1)} %bitcast.146) | data formatting | bytes 98304
  76.0 2.6 %all-to-all-start.3 = ((bf16[32,2,384]{2,1,0:T(2,128)(2,1)}), bf16[32,2,384]{2,1,0:T(2,128)(2,1)S(1)}, u32[]{:S(2)}, u32[]{:S(2)}) async-start(bf16[32,2,384]{2,1,0:T(2,128)(2,1)} %reshape.413), calls=%async_computation.3 | async-start | bytes 98304 | tf_op jit(solution)/shard_map/all_to_all | solution.py:136
  78.7 7.2 %all-to-all-done.3 = bf16[32,2,384]{2,1,0:T(2,128)(2,1)S(1)} async-done(((bf16[32,2,384]{2,1,0:T(2,128)(2,1)}), bf16[32,2,384]{2,1,0:T(2,128)(2,1)S(1)}, u32[]{:S(2)}, u32[]{:S(2)}) %all-to-all-start.3) | async-done | bytes 49184 | tf_op jit(solution)/shard_map/all_to_all | solution.py:136
  86.0 1.2 %reshape.414 = bf16[32,2,4,2,4,12]{5,4,3,2,1,0:T(4,128)(2,1)S(1)} reshape(bf16[32,2,384]{2,1,0:T(2,128)(2,1)S(1)} %all-to-all-done.3) | data formatting | bytes 98304
  87.5 0.6 copy.123
  88.1 0.7 reshape.347
  88.9 0.8 copy.124
  89.9 2.1 %scatter_custom_fusion.1 = f32[32,4096]{0,1:T(8,128)S(1)} fusion(s32[384]{0:T(512)} %copy-done.4, f32[384,32]{1,0:T(8,128)S(1)} %copy.127, f32[]{:T(128)} %constant.81.clone.1), kind=kCustom, calls=%fused_computation.32 | custom fusion | bytes 524800 | tf_op jit(solution)/shard_map/scatter | solution.py:148
  91.9 1.5 %copy.128 = f32[32,64,64]{1,2,0:T(8,128)S(1)} copy(f32[32,64,64]{0,2,1:T(8,128)S(1)} %bitcast.140) | data formatting | bytes 1048576 | tf_op jit(solution)/shard_map/reshape | solution.py:53
  93.4 1.1 %fusion.53 = f32[32,64,64]{2,1,0:T(8,128)S(1)} fusion(f32[32,64,64]{1,2,0:T(8,128)S(1)} %copy.128), kind=kOutput, calls=%fused_computation.81 | convolution fusion | flops 100720640 | bytes 1048576 | tf_op jit(solution)/shard_map/rnm,ns->rms/dot_general | solution.py:58
  94.6 3.2 %scatter_custom_fusion = f32[32,4096]{0,1:T(8,128)} fusion(s32[384]{0:T(512)} %copy-done.4, f32[384,32]{1,0:T(8,128)} %copy.124, f32[]{:T(128)} %constant.81.clone.1), kind=kCustom, calls=%fused_computation.34 | custom fusion | bytes 524800 | tf_op jit(solution)/shard_map/scatter | solution.py:147
  97.8 2.9 %copy.125 = f32[32,64,64]{1,2,0:T(8,128)S(1)} copy(f32[32,64,64]{0,2,1:T(8,128)} %bitcast.139) | data formatting | bytes 1048576 | tf_op jit(solution)/shard_map/reshape | solution.py:52
  100.7 1.1 %fusion.55 = f32[32,64,64]{2,1,0:T(8,128)S(1)} fusion(f32[32,64,64]{1,2,0:T(8,128)S(1)} %copy.125), kind=kOutput, calls=%fused_computation.83 | convolution fusion | flops 100720640 | bytes 1048576 | tf_op jit(solution)/shard_map/rnm,ns->rms/dot_general | solution.py:55
  101.9 1.1 %convolution_add_fusion = f32[32,64,64]{2,1,0:T(8,128)S(1)} fusion(f32[32,64,64]{2,1,0:T(8,128)S(1)} %fusion.53, f32[32,64,64]{1,2,0:T(8,128)S(1)} %copy.125), kind=kOutput, calls=%fused_computation.13 | convolution fusion | flops 100851712 | bytes 1572864 | tf_op jit(solution)/shard_map/rnm,ns->rms/dot_general | solution.py:58
  103.0 1.1 %convolution_subtract_fusion.1 = f32[32,64,64]{2,1,0:T(8,128)S(1)} fusion(f32[32,64,64]{2,1,0:T(8,128)S(1)} %fusion.55, f32[32,64,64]{1,2,0:T(8,128)S(1)} %copy.128), kind=kOutput, calls=%fused_computation.14 | convolution fusion | flops 100851712 | bytes 1572864 | tf_op jit(solution)/shard_map/rnm,ns->rms/dot_general | solution.py:55
  104.1 1.2 %fusion.17 = f32[64,32,64]{2,0,1:T(8,128)S(1)} fusion(f32[32,64,64]{2,1,0:T(8,128)S(1)} %convolution_add_fusion, f32[32,64,64]{2,1,0:T(8,128)S(1)} %convolution_subtract_fusion.1, f32[64,64]{1,0:T(8,128)S(1)} %copy.112, f32[64,64]{1,0:T(8,128)S(1)} %copy.111), kind=kOutput, calls=%fused_computation.28 | convolution fusion | flops 101113856 | bytes 1605632 | tf_op jit(solution)/shard_map/rms,mk->rks/dot_general | solution.py:65
  105.3 1.2 %fusion.6 = f32[32,64,64]{2,1,0:T(8,128)S(1)} fusion(f32[64,32,64]{2,0,1:T(8,128)S(1)} %fusion.17, f32[32,64,64]{2,1,0:T(8,128)S(1)} %convolution_add_fusion, f32[32,64,64]{2,1,0:T(8,128)S(1)} %convolution_subtract_fusion.1, f32[64,64]{1,0:T(8,128)S(1)} %copy.112, f32[64,64]{1,0:T(8,128)S(1)} %copy.111), kind=kOutput, calls=%fused_computation.12 | convolution fusion | flops 101244928 | bytes 2129920 | tf_op jit(solution)/shard_map/rms,mk->rks/dot_general | solution.py:65
  106.5 0.9 squeeze.25
  107.5 0.9 squeeze.24
  (51 shorter events, 4.0 us)
Async XLA Ops:
  0.6 9.6 %copy-start = (bf16[1,32,8,4,128]{4,3,2,1,0:T(4,128)(2,1)S(1)}, bf16[1,32,8,4,128]{4,3,2,1,0:T(4,128)(2,1)}, u32[]{:S(2)}) copy-start(bf16[1,32,8,4,128]{4,3,2,1,0:T(4,128)(2,1)} %param.8) | copy-start | bytes 786436
  2.1 17.0 %all-to-all-start = ((f32[32,1,8]{2,1,0:T(1,128)}), f32[32,1,8]{2,1,0:T(1,128)S(1)}, u32[]{:S(2)}, u32[]{:S(2)}) async-start(f32[32,1,8]{2,1,0:T(1,128)} %bitcast.1), calls=%async_computation | async-start | bytes 32768 | tf_op jit(solution)/shard_map/all_to_all | solution.py:93
  10.2 14.7 %copy-start.2 = (s32[384]{0:T(512)S(1)}, s32[384]{0:T(512)}, u32[]{:S(2)}) copy-start(s32[384]{0:T(512)} %param.12) | copy-start | bytes 4612
  19.1 21.4 %all-to-all-start.1 = ((f32[32,8,4,128]{3,2,1,0:T(4,128)}), f32[32,8,4,128]{3,2,1,0:T(4,128)S(1)}, u32[]{:S(2)}, u32[]{:S(2)}) async-start(f32[32,8,4,128]{3,2,1,0:T(4,128)} %fusion.13), calls=%async_computation.1 | async-start | bytes 1048576 | tf_op jit(solution)/shard_map/all_to_all | solution.py:92
  25.2 0.6 copy-start.4
  50.3 3.1 %copy-start.5 = (pred[384]{0:T(512)(128)(4,1)S(1)}, pred[384]{0:T(512)(128)(4,1)}, u32[]{:S(2)}) copy-start(pred[384]{0:T(512)(128)(4,1)} %compare_and_fusion) | copy-start | bytes 1156
  50.3 3.7 %copy-start.1 = (f32[4,32,12]{2,1,0:T(8,128)S(1)}, f32[4,32,12]{2,1,0:T(8,128)}, u32[]{:S(2)}) copy-start(f32[4,32,12]{2,1,0:T(8,128)} %get-tuple-element.14) | copy-start | bytes 18436
  55.2 10.3 %all-to-all-start.2 = ((bf16[32,2,192]{2,1,0:T(2,128)(2,1)}), bf16[32,2,192]{2,1,0:T(2,128)(2,1)S(1)}, u32[]{:S(2)}, u32[]{:S(2)}) async-start(bf16[32,2,192]{2,1,0:T(2,128)(2,1)} %reshape.411), calls=%async_computation.2 | async-start | bytes 65536 | tf_op jit(solution)/shard_map/all_to_all | solution.py:121
  73.9 4.7 %copy-start.3 = (f32[384,4]{0,1:T(4,128)S(1)}, f32[384,4]{0,1:T(4,128)}, u32[]{:S(2)}) copy-start(f32[384,4]{0,1:T(4,128)} %get-tuple-element.15) | copy-start | bytes 18436
  76.0 9.9 %all-to-all-start.3 = ((bf16[32,2,384]{2,1,0:T(2,128)(2,1)}), bf16[32,2,384]{2,1,0:T(2,128)(2,1)S(1)}, u32[]{:S(2)}, u32[]{:S(2)}) async-start(bf16[32,2,384]{2,1,0:T(2,128)(2,1)} %reshape.413), calls=%async_computation.3 | async-start | bytes 98304 | tf_op jit(solution)/shard_map/all_to_all | solution.py:136
where the time goes:
time: 109 us; the launch traced here: 108 us
  matrix products  31.8 us (29%)
  local copies, waits for them, and re-layouts  26 us (24%)
  waiting for transfers between devices  25.5 us (23%)
  starting transfers between devices  19 us (17%)
  other arithmetic  4.98 us (5%)
  between operations  1.12 us (1%)
    all_to_all x1, waiting for transfers between devices, per_device(): lax.all_to_all(partial_value, ('blk', 'ma'), split_axis=0, concat_axis=0,...  11.2 us
    dot_general x1, matrix products, per_device(): jnp.einsum('dcbs,dcsp->dcbp', groups, onehot, preferred_element_type=jnp....  8.65 us
    all_to_all x1, starting transfers between devices, per_device(): lax.all_to_all(sent_ids, ('blk', 'ma'), split_axis=0, concat_axis=0, tile...  7.3 us
    all_to_all x1, waiting for transfers between devices, per_device(): lax.all_to_all(outgoing_maps, ('blk', 'ma'), split_axis=4, concat_axis=0,...  7.22 us
    all_to_all x1, waiting for transfers between devices, per_device(): lax.all_to_all(outgoing, ('blk', 'ma'), split_axis=0, concat_axis=4, tile...  7.05 us
    all_to_all x1, starting transfers between devices, per_device(): lax.all_to_all(partial_value, ('blk', 'ma'), split_axis=0, concat_axis=0,...  5.84 us
    unnamed x18, local copies, waits for them, and re-layouts  5.48 us
    scatter x2, local copies, waits for them, and re-layouts, per_device(): jnp.zeros((row_total, cycle_length), jnp.float32).at[:, m_table]  5.3 us
  transfers between devices with their start and end apart: 4, of which 3 were waited for; matrix products, arithmetic and copies ran while one was open for 12% of the time, Pallas kernels for 0%

commit v1 on v0

v1 whole, which is shorter than its diff:
```python
import functools

import jax
import jax.numpy as jnp
import numpy as np
from jax import lax
from jax.experimental import pallas as pl
from jax.experimental.pallas import tpu as pltpu
from jax.sharding import Mesh, PartitionSpec as P

NPHI = 4096
BLOCK = 128
SEGMENTS = NPHI // BLOCK
LANES = 128

NT = (((1,), (1,)), ((), ()))
TN = (((0,), (0,)), ((), ()))


def dot(a, b, dims=(((1,), (0,)), ((), ()))):
    return lax.dot_general(a, b, dims, preferred_element_type=jnp.float32)


def high_low(x):
    high = x.astype(jnp.bfloat16)
    return high, (x - high.astype(jnp.float32)).astype(jnp.bfloat16)


def np_high_low(x):
    high = x.astype(np.float32).astype(jnp.bfloat16)
    return high, (x - high.astype(np.float64)).astype(np.float32).astype(jnp.bfloat16)


def analysis_tables(orders):
    m = np.arange(orders, dtype=np.int64)[:, None]
    p = np.arange(BLOCK, dtype=np.int64)[None, :]
    angle = (m * p % NPHI) * (2 * np.pi / NPHI)
    inner = np.concatenate(np_high_low(np.cos(angle)) + np_high_low(-np.sin(angle)), 1)
    half = np.arange(2 * SEGMENTS, dtype=np.int64)[None, :]
    steps = 2 * BLOCK * (half % SEGMENTS) + half // SEGMENTS
    angle = (m * steps % (2 * NPHI)) * (np.pi / NPHI)
    outer = np.concatenate(np_high_low(np.cos(angle) / NPHI) + np_high_low(-np.sin(angle) / NPHI), 1)
    return inner, outer


def bit_groups(devices):
    bits = list(range(1, devices.bit_length() - 1))
    return [bits[i : i + 2] for i in range(0, len(bits), 2)]


def positions(devices):
    order = [0]
    for group in bit_groups(devices):
        order = [p | (v << group[0]) for p in order for v in range(1 << len(group))]
    return order


def slot_rows(orders, slots):
    out = np.zeros((orders // 2, orders), np.float32)
    for block, position in enumerate(positions(orders // slots)):
        for slot in range(slots):
            out[block * slots + slot, position * slots + slot] = 1
    return out.astype(jnp.bfloat16)


def rolled(x, shift):
    return jnp.concatenate([x[:, shift:], x[:, :shift]], 1)


def exclusive_or(table, me, slots):
    orders = table.shape[1]
    block = lax.div(lax.broadcasted_iota(jnp.int32, table.shape, 1), slots)
    for bit in range((orders // slots).bit_length() - 1):
        shift = slots << bit
        swapped = jnp.where((block >> bit) % 2 == 0, rolled(table, shift), rolled(table, orders - shift))
        table = jnp.where(jnp.broadcast_to((me >> bit) & 1, table.shape) == 1, swapped, table)
    return table


def hot(condition):
    return jnp.where(condition, 1.0, 0.0).astype(jnp.bfloat16)


def half_modes(table, rows_ref, inner_ref, outer_ref, deposits, phase_hot, cycle_hot, out_ref):
    count, orders = rows_ref.shape
    cycles = cycle_hot.shape[0]
    wide = 2 * BLOCK
    held = hot(lax.broadcasted_iota(jnp.int32, (orders, orders), 0) == table)
    chunk = 192
    for start in range(0, count, chunk):
        pick = dot(rows_ref[start : start + chunk, :], held, NT).astype(jnp.bfloat16)
        inner = dot(pick, inner_ref[...]).astype(jnp.bfloat16)
        outer = dot(pick, outer_ref[...]).astype(jnp.bfloat16)
        outer_cos = dot(outer[:, :BLOCK], phase_hot)
        outer_sin = dot(outer[:, BLOCK:], phase_hot)
        for b, deposit in enumerate(deposits):
            inner_cos = dot(inner[:, :wide], deposit, NT)
            inner_sin = dot(inner[:, wide:], deposit, NT)
            real = inner_cos * outer_cos - inner_sin * outer_sin
            imag = inner_cos * outer_sin + inner_sin * outer_cos
            for part, value in ((0, real), (1, imag)):
                value = dot(value.astype(jnp.bfloat16), cycle_hot, NT)
                for tile in range(cycles // LANES):
                    at = out_ref.at[b * (cycles // LANES) + tile]
                    at[pl.ds(2 * start + part, chunk, stride=2), :] = value[:, tile * LANES : (tile + 1) * LANES]


def twice(x):
    return jnp.concatenate([x, x], 1)


def first_kernel(slots, staged, w_hbm, off_hbm, cnt_hbm, ids_hbm, table_hbm, rows_hbm, inner_hbm, outer_hbm, *refs):
    if staged:
        legendre_hbm, *refs = refs
    out_ref, deposit_ref, phase_ref, cycle_ref, table_ref, rows_ref, inner_ref, outer_ref, *refs = refs
    if staged:
        legendre_ref, *refs = refs
    w_ref, off_ref, cnt_ref, ids_ref, flat_ref, wide_ref, half_ref, sems = refs
    pairs = (
        (off_hbm, off_ref), (w_hbm, w_ref), (cnt_hbm, cnt_ref), (ids_hbm, ids_ref),
        (table_hbm, flat_ref), (rows_hbm, rows_ref), (inner_hbm, inner_ref), (outer_hbm, outer_ref),
    )
    if staged:
        pairs = pairs + ((legendre_hbm, legendre_ref),)
    copies = [pltpu.make_async_copy(a, b, sems.at[i]) for i, (a, b) in enumerate(pairs)]
    for copy in copies:
        copy.start()
    groups = off_ref.shape[0]
    capacity, devices = ids_ref.shape
    bins = w_ref.shape[0] // groups
    cycles = cycle_ref.shape[0]
    blocks_here = cycles * SEGMENTS // devices

    pack = 16
    pixel = lax.broadcasted_iota(jnp.int32, (pack, BLOCK), 0)
    pixels = [(pixel + pack * k).astype(jnp.float32).astype(jnp.bfloat16) for k in range(BLOCK // pack)]
    own = [hot(lax.div(lax.broadcasted_iota(jnp.int32, (4 * bins, BLOCK), 0), bins) == i) for i in range(4)]
    one = jnp.ones((pack, BLOCK), jnp.bfloat16)
    zero = jnp.zeros((pack, BLOCK), jnp.bfloat16)
    for copy in copies[:2]:
        copy.wait()

    def deposit(step, carry):
        start = pl.multiple_of(step * (4 * bins), 4 * bins)
        rows = w_ref[pl.ds(start, 4 * bins), :]
        left, right = [], []
        for i in range(4):
            left.append(rows * own[i])
            at = off_ref[pl.ds(step * 4 + i, 1), :].astype(jnp.float32)
            at = jnp.broadcast_to(at, (pack, BLOCK)).astype(jnp.bfloat16)
            right.append(jnp.concatenate([jnp.where(at == x, one, zero) for x in pixels], 0))
        wide_ref[pl.ds(start, 4 * bins), :] = dot(jnp.concatenate(left, 1), jnp.concatenate(right, 1), NT)
        return carry

    lax.fori_loop(0, groups // 4, deposit, 0, unroll=16)
    for copy in copies[2:8]:
        copy.wait()

    me = lax.axis_index("blk")
    for axis in ("y", "core"):
        me = me * lax.axis_size(axis) + lax.axis_index(axis)
    table = exclusive_or(flat_ref[...].reshape(table_ref.shape), me, slots)
    table_ref[...] = table

    owner = lax.div(lax.broadcasted_iota(jnp.int32, (devices, groups), 1), capacity)
    spread = hot(owner == lax.broadcasted_iota(jnp.int32, (devices, groups), 0))
    ids = dot(ids_ref[...].astype(jnp.float32).astype(jnp.bfloat16), spread)
    member = lax.rem(lax.broadcasted_iota(jnp.int32, (capacity, groups), 1), capacity)
    ids = jnp.where(member == lax.broadcasted_iota(jnp.int32, (capacity, groups), 0), ids, 0.0)
    ids = jnp.sum(ids, axis=0, keepdims=True)
    counts = jnp.broadcast_to(cnt_ref[...].astype(jnp.float32), (8, devices)).astype(jnp.bfloat16)
    counts = dot(counts, spread)[0:1, :]
    block = ids.astype(jnp.int32) + owner[0:1, :] * blocks_here
    live = member[0:1, :].astype(jnp.float32) < counts
    cycle = lax.div(block, SEGMENTS)
    phase = lax.rem(cycle, 2) * SEGMENTS + lax.rem(block, SEGMENTS)
    cycle = jnp.where(live, cycle, -1)
    phase = jnp.where(live, phase, -1)
    cycle_hot = hot(lax.broadcasted_iota(jnp.int32, (cycles, groups), 0) == cycle)
    half_hot = hot(lax.broadcasted_iota(jnp.int32, (2 * SEGMENTS, groups), 0) == phase)
    phase_hot = jnp.concatenate([half_hot, half_hot], 0)
    cycle_ref[...] = cycle_hot
    phase_ref[...] = phase_hot

    deposits = []
    for b in range(bins):
        value = wide_ref[pl.ds(b, groups, stride=bins), :].astype(jnp.bfloat16)
        deposit_ref[b] = value
        deposits.append(twice(value))
    half_modes(rolled(table, slots), rows_ref, inner_ref, outer_ref, deposits, phase_hot, cycle_hot, half_ref)
    for tile in range(half_ref.shape[0]):
        out_ref[:, tile * LANES : (tile + 1) * LANES] = half_ref[tile].astype(jnp.bfloat16)
    for copy in copies[8:]:
        copy.wait()


def second_kernel(deposit_ref, phase_ref, cycle_ref, table_ref, rows_ref, inner_ref, outer_ref, out_ref):
    deposits = [twice(deposit_ref[b]) for b in range(deposit_ref.shape[0])]
    half_modes(table_ref[...], rows_ref, inner_ref, outer_ref, deposits, phase_ref[...], cycle_ref[...], out_ref)


def split_sum(parts, tile, keep_ref, send_refs):
    rows = keep_ref.shape[0]
    lanes = slice(tile * LANES, (tile + 1) * LANES)
    for i, out_ref in enumerate((keep_ref, *send_refs)):
        value = sum(part(slice(i * rows, (i + 1) * rows), lanes) for part in parts)
        out_ref[:, lanes] = value.astype(out_ref.dtype)


def pair_kernel(mine_ref, other_ref, keep_ref, *send_refs):
    for tile in range(mine_ref.shape[0]):
        parts = (
            lambda rows, lanes: mine_ref[tile, rows, :],
            lambda rows, lanes: other_ref[rows, lanes].astype(jnp.float32),
        )
        split_sum(parts, tile, keep_ref, send_refs)


def merge_kernel(count, kept_ref, *refs):
    arrived, outs = refs[:count], refs[count:]
    for tile in range(kept_ref.shape[1] // LANES):
        parts = [lambda rows, lanes, ref=ref: ref[rows, lanes].astype(jnp.float32) for ref in (kept_ref, *arrived)]
        split_sum(parts, tile, outs[0], outs[1:])


def gain_column(degrees):
    l = np.arange(degrees, dtype=np.float32)
    return np.where(l > 0.5, np.float32(-20000.0) / np.maximum(l * (l + 1), np.float32(1)), np.float32(0)).astype(np.float32)[:, None] * np.ones((1, BLOCK), np.float32)


def interleave(cycles, cycles_here):
    out = np.zeros((2 * cycles, 2 * cycles), np.float32)
    for f in range(2):
        for c in range(cycles):
            out[f * cycles + c, (c // cycles_here * 2 + f) * cycles_here + c % cycles_here] = 1
    return out.astype(jnp.bfloat16)


def response_kernel(start, staged, legendre_ref, gain_ref, order_ref, out_ref, *scratch):
    count = out_ref.shape[0]
    if not staged:
        source, (legendre_ref, sems) = legendre_ref, scratch
        copies = [pltpu.make_async_copy(source.at[start + i], legendre_ref.at[i], sems.at[i]) for i in range(count)]
        for copy in copies:
            copy.start()
        start = 0
    for slot in range(count):
        if not staged:
            copies[slot].wait()
        basis = legendre_ref[start + slot]
        cycles = basis.shape[1]
        gain = jnp.concatenate([gain_ref[...]] * (cycles // BLOCK), 1)
        gained = (basis.astype(jnp.float32) * gain).astype(jnp.bfloat16)
        high, low = high_low(dot(basis, jnp.concatenate([basis, gained], 1), TN))
        out_ref[slot, :cycles, :] = dot(high, order_ref[...]).astype(jnp.bfloat16)
        out_ref[slot, cycles:, :] = dot(low, order_ref[...]).astype(jnp.bfloat16)


def slot_order(slots, bins):
    out = np.zeros((slots * 2 * bins, slots * 2 * bins), np.float32)
    for b in range(bins):
        for c in range(2):
            for t in range(slots):
                out[(t * 2 + c) * bins + b, (b * slots + t) * 2 + c] = 1
    return out.astype(jnp.bfloat16)


def synthesis_kernel(arrivals, pieces, kept_ref, *refs):
    partials, refs = refs[:arrivals], refs[arrivals:]
    response_refs, (order_ref, out_ref) = refs[:pieces], refs[pieces:]
    cycles = response_refs[0].shape[1] // 2
    bins = kept_ref.shape[1] // cycles
    slots = kept_ref.shape[0] // 2
    responses = [ref.at[i] for ref in response_refs for i in range(ref.shape[0])]
    total = kept_ref[...]
    for ref in partials:
        total = total + ref[...].astype(jnp.float32)
    modes = jnp.concatenate([total[:, b * cycles : (b + 1) * cycles] for b in range(bins)], 0)
    high, low = high_low(modes)
    high = dot(order_ref[...], high)
    low = dot(order_ref[...], low)
    per_slot = 2 * bins
    parts = []
    for t in range(slots):
        rows = slice(t * per_slot, (t + 1) * per_slot)
        left = jnp.concatenate([high[rows, :], low[rows, :]], 0).astype(jnp.bfloat16)
        part = dot(twice(left), responses[t][...])
        parts.append(part[:per_slot, :] + part[per_slot:, :])
    parts.append(jnp.zeros((128 - slots * per_slot, 2 * cycles), jnp.float32))
    result = jnp.concatenate(parts, 0)
    out_ref[...] = jnp.transpose(result).astype(jnp.bfloat16)


def inverse_tables(orders):
    half = NPHI // 2
    k = np.arange(half, dtype=np.int64)[None, :]
    tables = []
    for parity in range(2):
        m = np.arange(parity, orders, 2, dtype=np.int64)[:, None]
        angle = (m * k % NPHI) * (2 * np.pi / NPHI)
        tables += [np.cos(angle), -np.sin(angle)]
    chunks = np.split(np.stack(tables), half // 512, axis=2)
    return np.concatenate(chunks).reshape(-1, 512).astype(np.float32).astype(jnp.bfloat16)


def order_lanes(orders):
    padded = -(-(orders // 2) // 128) * 128
    out = np.full((2, padded), -1, np.int32)
    for parity in range(2):
        out[parity, : orders // 2] = np.arange(parity, orders, 2)
    return out.reshape(1, 2 * padded)


def turn_rows(order_row):
    m = np.maximum(order_row[0], 0).astype(np.float64)
    weight = np.where(order_row[0] == 0, 1.0, 2.0)
    parts = np_high_low(np.cos(np.pi * m / NPHI) * weight) + np_high_low(np.sin(np.pi * m / NPHI) * weight)
    return np.stack(parts + (weight.astype(jnp.bfloat16),) + (np.zeros_like(parts[0]),) * 11)


def part_rows(part, bins, cycles_here):
    shape = (2 * bins * cycles_here, 4 * bins * cycles_here)
    row = lax.broadcasted_iota(jnp.int32, shape, 0)
    column = lax.broadcasted_iota(jnp.int32, shape, 1)
    cycle = lax.rem(row, cycles_here)
    bin_number = lax.rem(lax.div(row, cycles_here), bins)
    filter_number = lax.div(row, cycles_here * bins)
    return hot(column == ((filter_number * cycles_here + cycle) * 2 + part) * bins + bin_number)


def inverse_kernel(arrived_ref, slots_hbm, lanes_hbm, turn_hbm, table_hbm, kappa_ref, potential_ref,
                   slots_ref, lanes_ref, turn_ref, table_ref, wide_ref, sems):
    copies = [
        pltpu.make_async_copy(a, b, sems.at[i])
        for i, (a, b) in enumerate(((slots_hbm, slots_ref), (lanes_hbm, lanes_ref), (turn_hbm, turn_ref)))
    ]
    half = NPHI // 2
    chunk = table_ref.shape[1]
    chunks = half // chunk
    part = table_ref.shape[0] // chunks
    for i in range(chunks):
        rows = pl.ds(i * part, part)
        copies.append(pltpu.make_async_copy(table_hbm.at[rows], table_ref.at[rows], sems.at[3 + i]))
    for copy in copies:
        copy.start()
    devices, slots = slots_ref.shape
    bins, cycles_here, _ = kappa_ref.shape
    half_orders = part // 4
    per_slot = 2 * bins
    per_source = 2 * cycles_here
    wide_ref[...] = arrived_ref[...].astype(jnp.float32)
    turned = [jnp.transpose(wide_ref[pl.ds(i, devices, stride=per_source), :]) for i in range(per_source)]
    for copy in copies[:3]:
        copy.wait()
    orders = lanes_ref[...]
    spectrum = None
    for t in range(slots):
        left = jnp.concatenate([x[t * per_slot : (t + 1) * per_slot, :] for x in turned], 0).astype(jnp.bfloat16)
        term = dot(left, hot(slots_ref[:, t : t + 1] == orders))
        spectrum = term if spectrum is None else spectrum + term
    spectrum = spectrum.astype(jnp.bfloat16)
    real_in = dot(part_rows(0, bins, cycles_here), spectrum)
    imag_in = dot(part_rows(1, bins, cycles_here), spectrum)
    turn = turn_ref[...].astype(jnp.float32)
    odd = lax.rem(lax.rem(lax.broadcasted_iota(jnp.int32, real_in.shape, 0), cycles_here), 2) == 1
    turn_cos = jnp.where(odd, turn[0:1, :] + turn[1:2, :], turn[4:5, :])
    turn_sin = jnp.where(odd, turn[2:3, :] + turn[3:4, :], 0.0)
    real = jnp.concatenate(high_low(real_in * turn_cos - imag_in * turn_sin), 0)
    imag = jnp.concatenate(high_low(real_in * turn_sin + imag_in * turn_cos), 0)
    count = real_in.shape[0]
    padded = real.shape[1] // 2
    for index in range(chunks):
        copies[3 + index].wait()
        start = index * chunk
        sums = []
        for parity in range(2):
            lanes = slice(parity * padded, parity * padded + half_orders)
            row = index * part + 2 * parity * half_orders
            both = dot(real[:, lanes], table_ref[row : row + half_orders, :])
            both = both + dot(imag[:, lanes], table_ref[row + half_orders : row + 2 * half_orders, :])
            sums.append(both[:count, :] + both[count:, :])
        first = sums[0] + sums[1]
        second = sums[0] - sums[1]
        for f, out_ref in ((0, kappa_ref), (1, potential_ref)):
            for b in range(bins):
                rows = slice((f * bins + b) * cycles_here, (f * bins + b + 1) * cycles_here)
                out_ref[b, :, start : start + chunk] = first[rows, :]
                out_ref[b, :, half + start : half + start + chunk] = second[rows, :]


def in_hbm(x):
    return pltpu.with_memory_space_constraint(jnp.asarray(x), pltpu.HBM)


def params(orders):
    small = 14 if orders <= 512 else 56
    return pltpu.CompilerParams(vmem_limit_bytes=small * 1024 * 1024)


def per_device(weights, offsets, counts, block_ids, m_table, legendre):
    axes = ("blk", "y", "core")
    _, devices, capacity, bins, _ = weights.shape
    slots, degrees, cycles = legendre.shape
    orders = m_table.shape[0]
    groups = devices * capacity
    cycles_here = cycles // devices
    width = bins * cycles
    staged = legendre.size <= 4 * 1024 * 1024
    limits = params(orders)
    hbm = pl.BlockSpec(memory_space=pltpu.HBM)
    vmem = pl.BlockSpec(memory_space=pltpu.VMEM)

    def shaped(*shape, dtype=jnp.bfloat16):
        return jax.ShapeDtypeStruct(shape, dtype)

    rows = slot_rows(orders, slots)
    inner, outer = analysis_tables(orders)
    shapes = [
        shaped(orders, width),
        shaped(bins, groups, BLOCK),
        shaped(4 * SEGMENTS, groups),
        shaped(cycles, groups),
        shaped(1, orders, dtype=jnp.int32),
        shaped(*rows.shape),
        shaped(*inner.shape),
        shaped(*outer.shape),
    ]
    operands = [
        weights.reshape(groups * bins, BLOCK),
        offsets.reshape(groups, BLOCK),
        counts,
        jnp.transpose(block_ids[0]),
        m_table,
        rows,
        inner,
        outer,
    ]
    if staged:
        shapes.append(shaped(*legendre.shape))
        operands.append(legendre)
    theirs, *shared = pl.pallas_call(
        functools.partial(first_kernel, slots, staged),
        in_specs=[hbm] * len(operands),
        out_specs=(vmem,) * len(shapes),
        out_shape=tuple(shapes),
        scratch_shapes=[
            pltpu.VMEM((groups * bins, BLOCK), jnp.bfloat16),
            pltpu.VMEM((groups, BLOCK), jnp.int32),
            pltpu.VMEM((1, devices), jnp.int32),
            pltpu.VMEM((capacity, devices), jnp.int32),
            pltpu.VMEM((orders,), jnp.int32),
            pltpu.VMEM((groups * bins, BLOCK), jnp.float32),
            pltpu.VMEM((width // LANES, orders, LANES), jnp.float32),
            pltpu.SemaphoreType.DMA((len(operands),)),
        ],
        compiler_params=limits,
        name="deposit_and_other_half",
    )(*[in_hbm(x) for x in operands])
    basis = shared.pop() if staged else in_hbm(legendre)

    def swap(x, mask):
        return lax.ppermute(x, axes, [(i, i ^ mask) for i in range(devices)])

    other = swap(theirs, 1)
    mine = pl.pallas_call(
        second_kernel,
        in_specs=[vmem] * 7,
        out_specs=vmem,
        out_shape=shaped(width // LANES, orders, LANES, dtype=jnp.float32),
        compiler_params=limits,
        cost_estimate=pl.CostEstimate(flops=8 * orders * 256 * bins * groups, bytes_accessed=4 * orders * width, transcendentals=0),
        name="own_half",
    )(*shared)

    groups_of_bits = bit_groups(devices)
    stages = len(groups_of_bits)
    gain, order = gain_column(degrees), interleave(cycles, cycles_here)
    blocks = devices // 2
    kernel, inputs = pair_kernel, (mine, other)
    responses = []
    for stage, bits in enumerate(groups_of_bits):
        ways = 1 << len(bits)
        blocks //= ways
        rows_here = blocks * 2 * slots
        kept, *sends = pl.pallas_call(
            kernel,
            in_specs=[vmem] * len(inputs),
            out_specs=(vmem,) * ways,
            out_shape=(shaped(rows_here, width, dtype=jnp.float32),) + (shaped(rows_here, width),) * (ways - 1),
            compiler_params=limits,
            name="pair_sum" if stage == 0 else "merge",
        )(*inputs)
        *sends, basis = lax.optimization_barrier((*sends, basis))
        arrived = [swap(x, (i + 1) << bits[0]) for i, x in enumerate(sends)]
        first, last = (min(slots, slots * 2 * k * (2 * stages - k) // (2 * stages * stages)) for k in (stage, stage + 1))
        count = last - first
        scratch = [] if staged else [pltpu.VMEM((count, degrees, cycles), jnp.bfloat16), pltpu.SemaphoreType.DMA((count,))]
        response = pl.pallas_call(
            functools.partial(response_kernel, first, staged),
            in_specs=[vmem if staged else hbm, vmem, vmem],
            out_specs=vmem,
            out_shape=shaped(count, 2 * cycles, 2 * cycles),
            scratch_shapes=scratch,
            compiler_params=limits,
            cost_estimate=pl.CostEstimate(
                flops=6 * count * degrees * cycles * cycles, bytes_accessed=2 * count * degrees * cycles, transcendentals=0
            ),
            name="response",
        )(basis, gain, order)
        *arrived, response = lax.optimization_barrier((*arrived, response))
        responses.append(response)
        kernel, inputs = functools.partial(merge_kernel, len(arrived)), (kept, *arrived)

    outgoing = pl.pallas_call(
        functools.partial(synthesis_kernel, len(inputs) - 1, len(responses)),
        in_specs=[vmem] * (len(inputs) + len(responses) + 1),
        out_specs=vmem,
        out_shape=shaped(2 * cycles, 128),
        compiler_params=limits,
        name="synthesis",
    )(*inputs, *responses, slot_order(slots, bins))
    outgoing = outgoing.reshape(devices, 2 * cycles_here, 128)
    outgoing, held = lax.optimization_barrier((outgoing, m_table))
    arrived = lax.all_to_all(outgoing, axes, split_axis=0, concat_axis=0, tiled=True)
    arrived = arrived.reshape(2 * cycles, 128)
    if staged:
        arrived = pltpu.with_memory_space_constraint(arrived, pltpu.VMEM)

    lanes = order_lanes(orders)
    constants = [lanes, turn_rows(lanes), inverse_tables(orders)]
    map_shape = shaped(bins, cycles_here, NPHI, dtype=jnp.float32)
    return pl.pallas_call(
        inverse_kernel,
        in_specs=[vmem] + [hbm] * 4,
        out_specs=(vmem, vmem),
        out_shape=(map_shape, map_shape),
        scratch_shapes=[
            pltpu.VMEM((devices, slots), jnp.int32),
            *[pltpu.VMEM(x.shape, x.dtype) for x in constants],
            pltpu.VMEM((2 * cycles, 128), jnp.float32),
            pltpu.SemaphoreType.DMA((3 + NPHI // 2 // constants[-1].shape[1],)),
        ],
        compiler_params=limits,
        name="inverse",
    )(arrived, in_hbm(held.reshape(devices, slots)), *[in_hbm(x) for x in constants])


def solution(mesh):
    blocks, columns = mesh.devices.shape
    fine = Mesh(mesh.devices.reshape(blocks, columns // 2, 2), ("blk", "y", "core"))
    axes = ("blk", "y", "core")
    placed = (
        P(axes, None, None, None, None),
        P(axes, None, None, None),
        P(axes, None),
        P(axes, None, None),
        P(),
        P(axes, None, None),
    )
    return jax.shard_map(
        per_device,
        mesh=fine,
        in_specs=placed,
        out_specs=(P(None, axes, None), P(None, axes, None)),
        check_vma=False,
    )
```

time: 109 us -> 43.3 us (0.40)
  matrix products: 31.8 us -> 0 us
  local copies, waits for them, and re-layouts: 26 us -> 0.73 us
  Pallas kernels: 0 us -> 17 us
  waiting for transfers between devices: 25.5 us -> 12.6 us
  starting transfers between devices: 19 us -> 11.9 us
  other arithmetic: 4.98 us -> 0 us
    dot_general x16 -> x0, matrix products: 31.8 us -> none  [the longest x1 8.65 us: per_device(): jnp.einsum('dcbs,dcsp->dcbp', groups, onehot, preferred_element_type=jnp....]
    all_to_all x4 -> x1, waiting for transfers between devices: 25.5 us -> 6.69 us  [per_device(): lax.all_to_all(outgoing, axes, split_axis=0, concat_axis=0, tiled=True)]
    pallas_call x0 -> x8, Pallas kernels: none -> 17 us  [the longest x1 5.98 us: per_device(): pl.pallas_call(functools.partial(first_kernel, slots, staged), in_specs=[...]
    all_to_all x4 -> x1, starting transfers between devices: 19 us -> 2.72 us  [per_device(): lax.all_to_all(outgoing, axes, split_axis=0, concat_axis=0, tiled=True)]
    ppermute x0 -> x7, starting transfers between devices: none -> 9.15 us  [swap(): return lax.ppermute(x, axes, [(i, i ^ mask) for i in range(devices)])]
    ppermute x0 -> x7, waiting for transfers between devices: none -> 5.9 us  [swap(): return lax.ppermute(x, axes, [(i, i ^ mask) for i in range(devices)])]
    reshape x7 -> x1, local copies, waits for them, and re-layouts: 6.55 us -> 0.7 us  [per_device(): held.reshape(devices, slots)]
    unnamed x18 -> x8, local copies, waits for them, and re-layouts: 5.48 us -> 0.03 us
  transfers between devices with their start and end apart: 4 -> 8, of which waited for: 3 -> 5; matrix products, arithmetic and copies ran while one was open for 12% -> 2% of each run, Pallas kernels for 0% -> 15%
where the time goes in v1:
time: 43.3 us; the launch traced here: 43 us
  Pallas kernels  17 us (39%)
  waiting for transfers between devices  12.6 us (29%)
  starting transfers between devices  11.9 us (27%)
  between operations  0.75 us (2%)
  local copies, waits for them, and re-layouts  0.73 us (2%)
    ppermute x7, starting transfers between devices, swap(): return lax.ppermute(x, axes, [(i, i ^ mask) for i in range(devices)])  9.15 us
    all_to_all x1, waiting for transfers between devices, per_device(): lax.all_to_all(outgoing, axes, split_axis=0, concat_axis=0, tiled=True)  6.69 us
    pallas_call x1, Pallas kernels, per_device(): pl.pallas_call(functools.partial(first_kernel, slots, staged), in_specs=[...  5.98 us
    ppermute x7, waiting for transfers between devices, swap(): return lax.ppermute(x, axes, [(i, i ^ mask) for i in range(devices)])  5.9 us
    pallas_call x2, Pallas kernels, per_device(): pl.pallas_call(functools.partial(response_kernel, first, staged), in_spec...  4.9 us
    pallas_call x1, Pallas kernels, per_device(): pl.pallas_call(inverse_kernel, in_specs=[vmem] + [hbm] * 4, out_specs=(vm...  3.24 us
    all_to_all x1, starting transfers between devices, per_device(): lax.all_to_all(outgoing, axes, split_axis=0, concat_axis=0, tiled=True)  2.72 us
    pallas_call x1, Pallas kernels, per_device(): pl.pallas_call(second_kernel, in_specs=[vmem] * 7, out_specs=vmem, out_sh...  1.64 us
  transfers between devices with their start and end apart: 8, of which 5 were waited for; matrix products, arithmetic and copies ran while one was open for 2% of the time, Pallas kernels for 15%

profile of v1, /device:TPU:0, one launch (start us, length us, event | category | flops | bytes accessed | tf_op | source)
XLA Modules:
  0.0 43.0 jit_solution(14772785559233474189)
XLA Ops:
  0.6 0.0 copy-start
  0.6 0.0 copy-start.1
  0.7 6.0 %deposit_and_other_half.1 = (bf16[384,512]{1,0:T(8,128)(2,1)S(1)}, bf16[4,256,128]{2,1,0:T(8,128)(2,1)S(1)}, bf16[128,256]{1,0:T(8,128)(2,1)S(1)}, bf16[128,256]...) custom-call(bf16[1024,128]{1,0:T(8,128)(2,1)} %bitcast.8, ...), custom_call_target="tpu_custom_call" | custom-call | tf_op jit(solution)/shard_map/deposit_and_other_half/pallas_call | solution.py:441
  6.6 0.5 %collective-permute-start = (bf16[384,512]{1,0:T(8,128)(2,1)S(1)}, bf16[384,512]{1,0:T(8,128)(2,1)S(1)}, u32[]{:S(2)}, u32[]{:S(2)}) collective-permute-start(bf16[384,512]{1,0:T(8,128)(2,1)S(1)} %get-tuple-element.44), channel_id=1, source_target_pairs={{0,1},{1,0},{2,3},{3,2},{4,5},{5,4},{6,7},{7,6},{8,9},{9,8},{10,11... | collective-permute-start | bytes 1179656 | tf_op jit(solution)/shard_map/ppermute | solution.py:462
  7.2 1.6 %own_half.1.mine_ref = f32[4,384,128]{2,1,0:T(8,128)S(1)} custom-call(bf16[4,256,128]{2,1,0:T(8,128)(2,1)S(1)} %get-tuple-element.37.deposit_ref, bf16[128,256]{1,0:T(8,128)(2,1)S(1)} %get-tuple-element.38.phase_ref, bf16[128,256]{1,0:T(8,128)(2,1)S(1)} %get-tuple-element.39.cycle_ref, s32[1,384]{1,0:T(1,128)S(1)} %get-tuple-element.40.table_ref, ...), custom_call_target="tpu_custom_call" | custom-call | flops 805306368 | bytes 786432 | tf_op jit(solution)/shard_map/own_half/pallas_call | solution.py:465
  8.8 0.0 collective-permute-done.other_ref
  8.8 0.1 pair_sum.1
  8.9 2.6 %collective-permute-start.1 = (bf16[96,512]{1,0:T(8,128)(2,1)S(1)}, bf16[96,512]{1,0:T(8,128)(2,1)S(1)}, u32[]{:S(2)}, u32[]{:S(2)}) collective-permute-start(bf16[96,512]{1,0:T(8,128)(2,1)S(1)} %get-tuple-element.50), channel_id=1, source_target_pairs={{0,2},{1,3},{2,0},{3,1},{4,6},{5,7},{6,4},{7,5},{8,10},{9,11},{10,... | collective-permute-start | bytes 294920 | tf_op jit(solution)/shard_map/ppermute | solution.py:462
  11.6 1.5 %collective-permute-start.2 = (bf16[96,512]{1,0:T(8,128)(2,1)S(1)}, bf16[96,512]{1,0:T(8,128)(2,1)S(1)}, u32[]{:S(2)}, u32[]{:S(2)}) collective-permute-start(bf16[96,512]{1,0:T(8,128)(2,1)S(1)} %get-tuple-element.51), channel_id=1, source_target_pairs={{0,4},{1,5},{2,6},{3,7},{4,0},{5,1},{6,2},{7,3},{8,12},{9,13},{10,... | collective-permute-start | bytes 294920 | tf_op jit(solution)/shard_map/ppermute | solution.py:462
  13.0 0.1 collective-permute-start.3
  13.1 0.0 copy-done
  13.1 0.0 copy-done.1
  13.1 3.6 %response.2.refs_3_ = bf16[9,256,256]{2,1,0:T(8,128)(2,1)S(1)} custom-call(bf16[12,1664,128]{2,1,0:T(8,128)(2,1)S(1)} %get-tuple-element.64.legendre_ref, f32[1664,128]{1,0:T(8,128)S(1)} %copy-done, bf16[256,256]{1,0:T(8,128)(2,1)S(1)} %copy-done.1), custom_call_target="tpu_custom_call" | custom-call | flops 1472200704 | bytes 3833856 | tf_op jit(solution)/shard_map/response/pallas_call | solution.py:498
  16.7 0.0 copy-start.2
  16.7 0.0 copy-start.3
  16.8 0.0 collective-permute-done.1.refs_0_
  16.8 0.4 %collective-permute-done.2.refs_1_ = bf16[96,512]{1,0:T(8,128)(2,1)S(1)} collective-permute-done((bf16[96,512]{1,0:T(8,128)(2,1)S(1)}, bf16[96,512]{1,0:T(8,128)(2,1)S(1)}, u32[]{:S(2)}, u32[]{:S(2)}) %collective-permute-start.2) | collective-permute-done | bytes 98336 | tf_op jit(solution)/shard_map/ppermute | solution.py:462
  17.2 1.4 %collective-permute-done.3.refs_2_ = bf16[96,512]{1,0:T(8,128)(2,1)S(1)} collective-permute-done((bf16[96,512]{1,0:T(8,128)(2,1)S(1)}, bf16[96,512]{1,0:T(8,128)(2,1)S(1)}, u32[]{:S(2)}, u32[]{:S(2)}) %collective-permute-start.3) | collective-permute-done | bytes 98336 | tf_op jit(solution)/shard_map/ppermute | solution.py:462
  18.6 0.1 merge.1
  18.6 1.6 %collective-permute-start.4 = (bf16[24,512]{1,0:T(8,128)(2,1)S(1)}, bf16[24,512]{1,0:T(8,128)(2,1)S(1)}, u32[]{:S(2)}, u32[]{:S(2)}) collective-permute-start(bf16[24,512]{1,0:T(8,128)(2,1)S(1)} %get-tuple-element.61), channel_id=1, source_target_pairs={{0,8},{1,9},{2,10},{3,11},{4,12},{5,13},{6,14},{7,15},{8,0},{9,1},... | collective-permute-start | bytes 73736 | tf_op jit(solution)/shard_map/ppermute | solution.py:462
  20.3 2.6 %collective-permute-start.5 = (bf16[24,512]{1,0:T(8,128)(2,1)S(1)}, bf16[24,512]{1,0:T(8,128)(2,1)S(1)}, u32[]{:S(2)}, u32[]{:S(2)}) collective-permute-start(bf16[24,512]{1,0:T(8,128)(2,1)S(1)} %get-tuple-element.62), channel_id=1, source_target_pairs={{0,16},{1,17},{2,18},{3,19},{4,20},{5,21},{6,22},{7,23},{8,24},{9,... | collective-permute-start | bytes 73736 | tf_op jit(solution)/shard_map/ppermute | solution.py:462
  22.8 0.2 collective-permute-start.6
  23.1 1.3 %response.3.refs_4_ = bf16[3,256,256]{2,1,0:T(8,128)(2,1)S(1)} custom-call(bf16[12,1664,128]{2,1,0:T(8,128)(2,1)S(1)} %get-tuple-element.64.legendre_ref, f32[1664,128]{1,0:T(8,128)S(1)} %copy-done, bf16[256,256]{1,0:T(8,128)(2,1)S(1)} %copy-done.1), custom_call_target="tpu_custom_call" | custom-call | flops 490733568 | bytes 1277952 | tf_op jit(solution)/shard_map/response/pallas_call | solution.py:498
  24.4 0.0 collective-permute-done.4.refs_0_
  24.4 0.8 %collective-permute-done.5.refs_1_ = bf16[24,512]{1,0:T(8,128)(2,1)S(1)} collective-permute-done((bf16[24,512]{1,0:T(8,128)(2,1)S(1)}, bf16[24,512]{1,0:T(8,128)(2,1)S(1)}, u32[]{:S(2)}, u32[]{:S(2)}) %collective-permute-start.5) | collective-permute-done | bytes 24608 | tf_op jit(solution)/shard_map/ppermute | solution.py:462
  25.1 3.3 %collective-permute-done.6.refs_2_ = bf16[24,512]{1,0:T(8,128)(2,1)S(1)} collective-permute-done((bf16[24,512]{1,0:T(8,128)(2,1)S(1)}, bf16[24,512]{1,0:T(8,128)(2,1)S(1)}, u32[]{:S(2)}, u32[]{:S(2)}) %collective-permute-start.6) | collective-permute-done | bytes 24608 | tf_op jit(solution)/shard_map/ppermute | solution.py:462
  28.5 0.0 copy-done.2
  28.5 1.1 %synthesis.1 = bf16[256,128]{1,0:T(8,128)(2,1)} custom-call(f32[24,512]{1,0:T(8,128)S(1)} %get-tuple-element.57.kept_ref, bf16[24,512]{1,0:T(8,128)(2,1)S(1)} %collective-permute-done.4.refs_0_, bf16[24,512]{1,0:T(8,128)(2,1)S(1)} %collective-permute-done.5.refs_1_, bf16[24,512]{1,0:T(8,128)(2,1)S(1)} %collective-permute-done.6.refs_2_, ...), custom_call_target="tpu_custom_call" | custom-call | tf_op jit(solution)/shard_map/synthesis/pallas_call | solution.py:514
  29.6 2.7 %all-to-all-start = ((bf16[32,8,128]{2,1,0:T(8,128)(2,1)}), bf16[32,8,128]{2,1,0:T(8,128)(2,1)S(1)}, u32[]{:S(2)}, u32[]{:S(2)}) async-start(bf16[32,8,128]{2,1,0:T(8,128)(2,1)} %bitcast.4), calls=%async_computation | async-start | bytes 131072 | tf_op jit(solution)/shard_map/all_to_all | solution.py:524
  32.3 0.0 copy-done.3
  32.4 0.7 %reshape.23.slots_hbm = s32[32,12]{1,0:T(8,128)} reshape(s32[384]{0:T(512)S(1)} %copy-done.3) | data formatting | bytes 3072 | tf_op jit(solution)/shard_map/reshape | solution.py:545
  33.1 6.7 %all-to-all-done = bf16[32,8,128]{2,1,0:T(8,128)(2,1)S(1)} async-done(((bf16[32,8,128]{2,1,0:T(8,128)(2,1)}), bf16[32,8,128]{2,1,0:T(8,128)(2,1)S(1)}, u32[]{:S(2)}, u32[]{:S(2)}) %all-to-all-start) | async-done | bytes 65568 | tf_op jit(solution)/shard_map/all_to_all | solution.py:524
  39.8 3.2 %inverse.1 = (f32[4,4,4096]{2,1,0:T(4,128)}, f32[4,4,4096]{2,1,0:T(4,128)}) custom-call(bf16[256,128]{1,0:T(8,128)(2,1)S(1)} %bitcast.7, s32[32,12]{1,0:T(8,128)} %reshape.23.slots_hbm, s32[1,512]{1,0:T(1,128)} %constant.24.clone.lanes_hbm, bf16[16,512]{1,0:T(8,128)(2,1)} %constant.25.clone.turn_hbm, bf16[3072,512]{1,0:T(8,128)(2,1)} %constant.26.clone.table_hbm), custom_call_target="tpu_custom_call" | custom-call | tf_op jit(solution)/shard_map/inverse/pallas_call | solution.py:532
Async XLA Ops:
  0.6 12.5 %copy-start = (f32[1664,128]{1,0:T(8,128)S(1)}, f32[1664,128]{1,0:T(8,128)}, u32[]{:S(2)}) copy-start(f32[1664,128]{1,0:T(8,128)} %constant.21.clone.gain_ref) | copy-start | bytes 2555908
  0.6 12.5 %copy-start.1 = (bf16[256,256]{1,0:T(8,128)(2,1)S(1)}, bf16[256,256]{1,0:T(8,128)(2,1)}, u32[]{:S(2)}) copy-start(bf16[256,256]{1,0:T(8,128)(2,1)} %constant.22.clone.order_ref) | copy-start | bytes 393220
  6.6 2.2 %collective-permute-start = (bf16[384,512]{1,0:T(8,128)(2,1)S(1)}, bf16[384,512]{1,0:T(8,128)(2,1)S(1)}, u32[]{:S(2)}, u32[]{:S(2)}) collective-permute-start(bf16[384,512]{1,0:T(8,128)(2,1)S(1)} %get-tuple-element.44), channel_id=1, source_target_pairs={{0,1},{1,0},{2,3},{3,2},{4,5},{5,4},{6,7},{7,6},{8,9},{9,8},{10,11... | collective-permute-start | bytes 1179656 | tf_op jit(solution)/shard_map/ppermute | solution.py:462
  8.9 7.9 %collective-permute-start.1 = (bf16[96,512]{1,0:T(8,128)(2,1)S(1)}, bf16[96,512]{1,0:T(8,128)(2,1)S(1)}, u32[]{:S(2)}, u32[]{:S(2)}) collective-permute-start(bf16[96,512]{1,0:T(8,128)(2,1)S(1)} %get-tuple-element.50), channel_id=1, source_target_pairs={{0,2},{1,3},{2,0},{3,1},{4,6},{5,7},{6,4},{7,5},{8,10},{9,11},{10,... | collective-permute-start | bytes 294920 | tf_op jit(solution)/shard_map/ppermute | solution.py:462
  11.6 5.6 %collective-permute-start.2 = (bf16[96,512]{1,0:T(8,128)(2,1)S(1)}, bf16[96,512]{1,0:T(8,128)(2,1)S(1)}, u32[]{:S(2)}, u32[]{:S(2)}) collective-permute-start(bf16[96,512]{1,0:T(8,128)(2,1)S(1)} %get-tuple-element.51), channel_id=1, source_target_pairs={{0,4},{1,5},{2,6},{3,7},{4,0},{5,1},{6,2},{7,3},{8,12},{9,13},{10,... | collective-permute-start | bytes 294920 | tf_op jit(solution)/shard_map/ppermute | solution.py:462
  13.0 5.5 %collective-permute-start.3 = (bf16[96,512]{1,0:T(8,128)(2,1)S(1)}, bf16[96,512]{1,0:T(8,128)(2,1)S(1)}, u32[]{:S(2)}, u32[]{:S(2)}) collective-permute-start(bf16[96,512]{1,0:T(8,128)(2,1)S(1)} %get-tuple-element.52), channel_id=1, source_target_pairs={{0,6},{1,7},{2,4},{3,5},{4,2},{5,3},{6,0},{7,1},{8,14},{9,15},{10,... | collective-permute-start | bytes 294920 | tf_op jit(solution)/shard_map/ppermute | solution.py:462
  16.7 11.7 %copy-start.2 = (bf16[96,96]{1,0:T(8,128)(2,1)S(1)}, bf16[96,96]{1,0:T(8,128)(2,1)}, u32[]{:S(2)}) copy-start(bf16[96,96]{1,0:T(8,128)(2,1)} %constant.23.clone.refs_5_) | copy-start | bytes 55300
  16.7 15.6 %copy-start.3 = (s32[384]{0:T(512)S(1)}, s32[384]{0:T(512)}, u32[]{:S(2)}) copy-start(s32[384]{0:T(512)} %table_hbm.2) | copy-start | bytes 4612
  18.6 5.7 %collective-permute-start.4 = (bf16[24,512]{1,0:T(8,128)(2,1)S(1)}, bf16[24,512]{1,0:T(8,128)(2,1)S(1)}, u32[]{:S(2)}, u32[]{:S(2)}) collective-permute-start(bf16[24,512]{1,0:T(8,128)(2,1)S(1)} %get-tuple-element.61), channel_id=1, source_target_pairs={{0,8},{1,9},{2,10},{3,11},{4,12},{5,13},{6,14},{7,15},{8,0},{9,1},... | collective-permute-start | bytes 73736 | tf_op jit(solution)/shard_map/ppermute | solution.py:462
  20.3 4.9 %collective-permute-start.5 = (bf16[24,512]{1,0:T(8,128)(2,1)S(1)}, bf16[24,512]{1,0:T(8,128)(2,1)S(1)}, u32[]{:S(2)}, u32[]{:S(2)}) collective-permute-start(bf16[24,512]{1,0:T(8,128)(2,1)S(1)} %get-tuple-element.62), channel_id=1, source_target_pairs={{0,16},{1,17},{2,18},{3,19},{4,20},{5,21},{6,22},{7,23},{8,24},{9,... | collective-permute-start | bytes 73736 | tf_op jit(solution)/shard_map/ppermute | solution.py:462
  22.8 5.6 %collective-permute-start.6 = (bf16[24,512]{1,0:T(8,128)(2,1)S(1)}, bf16[24,512]{1,0:T(8,128)(2,1)S(1)}, u32[]{:S(2)}, u32[]{:S(2)}) collective-permute-start(bf16[24,512]{1,0:T(8,128)(2,1)S(1)} %get-tuple-element.63), channel_id=1, source_target_pairs={{0,24},{1,25},{2,26},{3,27},{4,28},{5,29},{6,30},{7,31},{8,16},{9,... | collective-permute-start | bytes 73736 | tf_op jit(solution)/shard_map/ppermute | solution.py:462
  29.6 10.1 %all-to-all-start = ((bf16[32,8,128]{2,1,0:T(8,128)(2,1)}), bf16[32,8,128]{2,1,0:T(8,128)(2,1)S(1)}, u32[]{:S(2)}, u32[]{:S(2)}) async-start(bf16[32,8,128]{2,1,0:T(8,128)(2,1)} %bitcast.4), calls=%async_computation | async-start | bytes 131072 | tf_op jit(solution)/shard_map/all_to_all | solution.py:524

commit v2 on v1

v2 whole, which is shorter than its diff:
```python
import functools

import jax
import jax.numpy as jnp
import numpy as np
from jax import lax
from jax.experimental import pallas as pl
from jax.experimental.pallas import tpu as pltpu
from jax.sharding import Mesh, PartitionSpec as P

NPHI = 4096
BLOCK = 128
SEGMENTS = NPHI // BLOCK
LANES = 128
CHUNK = 192

NT = (((1,), (1,)), ((), ()))
TN = (((0,), (0,)), ((), ()))


def dot(a, b, dims=(((1,), (0,)), ((), ()))):
    return lax.dot_general(a, b, dims, preferred_element_type=jnp.float32)


def high_low(x):
    high = x.astype(jnp.bfloat16)
    return high, (x - high.astype(jnp.float32)).astype(jnp.bfloat16)


def np_high_low(x):
    high = x.astype(np.float32).astype(jnp.bfloat16)
    return high, (x - high.astype(np.float64)).astype(np.float32).astype(jnp.bfloat16)


def analysis_tables(orders):
    m = np.arange(orders, dtype=np.int64)[:, None]
    p = np.arange(BLOCK, dtype=np.int64)[None, :]
    angle = (m * p % NPHI) * (2 * np.pi / NPHI)
    inner = np.concatenate(np_high_low(np.cos(angle)) + np_high_low(-np.sin(angle)), 1)
    half = np.arange(2 * SEGMENTS, dtype=np.int64)[None, :]
    steps = 2 * BLOCK * (half % SEGMENTS) + half // SEGMENTS
    angle = (m * steps % (2 * NPHI)) * (np.pi / NPHI)
    outer = np.concatenate(np_high_low(np.cos(angle) / NPHI) + np_high_low(-np.sin(angle) / NPHI), 1)
    return inner, outer


def bit_groups(devices):
    bits = list(range(1, devices.bit_length() - 1))
    return [bits[i : i + 2] for i in range(0, len(bits), 2)]


def positions(devices):
    order = [0]
    for group in bit_groups(devices):
        order = [p | (v << group[0]) for p in order for v in range(1 << len(group))]
    return order


def slot_rows(orders, slots):
    out = np.zeros((orders // 2, orders), np.float32)
    for block, position in enumerate(positions(orders // slots)):
        for slot in range(slots):
            out[block * slots + slot, position * slots + slot] = 1
    return out.astype(jnp.bfloat16)


def rolled(x, shift):
    return jnp.concatenate([x[:, shift:], x[:, :shift]], 1)


def exclusive_or(table, me, slots):
    orders = table.shape[1]
    block = lax.div(lax.broadcasted_iota(jnp.int32, table.shape, 1), slots)
    for bit in range((orders // slots).bit_length() - 1):
        shift = slots << bit
        swapped = jnp.where((block >> bit) % 2 == 0, rolled(table, shift), rolled(table, orders - shift))
        table = jnp.where(jnp.broadcast_to((me >> bit) & 1, table.shape) == 1, swapped, table)
    return table


def hot(condition):
    return jnp.where(condition, 1.0, 0.0).astype(jnp.bfloat16)


def twice(x):
    return jnp.concatenate([x, x], 1)


def first_kernel(slots, blocks_here, w_hbm, off_hbm, cnt_hbm, ids_hbm, table_hbm, rows_hbm, inner_hbm, outer_hbm,
                 out_ref, table_ref, rows_ref, inner_ref, outer_ref,
                 w_ref, off_ref, cnt_ref, ids_ref, flat_ref, wide_ref, live_w_ref, live_off_ref, sems):
    pairs = (
        (cnt_hbm, cnt_ref), (ids_hbm, ids_ref), (off_hbm, off_ref), (w_hbm, w_ref),
        (table_hbm, flat_ref), (rows_hbm, rows_ref), (inner_hbm, inner_ref), (outer_hbm, outer_ref),
    )
    copies = [pltpu.make_async_copy(a, b, sems.at[i]) for i, (a, b) in enumerate(pairs)]
    for copy in copies[:4]:
        copy.start()
    groups = off_ref.shape[0]
    capacity, devices = ids_ref.shape
    bins, live, _ = live_w_ref.shape
    pack = 16
    key_tiles = (out_ref.shape[0] - bins * live) // pack

    owner = lax.div(lax.broadcasted_iota(jnp.int32, (devices, groups), 1), capacity)
    source = lax.broadcasted_iota(jnp.int32, (devices, groups), 0)
    member = lax.rem(lax.broadcasted_iota(jnp.int32, (capacity, groups), 1), capacity)
    own_row = lax.broadcasted_iota(jnp.int32, (capacity, groups), 0) == member
    for copy in copies[:2]:
        copy.wait()
    counts = jnp.broadcast_to(cnt_ref[...].astype(jnp.float32), (8, devices)).astype(jnp.bfloat16)
    count = dot(counts, hot(source == owner))[0:1, :]
    before = dot(counts, hot(source < owner))[0:1, :]
    number = member[0:1, :].astype(jnp.float32)
    place = jnp.where(number < count, before + number, -1.0).astype(jnp.int32)
    packing = hot(lax.broadcasted_iota(jnp.int32, (key_tiles * LANES, groups), 0) == place)

    ids = dot(ids_ref[...].astype(jnp.float32).astype(jnp.bfloat16), hot(source == owner))
    ids = jnp.sum(jnp.where(own_row, ids, 0.0), axis=0, keepdims=True)
    block = ids.astype(jnp.int32) + owner[0:1, :] * blocks_here
    cycle = lax.div(block, SEGMENTS)
    phase = lax.rem(cycle, 2) * SEGMENTS + lax.rem(block, SEGMENTS)
    row = lax.broadcasted_iota(jnp.int32, (pack, groups), 0)
    keys = jnp.where(row == 0, lax.div(cycle, 16), jnp.where(row == 1, lax.rem(cycle, 16), phase))
    keys = dot(keys.astype(jnp.float32).astype(jnp.bfloat16), packing, NT).astype(jnp.bfloat16)
    for tile in range(key_tiles):
        out_ref[bins * live + tile * pack : bins * live + (tile + 1) * pack, :] = keys[:, tile * LANES : (tile + 1) * LANES]

    for copy in copies[2:4]:
        copy.wait()
    for copy in copies[4:]:
        copy.start()
    packing = packing[:live, :]
    live_off_ref[...] = dot(packing, off_ref[...].astype(jnp.float32).astype(jnp.bfloat16))
    wide_ref[...] = w_ref[...].astype(jnp.float32)
    for b in range(bins):
        live_w_ref[b] = dot(packing, wide_ref[pl.ds(b, groups, stride=bins), :].astype(jnp.bfloat16)).astype(jnp.bfloat16)

    pixel = lax.broadcasted_iota(jnp.int32, (pack, BLOCK), 0)
    pixels = [(pixel + pack * k).astype(jnp.float32).astype(jnp.bfloat16) for k in range(BLOCK // pack)]
    alone = [hot(pixel == i) for i in range(pack)]
    one = jnp.ones((pack, BLOCK), jnp.bfloat16)
    zero = jnp.zeros((pack, BLOCK), jnp.bfloat16)

    def deposit(step, carry):
        start = pl.multiple_of(step * pack, pack)
        weights = [live_w_ref[b, pl.ds(start, pack), :] for b in range(bins)]
        left, right = [], []
        for i in range(pack):
            left.append(jnp.concatenate([w * alone[i] for w in weights], 0))
            at = jnp.broadcast_to(live_off_ref[pl.ds(start + i, 1), :], (pack, BLOCK)).astype(jnp.bfloat16)
            right.append(jnp.concatenate([jnp.where(at == x, one, zero) for x in pixels], 0))
        out = dot(jnp.concatenate(left, 1), jnp.concatenate(right, 1), NT).astype(jnp.bfloat16)
        for b in range(bins):
            out_ref[pl.ds(pl.multiple_of(b * live + start, pack), pack), :] = out[b * pack : (b + 1) * pack, :]
        return carry

    lax.fori_loop(0, live // pack, deposit, 0, unroll=9)
    for copy in copies[4:]:
        copy.wait()
    me = lax.axis_index("blk")
    for axis in ("y", "core"):
        me = me * lax.axis_size(axis) + lax.axis_index(axis)
    table_ref[...] = exclusive_or(flat_ref[...].reshape(table_ref.shape), me, slots)


def add_modes(bins, groups, cycles, groups_ref, inner_ref, outer_ref, add):
    pack = 16
    keys = groups_ref[bins * groups :, :].astype(jnp.float32)
    keys = jnp.concatenate([keys[i * pack : (i + 1) * pack, :] for i in range(keys.shape[0] // pack)], 1)
    cycle = (keys[0:1, :groups] * 16.0 + keys[1:2, :groups]).astype(jnp.int32)
    phase = keys[2:3, :groups].astype(jnp.int32)
    cycle_hot = hot(lax.broadcasted_iota(jnp.int32, (cycles, groups), 0) == cycle)
    half_hot = hot(lax.broadcasted_iota(jnp.int32, (2 * SEGMENTS, groups), 0) == phase)
    phase_hot = jnp.concatenate([half_hot, half_hot], 0)
    deposits = [twice(groups_ref[b * groups : (b + 1) * groups, :]) for b in range(bins)]
    for start in range(0, inner_ref.shape[0], 2 * CHUNK):
        rows = slice(start, start + 2 * CHUNK)
        outer = dot(outer_ref[rows, :], phase_hot)
        outer_cos, outer_sin = outer[:CHUNK, :], outer[CHUNK:, :]
        for b, deposit in enumerate(deposits):
            inner = dot(inner_ref[rows, :], deposit, NT)
            inner_cos, inner_sin = inner[:CHUNK, :], inner[CHUNK:, :]
            real = inner_cos * outer_cos - inner_sin * outer_sin
            imag = inner_cos * outer_sin + inner_sin * outer_cos
            both = dot(jnp.concatenate([real, imag], 0).astype(jnp.bfloat16), cycle_hot, NT)
            for part in range(2):
                value = both[part * CHUNK : (part + 1) * CHUNK, :]
                for tile in range(cycles // LANES):
                    add(b * (cycles // LANES) + tile, start + part, value[:, tile * LANES : (tile + 1) * LANES])


def own_kernel(bins, groups, cycles, groups_ref, table_ref, rows_ref, inner_ref, outer_ref, out_ref, inner_out, outer_out):
    count, orders = rows_ref.shape
    held = hot(lax.broadcasted_iota(jnp.int32, (orders, orders), 0) == table_ref[...])
    for start in range(0, count, CHUNK):
        pick = dot(rows_ref[start : start + CHUNK, :], held, NT).astype(jnp.bfloat16)
        inner = dot(pick, inner_ref[...]).astype(jnp.bfloat16)
        outer = dot(pick, outer_ref[...]).astype(jnp.bfloat16)
        for part in range(2):
            rows = slice(2 * start + part * CHUNK, 2 * start + (part + 1) * CHUNK)
            inner_out[rows, :] = inner[:, part * 2 * BLOCK : (part + 1) * 2 * BLOCK]
            outer_out[rows, :] = outer[:, part * BLOCK : (part + 1) * BLOCK]

    def add(tile, first, value):
        out_ref.at[tile][pl.ds(first, value.shape[0], stride=2), :] = value

    add_modes(bins, groups, cycles, groups_ref, inner_out, outer_out, add)


def split_sum(parts, tile, keep_ref, send_refs):
    rows = keep_ref.shape[0]
    lanes = slice(tile * LANES, (tile + 1) * LANES)
    for i, out_ref in enumerate((keep_ref, *send_refs)):
        value = sum(part(slice(i * rows, (i + 1) * rows), lanes) for part in parts)
        out_ref[:, lanes] = value.astype(out_ref.dtype)


def other_kernel(bins, groups, cycles, groups_ref, inner_ref, outer_ref, own_ref, keep_ref, *refs):
    *send_refs, other_ref = refs

    def add(tile, first, value):
        other_ref.at[tile][pl.ds(first, value.shape[0], stride=2), :] = value

    add_modes(bins, groups, cycles, groups_ref, inner_ref, outer_ref, add)
    for tile in range(own_ref.shape[0]):
        parts = (lambda rows, lanes: own_ref[tile, rows, :], lambda rows, lanes: other_ref[tile, rows, :])
        split_sum(parts, tile, keep_ref, send_refs)


def merge_kernel(count, kept_ref, *refs):
    arrived, outs = refs[:count], refs[count:]
    for tile in range(kept_ref.shape[1] // LANES):
        parts = [lambda rows, lanes, ref=ref: ref[rows, lanes].astype(jnp.float32) for ref in (kept_ref, *arrived)]
        split_sum(parts, tile, outs[0], outs[1:])


def gain_column(degrees):
    l = np.arange(degrees, dtype=np.float32)
    return np.where(l > 0.5, np.float32(-20000.0) / np.maximum(l * (l + 1), np.float32(1)), np.float32(0)).astype(np.float32)[:, None] * np.ones((1, BLOCK), np.float32)


def interleave(cycles, cycles_here):
    out = np.zeros((2 * cycles, 2 * cycles), np.float32)
    for f in range(2):
        for c in range(cycles):
            out[f * cycles + c, (c // cycles_here * 2 + f) * cycles_here + c % cycles_here] = 1
    return out.astype(jnp.bfloat16)


def response_kernel(start, from_hbm, rest, legendre_ref, gain_ref, order_ref, out_ref, *refs):
    count = out_ref.shape[0]
    copies = []
    if from_hbm:
        source, (*rest_refs, legendre_ref, sems) = legendre_ref, refs
        copies = [pltpu.make_async_copy(source.at[start + i], legendre_ref.at[i], sems.at[i]) for i in range(count)]
        for ref in rest_refs:
            copies.append(pltpu.make_async_copy(source.at[pl.ds(start + count, rest)], ref, sems.at[count]))
        for copy in copies:
            copy.start()
        start = 0
    for slot in range(count):
        if from_hbm:
            copies[slot].wait()
        basis = legendre_ref[start + slot]
        cycles = basis.shape[1]
        gain = jnp.concatenate([gain_ref[...]] * (cycles // BLOCK), 1)
        gained = (basis.astype(jnp.float32) * gain).astype(jnp.bfloat16)
        high, low = high_low(dot(basis, jnp.concatenate([basis, gained], 1), TN))
        out_ref[slot, :cycles, :] = dot(high, order_ref[...]).astype(jnp.bfloat16)
        out_ref[slot, cycles:, :] = dot(low, order_ref[...]).astype(jnp.bfloat16)
    for copy in copies[count:]:
        copy.wait()


def slot_order(slots, bins):
    out = np.zeros((slots * 2 * bins, slots * 2 * bins), np.float32)
    for b in range(bins):
        for c in range(2):
            for t in range(slots):
                out[(t * 2 + c) * bins + b, (b * slots + t) * 2 + c] = 1
    return out.astype(jnp.bfloat16)


def synthesis_kernel(arrivals, pieces, kept_ref, *refs):
    partials, refs = refs[:arrivals], refs[arrivals:]
    response_refs, (order_ref, out_ref) = refs[:pieces], refs[pieces:]
    cycles = response_refs[0].shape[1] // 2
    bins = kept_ref.shape[1] // cycles
    slots = kept_ref.shape[0] // 2
    responses = [ref.at[i] for ref in response_refs for i in range(ref.shape[0])]
    total = kept_ref[...]
    for ref in partials:
        total = total + ref[...].astype(jnp.float32)
    modes = jnp.concatenate([total[:, b * cycles : (b + 1) * cycles] for b in range(bins)], 0)
    high, low = high_low(modes)
    high = dot(order_ref[...], high)
    low = dot(order_ref[...], low)
    per_slot = 2 * bins
    parts = []
    for t in range(slots):
        rows = slice(t * per_slot, (t + 1) * per_slot)
        left = jnp.concatenate([high[rows, :], low[rows, :]], 0).astype(jnp.bfloat16)
        part = dot(twice(left), responses[t][...])
        parts.append(part[:per_slot, :] + part[per_slot:, :])
    parts.append(jnp.zeros((128 - slots * per_slot, 2 * cycles), jnp.float32))
    result = jnp.concatenate(parts, 0)
    out_ref[...] = jnp.transpose(result).astype(jnp.bfloat16)


def order_classes(orders):
    return [np.arange(0, orders, 4), np.arange(2, orders, 4), np.arange(1, orders, 2)]


def inverse_tables(orders):
    quarter = NPHI // 4
    k = np.arange(quarter, dtype=np.int64)[None, :]
    rows = []
    for m in order_classes(orders):
        angle = (m[:, None] * k % NPHI) * (2 * np.pi / NPHI)
        rows += [np.cos(angle), -np.sin(angle)]
    return np.concatenate(np.split(np.concatenate(rows), quarter // 512, axis=1)).astype(np.float32).astype(jnp.bfloat16)


def padded(count):
    return -(-count // LANES) * LANES


def order_lanes(orders):
    out = []
    for m in order_classes(orders):
        out.append(np.concatenate([m, np.full(padded(len(m)) - len(m), -1)]))
    return np.concatenate(out).astype(np.int32)[None, :]


def turn_rows(order_row):
    m = np.maximum(order_row[0], 0).astype(np.float64)
    weight = np.where(order_row[0] == 0, 1.0, 2.0)
    sign = np.where(order_row[0] % 4 == 3, 1.0, -1.0)
    parts = np_high_low(np.cos(np.pi * m / NPHI) * weight) + np_high_low(np.sin(np.pi * m / NPHI) * weight)
    parts = parts + (weight.astype(jnp.bfloat16), sign.astype(jnp.bfloat16))
    return np.stack(parts + (np.zeros_like(parts[0]),) * 10)


def part_rows(part, bins, cycles_here):
    shape = (2 * bins * cycles_here, 4 * bins * cycles_here)
    row = lax.broadcasted_iota(jnp.int32, shape, 0)
    column = lax.broadcasted_iota(jnp.int32, shape, 1)
    cycle = lax.rem(row, cycles_here)
    bin_number = lax.rem(lax.div(row, cycles_here), bins)
    filter_number = lax.div(row, cycles_here * bins)
    return hot(column == ((filter_number * cycles_here + cycle) * 2 + part) * bins + bin_number)


def inverse_kernel(arrived_ref, slots_hbm, turn_hbm, table_hbm, kappa_hbm, potential_hbm,
                   slots_ref, turn_ref, table_ref, wide_ref, kappa_ref, potential_ref, sems, out_sems):
    copies = [
        pltpu.make_async_copy(a, b, sems.at[i])
        for i, (a, b) in enumerate(((slots_hbm, slots_ref), (turn_hbm, turn_ref)))
    ]
    quarter = NPHI // 4
    chunk = table_ref.shape[1]
    chunks = quarter // chunk
    part = table_ref.shape[0] // chunks
    for i in range(chunks):
        rows = pl.ds(i * part, part)
        copies.append(pltpu.make_async_copy(table_hbm.at[rows], table_ref.at[rows], sems.at[2 + i]))
    for copy in copies:
        copy.start()
    devices, slots = slots_ref.shape
    bins, cycles_here, _ = kappa_ref.shape
    order_count = part // 2
    per_slot = 2 * bins
    per_source = 2 * cycles_here
    wide_ref[...] = arrived_ref[...].astype(jnp.float32)
    turned = [jnp.transpose(wide_ref[pl.ds(i, devices, stride=per_source), :]) for i in range(per_source)]
    few, many = order_count // 4, order_count // 2
    starts = [0, padded(few), 2 * padded(few)]
    lane = lax.broadcasted_iota(jnp.int32, (1, turn_ref.shape[1]), 1)
    orders = jnp.where(lane < few, 4 * lane, -1)
    within = lane - starts[1]
    orders = jnp.where((within >= 0) & (within < few), 4 * within + 2, orders)
    within = lane - starts[2]
    orders = jnp.where((within >= 0) & (within < many), 2 * within + 1, orders)
    for copy in copies[:2]:
        copy.wait()
    lefts, picks = [], []
    for t in range(slots):
        lefts.append(jnp.concatenate([x[t * per_slot : (t + 1) * per_slot, :] for x in turned], 0))
        picks.append(hot(slots_ref[:, t : t + 1] == orders))
    spectrum = dot(jnp.concatenate(lefts, 1).astype(jnp.bfloat16), jnp.concatenate(picks, 0))
    spectrum = spectrum.astype(jnp.bfloat16)
    real_in = dot(part_rows(0, bins, cycles_here), spectrum)
    imag_in = dot(part_rows(1, bins, cycles_here), spectrum)
    turn = turn_ref[...].astype(jnp.float32)
    odd = lax.rem(lax.rem(lax.broadcasted_iota(jnp.int32, real_in.shape, 0), cycles_here), 2) == 1
    turn_cos = jnp.where(odd, turn[0:1, :] + turn[1:2, :], turn[4:5, :])
    turn_sin = jnp.where(odd, turn[2:3, :] + turn[3:4, :], 0.0)
    real = real_in * turn_cos - imag_in * turn_sin
    imag = real_in * turn_sin + imag_in * turn_cos
    sign = turn[5:6, starts[2] :]
    count = real.shape[0]
    lefts = []
    for index, start in enumerate(starts):
        lanes = slice(start, start + (few if index < 2 else many))
        cos_rows, sin_rows = [real[:, lanes]], [imag[:, lanes]]
        if index == 2:
            cos_rows.append(imag[:, lanes] * sign[:, :many])
            sin_rows.append(-real[:, lanes] * sign[:, :many])
        for rows in (cos_rows, sin_rows):
            lefts.append(jnp.concatenate([y for x in rows for y in high_low(x)], 0))
    results = []
    for index in range(chunks):
        copies[2 + index].wait()
        row = index * part
        sums = []
        for at in range(3):
            height = few if at < 2 else many
            both = dot(lefts[2 * at], table_ref[row : row + height, :])
            both = both + dot(lefts[2 * at + 1], table_ref[row + height : row + 2 * height, :])
            row += 2 * height
            sums += [both[i : i + count, :] + both[i + count : i + 2 * count, :] for i in range(0, both.shape[0], 2 * count)]
        even, other = sums[0] + sums[1], sums[0] - sums[1]
        values = (even + sums[2], other + sums[3], even - sums[2], other - sums[3])
        for j, value in enumerate(values):
            lanes = pl.ds(j * quarter + index * chunk, chunk)
            for f, (out_ref, out_hbm) in enumerate(((kappa_ref, kappa_hbm), (potential_ref, potential_hbm))):
                for b in range(bins):
                    at = (f * bins + b) * cycles_here
                    out_ref[b, :, lanes] = value[at : at + cycles_here, :]
                copy = pltpu.make_async_copy(out_ref.at[:, :, lanes], out_hbm.at[:, :, lanes], out_sems.at[len(results)])
                copy.start()
                results.append(copy)
    for copy in results:
        copy.wait()


def in_hbm(x):
    return pltpu.with_memory_space_constraint(jnp.asarray(x), pltpu.HBM)


def params(orders):
    small = 14 if orders <= 512 else 56
    return pltpu.CompilerParams(vmem_limit_bytes=small * 1024 * 1024)


def per_device(weights, offsets, counts, block_ids, m_table, legendre):
    axes = ("blk", "y", "core")
    _, devices, capacity, bins, _ = weights.shape
    slots, degrees, cycles = legendre.shape
    orders = m_table.shape[0]
    groups = devices * capacity
    cycles_here = cycles // devices
    width = bins * cycles
    staged = legendre.size <= 4 * 1024 * 1024
    limits = params(orders)
    hbm = pl.BlockSpec(memory_space=pltpu.HBM)
    vmem = pl.BlockSpec(memory_space=pltpu.VMEM)

    def shaped(*shape, dtype=jnp.bfloat16):
        return jax.ShapeDtypeStruct(shape, dtype)

    rows = slot_rows(orders, slots)
    inner, outer = analysis_tables(orders)
    live = (capacity + 1) * devices // 2
    key_rows = -(-live // LANES) * 16
    shapes = [
        shaped(bins * live + key_rows, BLOCK),
        shaped(1, orders, dtype=jnp.int32),
        shaped(*rows.shape),
        shaped(*inner.shape),
        shaped(*outer.shape),
    ]
    operands = [
        weights.reshape(groups * bins, BLOCK),
        offsets.reshape(groups, BLOCK),
        counts,
        jnp.transpose(block_ids[0]),
        m_table,
        rows,
        inner,
        outer,
    ]
    deposits, *shared = pl.pallas_call(
        functools.partial(first_kernel, slots, cycles_here * SEGMENTS),
        in_specs=[hbm] * len(operands),
        out_specs=(vmem,) * len(shapes),
        out_shape=tuple(shapes),
        scratch_shapes=[
            pltpu.VMEM((groups * bins, BLOCK), jnp.bfloat16),
            pltpu.VMEM((groups, BLOCK), jnp.int32),
            pltpu.VMEM((1, devices), jnp.int32),
            pltpu.VMEM((capacity, devices), jnp.int32),
            pltpu.VMEM((orders,), jnp.int32),
            pltpu.VMEM((groups * bins, BLOCK), jnp.float32),
            pltpu.VMEM((bins, live, BLOCK), jnp.bfloat16),
            pltpu.VMEM((live, BLOCK), jnp.float32),
            pltpu.SemaphoreType.DMA((len(operands),)),
        ],
        compiler_params=limits,
        name="deposit",
    )(*[in_hbm(x) for x in operands])
    basis, moved = legendre, 0

    def swap(x, mask):
        return lax.ppermute(x, axes, [(i, i ^ mask) for i in range(devices)])

    other = swap(deposits, 1)
    cost = pl.CostEstimate(flops=8 * orders * 256 * bins * live, bytes_accessed=4 * orders * width, transcendentals=0)
    modes_shape = (width // LANES, orders, LANES)
    own, own_inner, own_outer = pl.pallas_call(
        functools.partial(own_kernel, bins, live, cycles),
        in_specs=[vmem] * 5,
        out_specs=(vmem,) * 3,
        out_shape=(
            shaped(*modes_shape, dtype=jnp.float32),
            shaped(orders, inner.shape[1] // 2),
            shaped(orders, outer.shape[1] // 2),
        ),
        compiler_params=limits,
        cost_estimate=cost,
        name="own_groups",
    )(deposits, *shared)

    groups_of_bits = bit_groups(devices)
    stages = len(groups_of_bits)
    gain, order = gain_column(degrees), interleave(cycles, cycles_here)
    blocks = devices // 2
    kernel, inputs = functools.partial(other_kernel, bins, live, cycles), (other, own_inner, own_outer, own)
    scratch = [pltpu.VMEM(modes_shape, jnp.float32)]
    responses = []
    for stage, bits in enumerate(groups_of_bits):
        ways = 1 << len(bits)
        blocks //= ways
        rows_here = blocks * 2 * slots
        kept, *sends = pl.pallas_call(
            kernel,
            in_specs=[vmem] * len(inputs),
            out_specs=(vmem,) * ways,
            out_shape=(shaped(rows_here, width, dtype=jnp.float32),) + (shaped(rows_here, width),) * (ways - 1),
            scratch_shapes=scratch,
            compiler_params=limits,
            name="merge" if stage else "other_groups",
        )(*inputs)
        *sends, basis = lax.optimization_barrier((*sends, basis))
        if stage == 0 or not staged:
            basis = in_hbm(basis)
        arrived = [swap(x, (i + 1) << bits[0]) for i, x in reversed(list(enumerate(sends)))]
        first, last = (min(slots, slots * 2 * k * (2 * stages - k) // (2 * stages * stages)) for k in (stage, stage + 1))
        count = last - first
        from_hbm = stage == 0 or not staged
        rest = slots - last if stage == 0 and staged else 0
        scratch = [pltpu.VMEM((count, degrees, cycles), jnp.bfloat16), pltpu.SemaphoreType.DMA((count + 1,))]
        response, *rests = pl.pallas_call(
            functools.partial(response_kernel, first if from_hbm else first - moved, from_hbm, rest),
            in_specs=[hbm if from_hbm else vmem, vmem, vmem],
            out_specs=(vmem,) * (2 if rest else 1),
            out_shape=(shaped(count, 2 * cycles, 2 * cycles),) + ((shaped(rest, degrees, cycles),) if rest else ()),
            scratch_shapes=scratch if from_hbm else [],
            compiler_params=limits,
            cost_estimate=pl.CostEstimate(
                flops=6 * count * degrees * cycles * cycles, bytes_accessed=2 * count * degrees * cycles, transcendentals=0
            ),
            name="response",
        )(basis, gain, order)
        if rests:
            basis, moved = rests[0], last
        *arrived, response = lax.optimization_barrier((*arrived, response))
        responses.append(response)
        kernel, inputs, scratch = functools.partial(merge_kernel, len(arrived)), (kept, *arrived), []

    outgoing = pl.pallas_call(
        functools.partial(synthesis_kernel, len(inputs) - 1, len(responses)),
        in_specs=[vmem] * (len(inputs) + len(responses) + 1),
        out_specs=vmem,
        out_shape=shaped(2 * cycles, 128),
        compiler_params=limits,
        name="synthesis",
    )(*inputs, *responses, slot_order(slots, bins))
    outgoing = outgoing.reshape(devices, 2 * cycles_here, 128)
    outgoing, held = lax.optimization_barrier((outgoing, m_table))
    arrived = lax.all_to_all(outgoing, axes, split_axis=0, concat_axis=0, tiled=True)
    arrived = arrived.reshape(2 * cycles, 128)
    if staged:
        arrived = pltpu.with_memory_space_constraint(arrived, pltpu.VMEM)

    lanes = order_lanes(orders)
    constants = [turn_rows(lanes), inverse_tables(orders)]
    chunks = NPHI // 4 // constants[-1].shape[1]
    map_shape = shaped(bins, cycles_here, NPHI, dtype=jnp.float32)
    return pl.pallas_call(
        inverse_kernel,
        in_specs=[vmem] + [hbm] * 3,
        out_specs=(hbm, hbm),
        out_shape=(map_shape, map_shape),
        scratch_shapes=[
            pltpu.VMEM((devices, slots), jnp.int32),
            *[pltpu.VMEM(x.shape, x.dtype) for x in constants],
            pltpu.VMEM((2 * cycles, 128), jnp.float32),
            pltpu.VMEM(map_shape.shape, jnp.float32),
            pltpu.VMEM(map_shape.shape, jnp.float32),
            pltpu.SemaphoreType.DMA((2 + chunks,)),
            pltpu.SemaphoreType.DMA((8 * chunks,)),
        ],
        compiler_params=limits,
        name="inverse",
    )(arrived, in_hbm(held.reshape(devices, slots)), *[in_hbm(x) for x in constants])


def solution(mesh):
    blocks, columns = mesh.devices.shape
    fine = Mesh(mesh.devices.reshape(blocks, columns // 2, 2), ("blk", "y", "core"))
    axes = ("blk", "y", "core")
    placed = (
        P(axes, None, None, None, None),
        P(axes, None, None, None),
        P(axes, None),
        P(axes, None, None),
        P(),
        P(axes, None, None),
    )
    return jax.shard_map(
        per_device,
        mesh=fine,
        in_specs=placed,
        out_specs=(P(None, axes, None), P(None, axes, None)),
        check_vma=False,
    )
```

time: 43.3 us -> 41.9 us (0.968)
  waiting for transfers between devices: 12.6 us -> 9.48 us
  starting transfers between devices: 11.9 us -> 13.8 us
    ppermute x7, waiting for transfers between devices: 5.9 us -> 2.79 us  [swap(): return lax.ppermute(x, axes, [(i, i ^ mask) for i in range(devices)])]
    all_to_all x1, starting transfers between devices: 2.72 us -> 4.27 us  [per_device(): lax.all_to_all(outgoing, axes, split_axis=0, concat_axis=0, tiled=True)]
    pallas_call x5, Pallas kernels: 15.8 us -> 14.8 us  [the longest x2 7.37 us: per_device(): pl.pallas_call(functools.partial(response_kernel, first if from_hbm else...]
    pallas_call x2, Pallas kernels: 0.13 us -> 0.93 us  [per_device(): pl.pallas_call(kernel, in_specs=[vmem] * len(inputs), out_specs=(vmem,) *...]
  transfers between devices with their start and end apart: 8 -> 8, of which waited for: 5 -> 2; matrix products, arithmetic and copies ran while one was open for 2% -> 2% of each run, Pallas kernels for 15% -> 21%
where the time goes in v2:
time: 41.9 us; the launch traced here: 41.6 us
  Pallas kernels  16.9 us (40%)
  starting transfers between devices  13.8 us (33%)
  waiting for transfers between devices  9.48 us (23%)
  between operations  0.76 us (2%)
  local copies, waits for them, and re-layouts  0.74 us (2%)
    ppermute x7, starting transfers between devices, swap(): return lax.ppermute(x, axes, [(i, i ^ mask) for i in range(devices)])  9.48 us
    pallas_call x2, Pallas kernels, per_device(): pl.pallas_call(functools.partial(response_kernel, first if from_hbm else...  7.37 us
    all_to_all x1, waiting for transfers between devices, per_device(): lax.all_to_all(outgoing, axes, split_axis=0, concat_axis=0, tiled=True)  6.69 us
    all_to_all x1, starting transfers between devices, per_device(): lax.all_to_all(outgoing, axes, split_axis=0, concat_axis=0, tiled=True)  4.27 us
    pallas_call x1, Pallas kernels, per_device(): pl.pallas_call(functools.partial(first_kernel, slots, cycles_here * SEGME...  3.54 us
    ppermute x7, waiting for transfers between devices, swap(): return lax.ppermute(x, axes, [(i, i ^ mask) for i in range(devices)])  2.79 us
    pallas_call x1, Pallas kernels, per_device(): pl.pallas_call(inverse_kernel, in_specs=[vmem] + [hbm] * 3, out_specs=(hb...  2.68 us
    pallas_call x1, Pallas kernels, per_device(): pl.pallas_call(functools.partial(own_kernel, bins, live, cycles), in_spec...  1.26 us
  transfers between devices with their start and end apart: 8, of which 2 were waited for; matrix products, arithmetic and copies ran while one was open for 2% of the time, Pallas kernels for 21%

profile of v2, /device:TPU:0, one launch (start us, length us, event | category | flops | bytes accessed | tf_op | source)
XLA Modules:
  0.0 41.6 jit_solution(3442270784920895816)
XLA Ops:
  0.6 3.5 %deposit.1 = (bf16[608,128]{1,0:T(8,128)(2,1)S(1)}, s32[1,384]{1,0:T(1,128)S(1)}, bf16[192,384]{1,0:T(8,128)(2,1)S(1)}, bf16[384,512]{1,0:T(8,128)(2,1)S(1)}, bf16[384,256]{1,0:T(8,128)(2,1)S(1)}) custom-call(bf16[1024,128]{1,0:T(8,128)(2,1)} %bitcast.8, s32[256,128]{1,0:T(8,128)} %bitcast.9, s32[1,32]{1,0:T(1,128)} %cnt_hbm.1, s32[8,32]{1,0:T(8,128)} %bitcast.10, ...), custom_call_target="tpu_custom_call" | custom-call | tf_op jit(solution)/shard_map/deposit/pallas_call | solution.py:484
  4.2 0.0 copy-start
  4.2 0.0 copy-start.1
  4.2 0.5 %collective-permute-start = (bf16[608,128]{1,0:T(8,128)(2,1)S(1)}, bf16[608,128]{1,0:T(8,128)(2,1)S(1)}, u32[]{:S(2)}, u32[]{:S(2)}) collective-permute-start(bf16[608,128]{1,0:T(8,128)(2,1)S(1)} %get-tuple-element.38.groups_ref), channel_id=1, source_target_pairs={{0,1},{1,0},{2,3},{3,2},{4,5},{5,4},{6,7},{7,6},{8,9},{9,8},{10,11... | collective-permute-start | bytes 466952 | tf_op jit(solution)/shard_map/ppermute | solution.py:506
  4.7 1.3 %own_groups.1 = (f32[4,384,128]{2,1,0:T(8,128)S(1)}, bf16[384,256]{1,0:T(8,128)(2,1)S(1)}, bf16[384,128]{1,0:T(8,128)(2,1)S(1)}) custom-call(bf16[608,128]{1,0:T(8,128)(2,1)S(1)} %get-tuple-element.38.groups_ref, s32[1,384]{1,0:T(1,128)S(1)} %get-tuple-element.39.table_ref, bf16[192,384]{1,0:T(8,128)(2,1)S(1)} %get-tuple-element.40.rows_ref, ...), custom_call_target="tpu_custom_call" | custom-call | flops 452984832 | bytes 786432 | tf_op jit(solution)/shard_map/own_groups/pallas_call | solution.py:511
  6.0 0.0 collective-permute-done.groups_ref
  6.0 0.9 %other_groups.1 = (f32[96,512]{1,0:T(8,128)S(1)}, bf16[96,512]{1,0:T(8,128)(2,1)S(1)}, bf16[96,512]{1,0:T(8,128)(2,1)S(1)}, bf16[96,512]{1,0:T(8,128)(2,1)S(1)}) custom-call(bf16[608,128]{1,0:T(8,128)(2,1)S(1)} %collective-permute-done.groups_ref, bf16[384,256]{1,0:T(8,128)(2,1)S(1)} %get-tuple-element.43.inner_ref, ...), custom_call_target="tpu_custom_call" | custom-call | tf_op jit(solution)/shard_map/other_groups/pallas_call | solution.py:536
  6.9 3.6 %collective-permute-start.1 = (bf16[96,512]{1,0:T(8,128)(2,1)S(1)}, bf16[96,512]{1,0:T(8,128)(2,1)S(1)}, u32[]{:S(2)}, u32[]{:S(2)}) collective-permute-start(bf16[96,512]{1,0:T(8,128)(2,1)S(1)} %get-tuple-element.50), channel_id=1, source_target_pairs={{0,6},{1,7},{2,4},{3,5},{4,2},{5,3},{6,0},{7,1},{8,14},{9,15},{10,... | collective-permute-start | bytes 294920 | tf_op jit(solution)/shard_map/ppermute | solution.py:506
  10.5 0.5 %collective-permute-start.2 = (bf16[96,512]{1,0:T(8,128)(2,1)S(1)}, bf16[96,512]{1,0:T(8,128)(2,1)S(1)}, u32[]{:S(2)}, u32[]{:S(2)}) collective-permute-start(bf16[96,512]{1,0:T(8,128)(2,1)S(1)} %get-tuple-element.51), channel_id=1, source_target_pairs={{0,4},{1,5},{2,6},{3,7},{4,0},{5,1},{6,2},{7,3},{8,12},{9,13},{10,... | collective-permute-start | bytes 294920 | tf_op jit(solution)/shard_map/ppermute | solution.py:506
  11.0 0.1 collective-permute-start.3
  11.1 0.0 copy-done
  11.1 0.0 copy-done.1
  11.1 6.1 %response.2 = (bf16[9,256,256]{2,1,0:T(8,128)(2,1)S(1)}, bf16[3,1664,128]{2,1,0:T(8,128)(2,1)S(1)}) custom-call(bf16[12,1664,128]{2,1,0:T(8,128)(2,1)} %legendre_ref, f32[1664,128]{1,0:T(8,128)S(1)} %copy-done, bf16[256,256]{1,0:T(8,128)(2,1)S(1)} %copy-done.1), custom_call_target="tpu_custom_call" | custom-call | flops 1472200704 | bytes 3833856 | tf_op jit(solution)/shard_map/response/pallas_call | solution.py:554
  17.2 0.0 collective-permute-done.1.refs_0_
  17.2 0.0 collective-permute-done.2.refs_1_
  17.3 0.0 collective-permute-done.3.refs_2_
  17.3 0.0 copy-start.2
  17.3 0.1 merge.1
  17.3 4.1 %collective-permute-start.4 = (bf16[24,512]{1,0:T(8,128)(2,1)S(1)}, bf16[24,512]{1,0:T(8,128)(2,1)S(1)}, u32[]{:S(2)}, u32[]{:S(2)}) collective-permute-start(bf16[24,512]{1,0:T(8,128)(2,1)S(1)} %get-tuple-element.63), channel_id=1, source_target_pairs={{0,24},{1,25},{2,26},{3,27},{4,28},{5,29},{6,30},{7,31},{8,16},{9,... | collective-permute-start | bytes 73736 | tf_op jit(solution)/shard_map/ppermute | solution.py:506
  21.4 0.0 collective-permute-start.5
  21.4 0.6 %collective-permute-start.6 = (bf16[24,512]{1,0:T(8,128)(2,1)S(1)}, bf16[24,512]{1,0:T(8,128)(2,1)S(1)}, u32[]{:S(2)}, u32[]{:S(2)}) collective-permute-start(bf16[24,512]{1,0:T(8,128)(2,1)S(1)} %get-tuple-element.65), channel_id=1, source_target_pairs={{0,8},{1,9},{2,10},{3,11},{4,12},{5,13},{6,14},{7,15},{8,0},{9,1},... | collective-permute-start | bytes 73736 | tf_op jit(solution)/shard_map/ppermute | solution.py:506
  22.0 1.3 %response.3.refs_4_ = bf16[3,256,256]{2,1,0:T(8,128)(2,1)S(1)} custom-call(bf16[3,1664,128]{2,1,0:T(8,128)(2,1)S(1)} %get-tuple-element.66.legendre_ref, f32[1664,128]{1,0:T(8,128)S(1)} %copy-done, bf16[256,256]{1,0:T(8,128)(2,1)S(1)} %copy-done.1), custom_call_target="tpu_custom_call" | custom-call | flops 490733568 | bytes 1277952 | tf_op jit(solution)/shard_map/response/pallas_call | solution.py:554
  23.3 0.0 copy-start.3
  23.3 0.0 collective-permute-done.4.refs_0_
  23.4 2.8 %collective-permute-done.5.refs_1_ = bf16[24,512]{1,0:T(8,128)(2,1)S(1)} collective-permute-done((bf16[24,512]{1,0:T(8,128)(2,1)S(1)}, bf16[24,512]{1,0:T(8,128)(2,1)S(1)}, u32[]{:S(2)}, u32[]{:S(2)}) %collective-permute-start.5) | collective-permute-done | bytes 24608 | tf_op jit(solution)/shard_map/ppermute | solution.py:506
  26.1 0.0 collective-permute-done.6.refs_2_
  26.1 0.0 copy-done.2
  26.1 1.1 %synthesis.1 = bf16[256,128]{1,0:T(8,128)(2,1)} custom-call(f32[24,512]{1,0:T(8,128)S(1)} %get-tuple-element.58.kept_ref, bf16[24,512]{1,0:T(8,128)(2,1)S(1)} %collective-permute-done.4.refs_0_, bf16[24,512]{1,0:T(8,128)(2,1)S(1)} %collective-permute-done.5.refs_1_, bf16[24,512]{1,0:T(8,128)(2,1)S(1)} %collective-permute-done.6.refs_2_, ...), custom_call_target="tpu_custom_call" | custom-call | tf_op jit(solution)/shard_map/synthesis/pallas_call | solution.py:572
  27.3 4.3 %all-to-all-start = ((bf16[32,8,128]{2,1,0:T(8,128)(2,1)}), bf16[32,8,128]{2,1,0:T(8,128)(2,1)S(1)}, u32[]{:S(2)}, u32[]{:S(2)}) async-start(bf16[32,8,128]{2,1,0:T(8,128)(2,1)} %bitcast.4), calls=%async_computation | async-start | bytes 131072 | tf_op jit(solution)/shard_map/all_to_all | solution.py:582
  31.6 0.0 copy-done.3
  31.6 0.7 %reshape.23.slots_hbm = s32[32,12]{1,0:T(8,128)} reshape(s32[384]{0:T(512)S(1)} %copy-done.3) | data formatting | bytes 3072 | tf_op jit(solution)/shard_map/reshape | solution.py:607
  32.3 6.7 %all-to-all-done = bf16[32,8,128]{2,1,0:T(8,128)(2,1)S(1)} async-done(((bf16[32,8,128]{2,1,0:T(8,128)(2,1)}), bf16[32,8,128]{2,1,0:T(8,128)(2,1)S(1)}, u32[]{:S(2)}, u32[]{:S(2)}) %all-to-all-start) | async-done | bytes 65568 | tf_op jit(solution)/shard_map/all_to_all | solution.py:582
  39.0 2.7 %inverse.1 = (f32[4,4,4096]{2,1,0:T(4,128)}, f32[4,4,4096]{2,1,0:T(4,128)}) custom-call(bf16[256,128]{1,0:T(8,128)(2,1)S(1)} %bitcast.7, s32[32,12]{1,0:T(8,128)} %reshape.23.slots_hbm, bf16[16,512]{1,0:T(8,128)(2,1)} %constant.22.clone.turn_hbm, bf16[1536,512]{1,0:T(8,128)(2,1)} %constant.23.clone.table_hbm), custom_call_target="tpu_custom_call" | custom-call | tf_op jit(solution)/shard_map/inverse/pallas_call | solution.py:591
Async XLA Ops:
  4.2 7.0 %copy-start = (f32[1664,128]{1,0:T(8,128)S(1)}, f32[1664,128]{1,0:T(8,128)}, u32[]{:S(2)}) copy-start(f32[1664,128]{1,0:T(8,128)} %constant.19.clone.gain_ref) | copy-start | bytes 2555908
  4.2 6.9 %copy-start.1 = (bf16[256,256]{1,0:T(8,128)(2,1)S(1)}, bf16[256,256]{1,0:T(8,128)(2,1)}, u32[]{:S(2)}) copy-start(bf16[256,256]{1,0:T(8,128)(2,1)} %constant.20.clone.order_ref) | copy-start | bytes 393220
  4.2 1.8 %collective-permute-start = (bf16[608,128]{1,0:T(8,128)(2,1)S(1)}, bf16[608,128]{1,0:T(8,128)(2,1)S(1)}, u32[]{:S(2)}, u32[]{:S(2)}) collective-permute-start(bf16[608,128]{1,0:T(8,128)(2,1)S(1)} %get-tuple-element.38.groups_ref), channel_id=1, source_target_pairs={{0,1},{1,0},{2,3},{3,2},{4,5},{5,4},{6,7},{7,6},{8,9},{9,8},{10,11... | collective-permute-start | bytes 466952 | tf_op jit(solution)/shard_map/ppermute | solution.py:506
  6.9 10.4 %collective-permute-start.1 = (bf16[96,512]{1,0:T(8,128)(2,1)S(1)}, bf16[96,512]{1,0:T(8,128)(2,1)S(1)}, u32[]{:S(2)}, u32[]{:S(2)}) collective-permute-start(bf16[96,512]{1,0:T(8,128)(2,1)S(1)} %get-tuple-element.50), channel_id=1, source_target_pairs={{0,6},{1,7},{2,4},{3,5},{4,2},{5,3},{6,0},{7,1},{8,14},{9,15},{10,... | collective-permute-start | bytes 294920 | tf_op jit(solution)/shard_map/ppermute | solution.py:506
  10.5 6.8 %collective-permute-start.2 = (bf16[96,512]{1,0:T(8,128)(2,1)S(1)}, bf16[96,512]{1,0:T(8,128)(2,1)S(1)}, u32[]{:S(2)}, u32[]{:S(2)}) collective-permute-start(bf16[96,512]{1,0:T(8,128)(2,1)S(1)} %get-tuple-element.51), channel_id=1, source_target_pairs={{0,4},{1,5},{2,6},{3,7},{4,0},{5,1},{6,2},{7,3},{8,12},{9,13},{10,... | collective-permute-start | bytes 294920 | tf_op jit(solution)/shard_map/ppermute | solution.py:506
  11.0 6.2 %collective-permute-start.3 = (bf16[96,512]{1,0:T(8,128)(2,1)S(1)}, bf16[96,512]{1,0:T(8,128)(2,1)S(1)}, u32[]{:S(2)}, u32[]{:S(2)}) collective-permute-start(bf16[96,512]{1,0:T(8,128)(2,1)S(1)} %get-tuple-element.52), channel_id=1, source_target_pairs={{0,2},{1,3},{2,0},{3,1},{4,6},{5,7},{6,4},{7,5},{8,10},{9,11},{10,... | collective-permute-start | bytes 294920 | tf_op jit(solution)/shard_map/ppermute | solution.py:506
  17.3 8.9 %copy-start.2 = (bf16[96,96]{1,0:T(8,128)(2,1)S(1)}, bf16[96,96]{1,0:T(8,128)(2,1)}, u32[]{:S(2)}) copy-start(bf16[96,96]{1,0:T(8,128)(2,1)} %constant.21.clone.refs_5_) | copy-start | bytes 55300
  17.3 6.0 %collective-permute-start.4 = (bf16[24,512]{1,0:T(8,128)(2,1)S(1)}, bf16[24,512]{1,0:T(8,128)(2,1)S(1)}, u32[]{:S(2)}, u32[]{:S(2)}) collective-permute-start(bf16[24,512]{1,0:T(8,128)(2,1)S(1)} %get-tuple-element.63), channel_id=1, source_target_pairs={{0,24},{1,25},{2,26},{3,27},{4,28},{5,29},{6,30},{7,31},{8,16},{9,... | collective-permute-start | bytes 73736 | tf_op jit(solution)/shard_map/ppermute | solution.py:506
  21.4 4.7 %collective-permute-start.5 = (bf16[24,512]{1,0:T(8,128)(2,1)S(1)}, bf16[24,512]{1,0:T(8,128)(2,1)S(1)}, u32[]{:S(2)}, u32[]{:S(2)}) collective-permute-start(bf16[24,512]{1,0:T(8,128)(2,1)S(1)} %get-tuple-element.64), channel_id=1, source_target_pairs={{0,16},{1,17},{2,18},{3,19},{4,20},{5,21},{6,22},{7,23},{8,24},{9,... | collective-permute-start | bytes 73736 | tf_op jit(solution)/shard_map/ppermute | solution.py:506
  21.4 4.7 %collective-permute-start.6 = (bf16[24,512]{1,0:T(8,128)(2,1)S(1)}, bf16[24,512]{1,0:T(8,128)(2,1)S(1)}, u32[]{:S(2)}, u32[]{:S(2)}) collective-permute-start(bf16[24,512]{1,0:T(8,128)(2,1)S(1)} %get-tuple-element.65), channel_id=1, source_target_pairs={{0,8},{1,9},{2,10},{3,11},{4,12},{5,13},{6,14},{7,15},{8,0},{9,1},... | collective-permute-start | bytes 73736 | tf_op jit(solution)/shard_map/ppermute | solution.py:506
  23.3 8.2 %copy-start.3 = (s32[384]{0:T(512)S(1)}, s32[384]{0:T(512)}, u32[]{:S(2)}) copy-start(s32[384]{0:T(512)} %table_hbm.2) | copy-start | bytes 4612
  27.3 11.7 %all-to-all-start = ((bf16[32,8,128]{2,1,0:T(8,128)(2,1)}), bf16[32,8,128]{2,1,0:T(8,128)(2,1)S(1)}, u32[]{:S(2)}, u32[]{:S(2)}) async-start(bf16[32,8,128]{2,1,0:T(8,128)(2,1)} %bitcast.4), calls=%async_computation | async-start | bytes 131072 | tf_op jit(solution)/shard_map/all_to_all | solution.py:582

commit v3 on v2

--- a/solution.py
+++ b/solution.py
@@ -86,13 +86,19 @@
     return jnp.concatenate([x, x], 1)
 
 
-def first_kernel(slots, blocks_here, w_hbm, off_hbm, cnt_hbm, ids_hbm, table_hbm, rows_hbm, inner_hbm, outer_hbm,
-                 out_ref, table_ref, rows_ref, inner_ref, outer_ref,
-                 w_ref, off_ref, cnt_ref, ids_ref, flat_ref, wide_ref, live_w_ref, live_off_ref, sems):
+def first_kernel(slots, blocks_here, staged, w_hbm, off_hbm, cnt_hbm, ids_hbm, table_hbm, rows_hbm, inner_hbm, outer_hbm, *refs):
+    if staged:
+        legendre_hbm, *refs = refs
+    out_ref, table_ref, rows_ref, inner_ref, outer_ref, *refs = refs
+    if staged:
+        legendre_ref, *refs = refs
+    w_ref, off_ref, cnt_ref, ids_ref, flat_ref, wide_ref, live_w_ref, live_off_ref, sems = refs
     pairs = (
         (cnt_hbm, cnt_ref), (ids_hbm, ids_ref), (off_hbm, off_ref), (w_hbm, w_ref),
         (table_hbm, flat_ref), (rows_hbm, rows_ref), (inner_hbm, inner_ref), (outer_hbm, outer_ref),
     )
+    if staged:
+        pairs = pairs + ((legendre_hbm.at[pl.ds(0, staged)], legendre_ref),)
     copies = [pltpu.make_async_copy(a, b, sems.at[i]) for i, (a, b) in enumerate(pairs)]
     for copy in copies[:4]:
         copy.start()
@@ -156,12 +162,14 @@
         return carry
 
     lax.fori_loop(0, live // pack, deposit, 0, unroll=9)
-    for copy in copies[4:]:
+    for copy in copies[4:8]:
         copy.wait()
     me = lax.axis_index("blk")
     for axis in ("y", "core"):
         me = me * lax.axis_size(axis) + lax.axis_index(axis)
     table_ref[...] = exclusive_or(flat_ref[...].reshape(table_ref.shape), me, slots)
+    for copy in copies[8:]:
+        copy.wait()
 
 
 def add_modes(bins, groups, cycles, groups_ref, inner_ref, outer_ref, add):
@@ -248,29 +256,44 @@
     return out.astype(jnp.bfloat16)
 
 
-def response_kernel(start, from_hbm, rest, legendre_ref, gain_ref, order_ref, out_ref, *refs):
+def respond(basis, gain_ref, order_ref, out_ref, slot):
+    cycles = basis.shape[1]
+    gain = jnp.concatenate([gain_ref[...]] * (cycles // BLOCK), 1)
+    gained = (basis.astype(jnp.float32) * gain).astype(jnp.bfloat16)
+    high, low = high_low(dot(basis, jnp.concatenate([basis, gained], 1), TN))
+    out_ref[slot, :cycles, :] = dot(high, order_ref[...]).astype(jnp.bfloat16)
+    out_ref[slot, cycles:, :] = dot(low, order_ref[...]).astype(jnp.bfloat16)
+
+
+def first_response_kernel(staged_ref, legendre_hbm, gain_ref, order_ref, out_ref, rest_ref, sems):
+    staged = staged_ref.shape[0]
+    count = out_ref.shape[0]
+    copies = []
+    for i, (first, last) in enumerate(((staged, count), (count, staged + rest_ref.shape[0]))):
+        target = rest_ref.at[pl.ds(first - staged, last - first)]
+        copies.append(pltpu.make_async_copy(legendre_hbm.at[pl.ds(first, last - first)], target, sems.at[i]))
+        copies[-1].start()
+    for slot in range(staged):
+        respond(staged_ref[slot], gain_ref, order_ref, out_ref, slot)
+    copies[0].wait()
+    for slot in range(staged, count):
+        respond(rest_ref[slot - staged], gain_ref, order_ref, out_ref, slot)
+    copies[1].wait()
+
+
+def response_kernel(start, from_hbm, legendre_ref, gain_ref, order_ref, out_ref, *scratch):
     count = out_ref.shape[0]
     copies = []
     if from_hbm:
-        source, (*rest_refs, legendre_ref, sems) = legendre_ref, refs
+        source, (legendre_ref, sems) = legendre_ref, scratch
         copies = [pltpu.make_async_copy(source.at[start + i], legendre_ref.at[i], sems.at[i]) for i in range(count)]
-        for ref in rest_refs:
-            copies.append(pltpu.make_async_copy(source.at[pl.ds(start + count, rest)], ref, sems.at[count]))
         for copy in copies:
             copy.start()
         start = 0
     for slot in range(count):
         if from_hbm:
             copies[slot].wait()
-        basis = legendre_ref[start + slot]
-        cycles = basis.shape[1]
-        gain = jnp.concatenate([gain_ref[...]] * (cycles // BLOCK), 1)
-        gained = (basis.astype(jnp.float32) * gain).astype(jnp.bfloat16)
-        high, low = high_low(dot(basis, jnp.concatenate([basis, gained], 1), TN))
-        out_ref[slot, :cycles, :] = dot(high, order_ref[...]).astype(jnp.bfloat16)
-        out_ref[slot, cycles:, :] = dot(low, order_ref[...]).astype(jnp.bfloat16)
-    for copy in copies[count:]:
-        copy.wait()
+        respond(legendre_ref[start + slot], gain_ref, order_ref, out_ref, slot)
 
 
 def slot_order(slots, bins):
@@ -481,8 +504,12 @@
         inner,
         outer,
     ]
+    ahead = slots // 2 if staged else 0
+    if staged:
+        shapes.append(shaped(ahead, degrees, cycles))
+        operands.append(legendre)
     deposits, *shared = pl.pallas_call(
-        functools.partial(first_kernel, slots, cycles_here * SEGMENTS),
+        functools.partial(first_kernel, slots, cycles_here * SEGMENTS, ahead),
         in_specs=[hbm] * len(operands),
         out_specs=(vmem,) * len(shapes),
         out_shape=tuple(shapes),
@@ -500,7 +527,8 @@
         compiler_params=limits,
         name="deposit",
     )(*[in_hbm(x) for x in operands])
-    basis, moved = legendre, 0
+    early = shared.pop() if staged else None
+    basis = legendre
 
     def swap(x, mask):
         return lax.ppermute(x, axes, [(i, i ^ mask) for i in range(devices)])
@@ -548,23 +576,32 @@
         arrived = [swap(x, (i + 1) << bits[0]) for i, x in reversed(list(enumerate(sends)))]
         first, last = (min(slots, slots * 2 * k * (2 * stages - k) // (2 * stages * stages)) for k in (stage, stage + 1))
         count = last - first
-        from_hbm = stage == 0 or not staged
-        rest = slots - last if stage == 0 and staged else 0
-        scratch = [pltpu.VMEM((count, degrees, cycles), jnp.bfloat16), pltpu.SemaphoreType.DMA((count + 1,))]
-        response, *rests = pl.pallas_call(
-            functools.partial(response_kernel, first if from_hbm else first - moved, from_hbm, rest),
-            in_specs=[hbm if from_hbm else vmem, vmem, vmem],
-            out_specs=(vmem,) * (2 if rest else 1),
-            out_shape=(shaped(count, 2 * cycles, 2 * cycles),) + ((shaped(rest, degrees, cycles),) if rest else ()),
-            scratch_shapes=scratch if from_hbm else [],
-            compiler_params=limits,
-            cost_estimate=pl.CostEstimate(
-                flops=6 * count * degrees * cycles * cycles, bytes_accessed=2 * count * degrees * cycles, transcendentals=0
-            ),
-            name="response",
-        )(basis, gain, order)
-        if rests:
-            basis, moved = rests[0], last
+        shape = shaped(count, 2 * cycles, 2 * cycles)
+        cost = pl.CostEstimate(
+            flops=6 * count * degrees * cycles * cycles, bytes_accessed=2 * count * degrees * cycles, transcendentals=0
+        )
+        if staged and stage == 0:
+            response, basis = pl.pallas_call(
+                first_response_kernel,
+                in_specs=[vmem, hbm, vmem, vmem],
+                out_specs=(vmem, vmem),
+                out_shape=(shape, shaped(slots - ahead, degrees, cycles)),
+                scratch_shapes=[pltpu.SemaphoreType.DMA((2,))],
+                compiler_params=limits,
+                cost_estimate=cost,
+                name="response",
+            )(early, basis, gain, order)
+        else:
+            response = pl.pallas_call(
+                functools.partial(response_kernel, first - ahead, not staged),
+                in_specs=[vmem if staged else hbm, vmem, vmem],
+                out_specs=vmem,
+                out_shape=shape,
+                scratch_shapes=[] if staged else [pltpu.VMEM((count, degrees, cycles), jnp.bfloat16), pltpu.SemaphoreType.DMA((count,))],
+                compiler_params=limits,
+                cost_estimate=cost,
+                name="response",
+            )(basis, gain, order)
         *arrived, response = lax.optimization_barrier((*arrived, response))
         responses.append(response)
         kernel, inputs, scratch = functools.partial(merge_kernel, len(arrived)), (kept, *arrived), []

time: 41.9 us -> 40.6 us (0.969)
  Pallas kernels: 16.9 us -> 15.6 us
    pallas_call x2, Pallas kernels: 7.37 us -> 6.06 us  [the longest x1 4.78 us: per_device(): pl.pallas_call(first_response_kernel, in_specs=[vmem, hbm, vmem, vmem], o...]
  transfers between devices with their start and end apart: 8 -> 8, of which waited for: 2 -> 3; matrix products, arithmetic and copies ran while one was open for 2% -> 2% of each run, Pallas kernels for 21% -> 18%
where the time goes in v3:
time: 40.6 us; the launch traced here: 40.4 us
  Pallas kernels  15.6 us (38%)
  starting transfers between devices  13.5 us (33%)
  waiting for transfers between devices  9.77 us (24%)
  local copies, waits for them, and re-layouts  0.74 us (2%)
  between operations  0.74 us (2%)
    ppermute x7, starting transfers between devices, swap(): return lax.ppermute(x, axes, [(i, i ^ mask) for i in range(devices)])  9.23 us
    all_to_all x1, waiting for transfers between devices, per_device(): lax.all_to_all(outgoing, axes, split_axis=0, concat_axis=0, tiled=True)  6.69 us
    pallas_call x1, Pallas kernels, per_device(): pl.pallas_call(first_response_kernel, in_specs=[vmem, hbm, vmem, vmem], o...  4.78 us
    all_to_all x1, starting transfers between devices, per_device(): lax.all_to_all(outgoing, axes, split_axis=0, concat_axis=0, tiled=True)  4.27 us
    pallas_call x1, Pallas kernels, per_device(): pl.pallas_call(functools.partial(first_kernel, slots, cycles_here * SEGME...  3.55 us
    ppermute x7, waiting for transfers between devices, swap(): return lax.ppermute(x, axes, [(i, i ^ mask) for i in range(devices)])  3.08 us
    pallas_call x1, Pallas kernels, per_device(): pl.pallas_call(inverse_kernel, in_specs=[vmem] + [hbm] * 3, out_specs=(hb...  2.68 us
    pallas_call x1, Pallas kernels, per_device(): pl.pallas_call(functools.partial(response_kernel, first - ahead, not stag...  1.28 us
  transfers between devices with their start and end apart: 8, of which 3 were waited for; matrix products, arithmetic and copies ran while one was open for 2% of the time, Pallas kernels for 18%

profile of v3, /device:TPU:0, one launch (start us, length us, event | category | flops | bytes accessed | tf_op | source)
XLA Modules:
  0.0 40.4 jit_solution(5006852178869272498)
XLA Ops:
  0.6 3.5 %deposit.1 = (bf16[608,128]{1,0:T(8,128)(2,1)S(1)}, s32[1,384]{1,0:T(1,128)S(1)}, bf16[192,384]{1,0:T(8,128)(2,1)S(1)}, bf16[384,512]{1,0:T(8,128)(2,1)S(1)}, bf...) custom-call(bf16[1024,128]{1,0:T(8,128)(2,1)} %bitcast.8, s32[256,128]{1,0:T(8,128)} %bitcast.9, ...), custom_call_target="tpu_custom_call" | custom-call | tf_op jit(solution)/shard_map/deposit/pallas_call | solution.py:511
  4.2 0.0 copy-start
  4.2 0.0 copy-start.1
  4.2 0.5 %collective-permute-start = (bf16[608,128]{1,0:T(8,128)(2,1)S(1)}, bf16[608,128]{1,0:T(8,128)(2,1)S(1)}, u32[]{:S(2)}, u32[]{:S(2)}) collective-permute-start(bf16[608,128]{1,0:T(8,128)(2,1)S(1)} %get-tuple-element.39.groups_ref), channel_id=1, source_target_pairs={{0,1},{1,0},{2,3},{3,2},{4,5},{5,4},{6,7},{7,6},{8,9},{9,8},{10,11... | collective-permute-start | bytes 466952 | tf_op jit(solution)/shard_map/ppermute | solution.py:534
  4.7 1.3 %own_groups.1 = (f32[4,384,128]{2,1,0:T(8,128)S(1)}, bf16[384,256]{1,0:T(8,128)(2,1)S(1)}, bf16[384,128]{1,0:T(8,128)(2,1)S(1)}) custom-call(bf16[608,128]{1,0:T(8,128)(2,1)S(1)} %get-tuple-element.39.groups_ref, s32[1,384]{1,0:T(1,128)S(1)} %get-tuple-element.40.table_ref, bf16[192,384]{1,0:T(8,128)(2,1)S(1)} %get-tuple-element.41.rows_ref, ...), custom_call_target="tpu_custom_call" | custom-call | flops 452984832 | bytes 786432 | tf_op jit(solution)/shard_map/own_groups/pallas_call | solution.py:539
  6.0 0.0 collective-permute-done.groups_ref
  6.0 0.9 %other_groups.1 = (f32[96,512]{1,0:T(8,128)S(1)}, bf16[96,512]{1,0:T(8,128)(2,1)S(1)}, bf16[96,512]{1,0:T(8,128)(2,1)S(1)}, bf16[96,512]{1,0:T(8,128)(2,1)S(1)}) custom-call(bf16[608,128]{1,0:T(8,128)(2,1)S(1)} %collective-permute-done.groups_ref, bf16[384,256]{1,0:T(8,128)(2,1)S(1)} %get-tuple-element.44.inner_ref, ...), custom_call_target="tpu_custom_call" | custom-call | tf_op jit(solution)/shard_map/other_groups/pallas_call | solution.py:564
  6.9 3.6 %collective-permute-start.1 = (bf16[96,512]{1,0:T(8,128)(2,1)S(1)}, bf16[96,512]{1,0:T(8,128)(2,1)S(1)}, u32[]{:S(2)}, u32[]{:S(2)}) collective-permute-start(bf16[96,512]{1,0:T(8,128)(2,1)S(1)} %get-tuple-element.51), channel_id=1, source_target_pairs={{0,6},{1,7},{2,4},{3,5},{4,2},{5,3},{6,0},{7,1},{8,14},{9,15},{10,... | collective-permute-start | bytes 294920 | tf_op jit(solution)/shard_map/ppermute | solution.py:534
  10.5 0.5 %collective-permute-start.2 = (bf16[96,512]{1,0:T(8,128)(2,1)S(1)}, bf16[96,512]{1,0:T(8,128)(2,1)S(1)}, u32[]{:S(2)}, u32[]{:S(2)}) collective-permute-start(bf16[96,512]{1,0:T(8,128)(2,1)S(1)} %get-tuple-element.52), channel_id=1, source_target_pairs={{0,4},{1,5},{2,6},{3,7},{4,0},{5,1},{6,2},{7,3},{8,12},{9,13},{10,... | collective-permute-start | bytes 294920 | tf_op jit(solution)/shard_map/ppermute | solution.py:534
  11.0 0.1 collective-permute-start.3
  11.1 0.0 copy-done
  11.1 0.0 copy-done.1
  11.1 4.8 %response.2 = (bf16[9,256,256]{2,1,0:T(8,128)(2,1)S(1)}, bf16[6,1664,128]{2,1,0:T(8,128)(2,1)S(1)}) custom-call(bf16[6,1664,128]{2,1,0:T(8,128)(2,1)S(1)} %get-tuple-element.54.staged_ref, bf16[12,1664,128]{2,1,0:T(8,128)(2,1)} %legendre_hbm, f32[1664,128]{1,0:T(8,128)S(1)} %copy-done, bf16[256,256]{1,0:T(8,128)(2,1)S(1)} %copy-done.1), custom_call_target="tpu_custom_call" | custom-call | flops 1472200704 | bytes 3833856 | tf_op jit(solution)/shard_map/response/pallas_call | solution.py:584
  15.9 0.0 copy-start.2
  15.9 0.0 collective-permute-done.1.refs_0_
  16.0 0.3 collective-permute-done.2.refs_1_
  16.2 0.0 collective-permute-done.3.refs_2_
  16.2 0.1 merge.1
  16.3 0.0 copy-start.3
  16.3 3.8 %collective-permute-start.4 = (bf16[24,512]{1,0:T(8,128)(2,1)S(1)}, bf16[24,512]{1,0:T(8,128)(2,1)S(1)}, u32[]{:S(2)}, u32[]{:S(2)}) collective-permute-start(bf16[24,512]{1,0:T(8,128)(2,1)S(1)} %get-tuple-element.65), channel_id=1, source_target_pairs={{0,24},{1,25},{2,26},{3,27},{4,28},{5,29},{6,30},{7,31},{8,16},{9,... | collective-permute-start | bytes 73736 | tf_op jit(solution)/shard_map/ppermute | solution.py:534
  20.1 0.0 collective-permute-start.5
  20.1 0.6 %collective-permute-start.6 = (bf16[24,512]{1,0:T(8,128)(2,1)S(1)}, bf16[24,512]{1,0:T(8,128)(2,1)S(1)}, u32[]{:S(2)}, u32[]{:S(2)}) collective-permute-start(bf16[24,512]{1,0:T(8,128)(2,1)S(1)} %get-tuple-element.67), channel_id=1, source_target_pairs={{0,8},{1,9},{2,10},{3,11},{4,12},{5,13},{6,14},{7,15},{8,0},{9,1},... | collective-permute-start | bytes 73736 | tf_op jit(solution)/shard_map/ppermute | solution.py:534
  20.8 1.3 %response.3.refs_4_ = bf16[3,256,256]{2,1,0:T(8,128)(2,1)S(1)} custom-call(bf16[6,1664,128]{2,1,0:T(8,128)(2,1)S(1)} %get-tuple-element.68.legendre_ref, f32[1664,128]{1,0:T(8,128)S(1)} %copy-done, bf16[256,256]{1,0:T(8,128)(2,1)S(1)} %copy-done.1), custom_call_target="tpu_custom_call" | custom-call | flops 490733568 | bytes 1277952 | tf_op jit(solution)/shard_map/response/pallas_call | solution.py:595
  22.0 0.0 collective-permute-done.4.refs_0_
  22.1 2.7 %collective-permute-done.5.refs_1_ = bf16[24,512]{1,0:T(8,128)(2,1)S(1)} collective-permute-done((bf16[24,512]{1,0:T(8,128)(2,1)S(1)}, bf16[24,512]{1,0:T(8,128)(2,1)S(1)}, u32[]{:S(2)}, u32[]{:S(2)}) %collective-permute-start.5) | collective-permute-done | bytes 24608 | tf_op jit(solution)/shard_map/ppermute | solution.py:534
  24.8 0.0 collective-permute-done.6.refs_2_
  24.8 0.0 copy-done.2
  24.8 1.1 %synthesis.1 = bf16[256,128]{1,0:T(8,128)(2,1)} custom-call(f32[24,512]{1,0:T(8,128)S(1)} %get-tuple-element.60.kept_ref, bf16[24,512]{1,0:T(8,128)(2,1)S(1)} %collective-permute-done.4.refs_0_, bf16[24,512]{1,0:T(8,128)(2,1)S(1)} %collective-permute-done.5.refs_1_, bf16[24,512]{1,0:T(8,128)(2,1)S(1)} %collective-permute-done.6.refs_2_, ...), custom_call_target="tpu_custom_call" | custom-call | tf_op jit(solution)/shard_map/synthesis/pallas_call | solution.py:609
  26.0 4.3 %all-to-all-start = ((bf16[32,8,128]{2,1,0:T(8,128)(2,1)}), bf16[32,8,128]{2,1,0:T(8,128)(2,1)S(1)}, u32[]{:S(2)}, u32[]{:S(2)}) async-start(bf16[32,8,128]{2,1,0:T(8,128)(2,1)} %bitcast.4), calls=%async_computation | async-start | bytes 131072 | tf_op jit(solution)/shard_map/all_to_all | solution.py:619
  30.3 0.0 copy-done.3
  30.3 0.7 %reshape.23.slots_hbm = s32[32,12]{1,0:T(8,128)} reshape(s32[384]{0:T(512)S(1)} %copy-done.3) | data formatting | bytes 3072 | tf_op jit(solution)/shard_map/reshape | solution.py:644
  31.0 6.7 %all-to-all-done = bf16[32,8,128]{2,1,0:T(8,128)(2,1)S(1)} async-done(((bf16[32,8,128]{2,1,0:T(8,128)(2,1)}), bf16[32,8,128]{2,1,0:T(8,128)(2,1)S(1)}, u32[]{:S(2)}, u32[]{:S(2)}) %all-to-all-start) | async-done | bytes 65568 | tf_op jit(solution)/shard_map/all_to_all | solution.py:619
  37.7 2.7 %inverse.1 = (f32[4,4,4096]{2,1,0:T(4,128)}, f32[4,4,4096]{2,1,0:T(4,128)}) custom-call(bf16[256,128]{1,0:T(8,128)(2,1)S(1)} %bitcast.7, s32[32,12]{1,0:T(8,128)} %reshape.23.slots_hbm, bf16[16,512]{1,0:T(8,128)(2,1)} %constant.22.clone.turn_hbm, bf16[1536,512]{1,0:T(8,128)(2,1)} %constant.23.clone.table_hbm), custom_call_target="tpu_custom_call" | custom-call | tf_op jit(solution)/shard_map/inverse/pallas_call | solution.py:628
Async XLA Ops:
  4.2 7.0 %copy-start = (f32[1664,128]{1,0:T(8,128)S(1)}, f32[1664,128]{1,0:T(8,128)}, u32[]{:S(2)}) copy-start(f32[1664,128]{1,0:T(8,128)} %constant.19.clone.gain_ref) | copy-start | bytes 2555908
  4.2 6.9 %copy-start.1 = (bf16[256,256]{1,0:T(8,128)(2,1)S(1)}, bf16[256,256]{1,0:T(8,128)(2,1)}, u32[]{:S(2)}) copy-start(bf16[256,256]{1,0:T(8,128)(2,1)} %constant.20.clone.order_ref) | copy-start | bytes 393220
  4.2 1.8 %collective-permute-start = (bf16[608,128]{1,0:T(8,128)(2,1)S(1)}, bf16[608,128]{1,0:T(8,128)(2,1)S(1)}, u32[]{:S(2)}, u32[]{:S(2)}) collective-permute-start(bf16[608,128]{1,0:T(8,128)(2,1)S(1)} %get-tuple-element.39.groups_ref), channel_id=1, source_target_pairs={{0,1},{1,0},{2,3},{3,2},{4,5},{5,4},{6,7},{7,6},{8,9},{9,8},{10,11... | collective-permute-start | bytes 466952 | tf_op jit(solution)/shard_map/ppermute | solution.py:534
  6.9 9.1 %collective-permute-start.1 = (bf16[96,512]{1,0:T(8,128)(2,1)S(1)}, bf16[96,512]{1,0:T(8,128)(2,1)S(1)}, u32[]{:S(2)}, u32[]{:S(2)}) collective-permute-start(bf16[96,512]{1,0:T(8,128)(2,1)S(1)} %get-tuple-element.51), channel_id=1, source_target_pairs={{0,6},{1,7},{2,4},{3,5},{4,2},{5,3},{6,0},{7,1},{8,14},{9,15},{10,... | collective-permute-start | bytes 294920 | tf_op jit(solution)/shard_map/ppermute | solution.py:534
  10.5 5.7 %collective-permute-start.2 = (bf16[96,512]{1,0:T(8,128)(2,1)S(1)}, bf16[96,512]{1,0:T(8,128)(2,1)S(1)}, u32[]{:S(2)}, u32[]{:S(2)}) collective-permute-start(bf16[96,512]{1,0:T(8,128)(2,1)S(1)} %get-tuple-element.52), channel_id=1, source_target_pairs={{0,4},{1,5},{2,6},{3,7},{4,0},{5,1},{6,2},{7,3},{8,12},{9,13},{10,... | collective-permute-start | bytes 294920 | tf_op jit(solution)/shard_map/ppermute | solution.py:534
  11.0 5.2 %collective-permute-start.3 = (bf16[96,512]{1,0:T(8,128)(2,1)S(1)}, bf16[96,512]{1,0:T(8,128)(2,1)S(1)}, u32[]{:S(2)}, u32[]{:S(2)}) collective-permute-start(bf16[96,512]{1,0:T(8,128)(2,1)S(1)} %get-tuple-element.53), channel_id=1, source_target_pairs={{0,2},{1,3},{2,0},{3,1},{4,6},{5,7},{6,4},{7,5},{8,10},{9,11},{10,... | collective-permute-start | bytes 294920 | tf_op jit(solution)/shard_map/ppermute | solution.py:534
  15.9 8.9 %copy-start.2 = (bf16[96,96]{1,0:T(8,128)(2,1)S(1)}, bf16[96,96]{1,0:T(8,128)(2,1)}, u32[]{:S(2)}) copy-start(bf16[96,96]{1,0:T(8,128)(2,1)} %constant.21.clone.refs_5_) | copy-start | bytes 55300
  16.3 14.0 %copy-start.3 = (s32[384]{0:T(512)S(1)}, s32[384]{0:T(512)}, u32[]{:S(2)}) copy-start(s32[384]{0:T(512)} %table_hbm.2) | copy-start | bytes 4612
  16.3 5.8 %collective-permute-start.4 = (bf16[24,512]{1,0:T(8,128)(2,1)S(1)}, bf16[24,512]{1,0:T(8,128)(2,1)S(1)}, u32[]{:S(2)}, u32[]{:S(2)}) collective-permute-start(bf16[24,512]{1,0:T(8,128)(2,1)S(1)} %get-tuple-element.65), channel_id=1, source_target_pairs={{0,24},{1,25},{2,26},{3,27},{4,28},{5,29},{6,30},{7,31},{8,16},{9,... | collective-permute-start | bytes 73736 | tf_op jit(solution)/shard_map/ppermute | solution.py:534
  20.1 4.7 %collective-permute-start.5 = (bf16[24,512]{1,0:T(8,128)(2,1)S(1)}, bf16[24,512]{1,0:T(8,128)(2,1)S(1)}, u32[]{:S(2)}, u32[]{:S(2)}) collective-permute-start(bf16[24,512]{1,0:T(8,128)(2,1)S(1)} %get-tuple-element.66), channel_id=1, source_target_pairs={{0,16},{1,17},{2,18},{3,19},{4,20},{5,21},{6,22},{7,23},{8,24},{9,... | collective-permute-start | bytes 73736 | tf_op jit(solution)/shard_map/ppermute | solution.py:534
  20.1 4.7 %collective-permute-start.6 = (bf16[24,512]{1,0:T(8,128)(2,1)S(1)}, bf16[24,512]{1,0:T(8,128)(2,1)S(1)}, u32[]{:S(2)}, u32[]{:S(2)}) collective-permute-start(bf16[24,512]{1,0:T(8,128)(2,1)S(1)} %get-tuple-element.67), channel_id=1, source_target_pairs={{0,8},{1,9},{2,10},{3,11},{4,12},{5,13},{6,14},{7,15},{8,0},{9,1},... | collective-permute-start | bytes 73736 | tf_op jit(solution)/shard_map/ppermute | solution.py:534
  26.0 11.7 %all-to-all-start = ((bf16[32,8,128]{2,1,0:T(8,128)(2,1)}), bf16[32,8,128]{2,1,0:T(8,128)(2,1)S(1)}, u32[]{:S(2)}, u32[]{:S(2)}) async-start(bf16[32,8,128]{2,1,0:T(8,128)(2,1)} %bitcast.4), calls=%async_computation | async-start | bytes 131072 | tf_op jit(solution)/shard_map/all_to_all | solution.py:619

commit v4 on v3

--- a/solution.py
+++ b/solution.py
@@ -198,7 +198,13 @@
                     add(b * (cycles // LANES) + tile, start + part, value[:, tile * LANES : (tile + 1) * LANES])
 
 
-def own_kernel(bins, groups, cycles, groups_ref, table_ref, rows_ref, inner_ref, outer_ref, out_ref, inner_out, outer_out):
+def own_kernel(bins, groups, cycles, staged, groups_ref, table_ref, rows_ref, inner_ref, outer_ref, *refs):
+    if staged:
+        legendre_hbm, out_ref, inner_out, outer_out, legendre_ref, sem = refs
+        late = pltpu.make_async_copy(legendre_hbm.at[pl.ds(staged, legendre_ref.shape[0])], legendre_ref, sem)
+        late.start()
+    else:
+        out_ref, inner_out, outer_out = refs
     count, orders = rows_ref.shape
     held = hot(lax.broadcasted_iota(jnp.int32, (orders, orders), 0) == table_ref[...])
     for start in range(0, count, CHUNK):
@@ -214,6 +220,8 @@
         out_ref.at[tile][pl.ds(first, value.shape[0], stride=2), :] = value
 
     add_modes(bins, groups, cycles, groups_ref, inner_out, outer_out, add)
+    if staged:
+        late.wait()
 
 
 def split_sum(parts, tile, keep_ref, send_refs):
@@ -224,6 +232,10 @@
         out_ref[:, lanes] = value.astype(out_ref.dtype)
 
 
+def send_order(ways):
+    return [(1, 2), (2, 1), (3, 3)] if ways == 4 else [(i, i) for i in range(1, ways)]
+
+
 def other_kernel(bins, groups, cycles, groups_ref, inner_ref, outer_ref, own_ref, keep_ref, *refs):
     *send_refs, other_ref = refs
 
@@ -231,9 +243,14 @@
         other_ref.at[tile][pl.ds(first, value.shape[0], stride=2), :] = value
 
     add_modes(bins, groups, cycles, groups_ref, inner_ref, outer_ref, add)
-    for tile in range(own_ref.shape[0]):
-        parts = (lambda rows, lanes: own_ref[tile, rows, :], lambda rows, lanes: other_ref[tile, rows, :])
-        split_sum(parts, tile, keep_ref, send_refs)
+    rows = keep_ref.shape[0]
+    core = lax.axis_index("core")
+    blocks = [(0, 0)] + send_order(len(send_refs) + 1)
+    for (even, odd), out_ref in zip(blocks, (keep_ref, *send_refs)):
+        first = even * rows if even == odd else pl.multiple_of((even + core * (odd - even)) * rows, rows)
+        for tile in range(own_ref.shape[0]):
+            value = own_ref[tile, pl.ds(first, rows), :] + other_ref[tile, pl.ds(first, rows), :]
+            out_ref[:, tile * LANES : (tile + 1) * LANES] = value.astype(out_ref.dtype)
 
 
 def merge_kernel(count, kept_ref, *refs):
@@ -265,35 +282,21 @@
     out_ref[slot, cycles:, :] = dot(low, order_ref[...]).astype(jnp.bfloat16)
 
 
-def first_response_kernel(staged_ref, legendre_hbm, gain_ref, order_ref, out_ref, rest_ref, sems):
-    staged = staged_ref.shape[0]
+def staged_response_kernel(start, early_ref, late_ref, gain_ref, order_ref, out_ref):
+    early = early_ref.shape[0]
+    for slot in range(out_ref.shape[0]):
+        at = start + slot
+        respond(early_ref[at] if at < early else late_ref[at - early], gain_ref, order_ref, out_ref, slot)
+
+
+def response_kernel(start, legendre_hbm, gain_ref, order_ref, out_ref, legendre_ref, sems):
     count = out_ref.shape[0]
-    copies = []
-    for i, (first, last) in enumerate(((staged, count), (count, staged + rest_ref.shape[0]))):
-        target = rest_ref.at[pl.ds(first - staged, last - first)]
-        copies.append(pltpu.make_async_copy(legendre_hbm.at[pl.ds(first, last - first)], target, sems.at[i]))
-        copies[-1].start()
-    for slot in range(staged):
-        respond(staged_ref[slot], gain_ref, order_ref, out_ref, slot)
-    copies[0].wait()
-    for slot in range(staged, count):
-        respond(rest_ref[slot - staged], gain_ref, order_ref, out_ref, slot)
-    copies[1].wait()
-
-
-def response_kernel(start, from_hbm, legendre_ref, gain_ref, order_ref, out_ref, *scratch):
-    count = out_ref.shape[0]
-    copies = []
-    if from_hbm:
-        source, (legendre_ref, sems) = legendre_ref, scratch
-        copies = [pltpu.make_async_copy(source.at[start + i], legendre_ref.at[i], sems.at[i]) for i in range(count)]
-        for copy in copies:
-            copy.start()
-        start = 0
+    copies = [pltpu.make_async_copy(legendre_hbm.at[start + i], legendre_ref.at[i], sems.at[i]) for i in range(count)]
+    for copy in copies:
+        copy.start()
     for slot in range(count):
-        if from_hbm:
-            copies[slot].wait()
-        respond(legendre_ref[start + slot], gain_ref, order_ref, out_ref, slot)
+        copies[slot].wait()
+        respond(legendre_ref[slot], gain_ref, order_ref, out_ref, slot)
 
 
 def slot_order(slots, bins):
@@ -375,19 +378,16 @@
     return hot(column == ((filter_number * cycles_here + cycle) * 2 + part) * bins + bin_number)
 
 
-def inverse_kernel(arrived_ref, slots_hbm, turn_hbm, table_hbm, kappa_hbm, potential_hbm,
-                   slots_ref, turn_ref, table_ref, wide_ref, kappa_ref, potential_ref, sems, out_sems):
-    copies = [
-        pltpu.make_async_copy(a, b, sems.at[i])
-        for i, (a, b) in enumerate(((slots_hbm, slots_ref), (turn_hbm, turn_ref)))
-    ]
+def inverse_kernel(arrived_ref, slots_ref, turn_hbm, table_hbm, kappa_hbm, potential_hbm,
+                   turn_ref, table_ref, wide_ref, kappa_ref, potential_ref, sems, out_sems):
+    copies = [pltpu.make_async_copy(turn_hbm, turn_ref, sems.at[0])]
     quarter = NPHI // 4
     chunk = table_ref.shape[1]
     chunks = quarter // chunk
     part = table_ref.shape[0] // chunks
     for i in range(chunks):
         rows = pl.ds(i * part, part)
-        copies.append(pltpu.make_async_copy(table_hbm.at[rows], table_ref.at[rows], sems.at[2 + i]))
+        copies.append(pltpu.make_async_copy(table_hbm.at[rows], table_ref.at[rows], sems.at[1 + i]))
     for copy in copies:
         copy.start()
     devices, slots = slots_ref.shape
@@ -405,8 +405,6 @@
     orders = jnp.where((within >= 0) & (within < few), 4 * within + 2, orders)
     within = lane - starts[2]
     orders = jnp.where((within >= 0) & (within < many), 2 * within + 1, orders)
-    for copy in copies[:2]:
-        copy.wait()
     lefts, picks = [], []
     for t in range(slots):
         lefts.append(jnp.concatenate([x[t * per_slot : (t + 1) * per_slot, :] for x in turned], 0))
@@ -415,6 +413,7 @@
     spectrum = spectrum.astype(jnp.bfloat16)
     real_in = dot(part_rows(0, bins, cycles_here), spectrum)
     imag_in = dot(part_rows(1, bins, cycles_here), spectrum)
+    copies[0].wait()
     turn = turn_ref[...].astype(jnp.float32)
     odd = lax.rem(lax.rem(lax.broadcasted_iota(jnp.int32, real_in.shape, 0), cycles_here), 2) == 1
     turn_cos = jnp.where(odd, turn[0:1, :] + turn[1:2, :], turn[4:5, :])
@@ -434,7 +433,7 @@
             lefts.append(jnp.concatenate([y for x in rows for y in high_low(x)], 0))
     results = []
     for index in range(chunks):
-        copies[2 + index].wait()
+        copies[1 + index].wait()
         row = index * part
         sums = []
         for at in range(3):
@@ -504,7 +503,7 @@
         inner,
         outer,
     ]
-    ahead = slots // 2 if staged else 0
+    ahead = slots * 5 // 6 if staged else 0
     if staged:
         shapes.append(shaped(ahead, degrees, cycles))
         operands.append(legendre)
@@ -528,27 +527,30 @@
         name="deposit",
     )(*[in_hbm(x) for x in operands])
     early = shared.pop() if staged else None
-    basis = legendre
-
-    def swap(x, mask):
-        return lax.ppermute(x, axes, [(i, i ^ mask) for i in range(devices)])
+
+    def swap(x, mask, odd_mask=None):
+        masks = (mask, mask if odd_mask is None else odd_mask)
+        return lax.ppermute(x, axes, [(i, i ^ masks[i % 2]) for i in range(devices)])
 
     other = swap(deposits, 1)
     cost = pl.CostEstimate(flops=8 * orders * 256 * bins * live, bytes_accessed=4 * orders * width, transcendentals=0)
     modes_shape = (width // LANES, orders, LANES)
-    own, own_inner, own_outer = pl.pallas_call(
-        functools.partial(own_kernel, bins, live, cycles),
-        in_specs=[vmem] * 5,
-        out_specs=(vmem,) * 3,
+    own, own_inner, own_outer, *late = pl.pallas_call(
+        functools.partial(own_kernel, bins, live, cycles, ahead),
+        in_specs=[vmem] * 5 + [hbm] * staged,
+        out_specs=(vmem,) * (3 + staged),
         out_shape=(
             shaped(*modes_shape, dtype=jnp.float32),
             shaped(orders, inner.shape[1] // 2),
             shaped(orders, outer.shape[1] // 2),
-        ),
+        ) + (shaped(slots - ahead, degrees, cycles),) * staged,
+        scratch_shapes=[pltpu.SemaphoreType.DMA] * staged,
         compiler_params=limits,
         cost_estimate=cost,
         name="own_groups",
-    )(deposits, *shared)
+    )(deposits, *shared, *[in_hbm(legendre)] * staged)
+
+    basis = [early, *late] if staged else [legendre]
 
     groups_of_bits = bit_groups(devices)
     stages = len(groups_of_bits)
@@ -570,38 +572,33 @@
             compiler_params=limits,
             name="merge" if stage else "other_groups",
         )(*inputs)
-        *sends, basis = lax.optimization_barrier((*sends, basis))
-        if stage == 0 or not staged:
-            basis = in_hbm(basis)
-        arrived = [swap(x, (i + 1) << bits[0]) for i, x in reversed(list(enumerate(sends)))]
+        sends, basis = lax.optimization_barrier((sends, basis))
+        if stage == 0:
+            order_of = send_order(ways)
+            arrived = [swap(x, even << bits[0], odd << bits[0]) for x, (even, odd) in zip(sends, order_of)]
+        else:
+            arrived = [swap(x, (i + 1) << bits[0]) for i, x in reversed(list(enumerate(sends)))]
         first, last = (min(slots, slots * 2 * k * (2 * stages - k) // (2 * stages * stages)) for k in (stage, stage + 1))
         count = last - first
         shape = shaped(count, 2 * cycles, 2 * cycles)
         cost = pl.CostEstimate(
             flops=6 * count * degrees * cycles * cycles, bytes_accessed=2 * count * degrees * cycles, transcendentals=0
         )
-        if staged and stage == 0:
-            response, basis = pl.pallas_call(
-                first_response_kernel,
-                in_specs=[vmem, hbm, vmem, vmem],
-                out_specs=(vmem, vmem),
-                out_shape=(shape, shaped(slots - ahead, degrees, cycles)),
-                scratch_shapes=[pltpu.SemaphoreType.DMA((2,))],
-                compiler_params=limits,
-                cost_estimate=cost,
-                name="response",
-            )(early, basis, gain, order)
+        if staged:
+            kernel, scratch = functools.partial(staged_response_kernel, first), []
         else:
-            response = pl.pallas_call(
-                functools.partial(response_kernel, first - ahead, not staged),
-                in_specs=[vmem if staged else hbm, vmem, vmem],
-                out_specs=vmem,
-                out_shape=shape,
-                scratch_shapes=[] if staged else [pltpu.VMEM((count, degrees, cycles), jnp.bfloat16), pltpu.SemaphoreType.DMA((count,))],
-                compiler_params=limits,
-                cost_estimate=cost,
-                name="response",
-            )(basis, gain, order)
+            kernel = functools.partial(response_kernel, first)
+            scratch = [pltpu.VMEM((count, degrees, cycles), jnp.bfloat16), pltpu.SemaphoreType.DMA((count,))]
+        response = pl.pallas_call(
+            kernel,
+            in_specs=[vmem if staged else hbm] * len(basis) + [vmem] * 2,
+            out_specs=vmem,
+            out_shape=shape,
+            scratch_shapes=scratch,
+            compiler_params=limits,
+            cost_estimate=cost,
+            name="response",
+        )(*basis if staged else [in_hbm(x) for x in basis], gain, order)
         *arrived, response = lax.optimization_barrier((*arrived, response))
         responses.append(response)
         kernel, inputs, scratch = functools.partial(merge_kernel, len(arrived)), (kept, *arrived), []
@@ -627,21 +624,20 @@
     map_shape = shaped(bins, cycles_here, NPHI, dtype=jnp.float32)
     return pl.pallas_call(
         inverse_kernel,
-        in_specs=[vmem] + [hbm] * 3,
+        in_specs=[vmem] * 2 + [hbm] * 2,
         out_specs=(hbm, hbm),
         out_shape=(map_shape, map_shape),
         scratch_shapes=[
-            pltpu.VMEM((devices, slots), jnp.int32),
             *[pltpu.VMEM(x.shape, x.dtype) for x in constants],
             pltpu.VMEM((2 * cycles, 128), jnp.float32),
             pltpu.VMEM(map_shape.shape, jnp.float32),
             pltpu.VMEM(map_shape.shape, jnp.float32),
-            pltpu.SemaphoreType.DMA((2 + chunks,)),
+            pltpu.SemaphoreType.DMA((1 + chunks,)),
             pltpu.SemaphoreType.DMA((8 * chunks,)),
         ],
         compiler_params=limits,
         name="inverse",
-    )(arrived, in_hbm(held.reshape(devices, slots)), *[in_hbm(x) for x in constants])
+    )(arrived, held.reshape(devices, slots), *[in_hbm(x) for x in constants])
 
 
 def solution(mesh):

time: 40.6 us -> 39.9 us (0.983)
  waiting for transfers between devices: 9.77 us -> 11.8 us
  Pallas kernels: 15.6 us -> 14.5 us
  starting transfers between devices: 13.5 us -> 12.5 us
  local copies, waits for them, and re-layouts: 0.74 us -> 0.12 us
    ppermute x7, waiting for transfers between devices: 3.08 us -> 4.46 us  [swap(): lax.ppermute(x, axes, [(i, i ^ masks[i % 2]) for i in range(devices)])]
    pallas_call x4, Pallas kernels: 9.99 us -> 8.8 us  [the longest x2 4.9 us: per_device(): pl.pallas_call(kernel, in_specs=[vmem if staged else hbm] * len(basis) +...]
    all_to_all x1, starting transfers between devices: 4.27 us -> 3.3 us  [per_device(): lax.all_to_all(outgoing, axes, split_axis=0, concat_axis=0, tiled=True)]
    reshape x1, local copies, waits for them, and re-layouts: 0.71 us -> 0.1 us  [per_device(): held.reshape(devices, slots)]
    all_to_all x1, waiting for transfers between devices: 6.69 us -> 7.3 us  [per_device(): lax.all_to_all(outgoing, axes, split_axis=0, concat_axis=0, tiled=True)]
  transfers between devices with their start and end apart: 8 -> 8, of which waited for: 3 -> 4; matrix products, arithmetic and copies ran while one was open for 2% -> 0% of each run, Pallas kernels for 18% -> 16%
where the time goes in v4:
time: 39.9 us; the launch traced here: 39.6 us
  Pallas kernels  14.5 us (36%)
  starting transfers between devices  12.5 us (31%)
  waiting for transfers between devices  11.8 us (30%)
  between operations  0.76 us (2%)
    ppermute x7, starting transfers between devices, swap(): lax.ppermute(x, axes, [(i, i ^ masks[i % 2]) for i in range(devices)])  9.17 us
    all_to_all x1, waiting for transfers between devices, per_device(): lax.all_to_all(outgoing, axes, split_axis=0, concat_axis=0, tiled=True)  7.3 us
    pallas_call x2, Pallas kernels, per_device(): pl.pallas_call(kernel, in_specs=[vmem if staged else hbm] * len(basis) +...  4.9 us
    ppermute x7, waiting for transfers between devices, swap(): lax.ppermute(x, axes, [(i, i ^ masks[i % 2]) for i in range(devices)])  4.46 us
    pallas_call x1, Pallas kernels, per_device(): pl.pallas_call(functools.partial(first_kernel, slots, cycles_here * SEGME...  3.62 us
    all_to_all x1, starting transfers between devices, per_device(): lax.all_to_all(outgoing, axes, split_axis=0, concat_axis=0, tiled=True)  3.3 us
    pallas_call x1, Pallas kernels, per_device(): pl.pallas_call(inverse_kernel, in_specs=[vmem] * 2 + [hbm] * 2, out_specs...  2.61 us
    pallas_call x1, Pallas kernels, per_device(): pl.pallas_call(functools.partial(own_kernel, bins, live, cycles, ahead),...  1.29 us
  transfers between devices with their start and end apart: 8, of which 4 were waited for; matrix products, arithmetic and copies ran while one was open for 0% of the time, Pallas kernels for 16%

profile of v4, /device:TPU:0, one launch (start us, length us, event | category | flops | bytes accessed | tf_op | source)
XLA Modules:
  0.0 39.6 jit_solution(8682054785840182846)
XLA Ops:
  0.6 3.6 %deposit.1 = (bf16[608,128]{1,0:T(8,128)(2,1)S(1)}, s32[1,384]{1,0:T(1,128)S(1)}, bf16[192,384]{1,0:T(8,128)(2,1)S(1)}, bf16[384,512]{1,0:T(8,128)(2,1)S(1)}, bf...) custom-call(bf16[1024,128]{1,0:T(8,128)(2,1)} %bitcast.8, s32[256,128]{1,0:T(8,128)} %bitcast.9, ...), custom_call_target="tpu_custom_call" | custom-call | tf_op jit(solution)/shard_map/deposit/pallas_call | solution.py:510
  4.3 0.0 copy-start
  4.3 0.0 copy-start.1
  4.3 0.5 %collective-permute-start = (bf16[608,128]{1,0:T(8,128)(2,1)S(1)}, bf16[608,128]{1,0:T(8,128)(2,1)S(1)}, u32[]{:S(2)}, u32[]{:S(2)}) collective-permute-start(bf16[608,128]{1,0:T(8,128)(2,1)S(1)} %get-tuple-element.40.groups_ref), channel_id=1, source_target_pairs={{0,1},{1,0},{2,3},{3,2},{4,5},{5,4},{6,7},{7,6},{8,9},{9,8},{10,11... | collective-permute-start | bytes 466952 | tf_op jit(solution)/shard_map/ppermute | solution.py:533
  4.8 1.3 %own_groups.1 = (f32[4,384,128]{2,1,0:T(8,128)S(1)}, bf16[384,256]{1,0:T(8,128)(2,1)S(1)}, bf16[384,128]{1,0:T(8,128)(2,1)S(1)}, bf16[2,1664,128]{2,1,0:T(8,128)(2,1)S(1)}) custom-call(bf16[608,128]{1,0:T(8,128)(2,1)S(1)} %get-tuple-element.40.groups_ref, s32[1,384]{1,0:T(1,128)S(1)} %get-tuple-element.41.table_ref, ...), custom_call_target="tpu_custom_call" | custom-call | flops 452984832 | bytes 786432 | tf_op jit(solution)/shard_map/own_groups/pallas_call | solution.py:538
  6.1 0.0 collective-permute-done.groups_ref
  6.1 0.9 %other_groups.1 = (f32[96,512]{1,0:T(8,128)S(1)}, bf16[96,512]{1,0:T(8,128)(2,1)S(1)}, bf16[96,512]{1,0:T(8,128)(2,1)S(1)}, bf16[96,512]{1,0:T(8,128)(2,1)S(1)}) custom-call(bf16[608,128]{1,0:T(8,128)(2,1)S(1)} %collective-permute-done.groups_ref, bf16[384,256]{1,0:T(8,128)(2,1)S(1)} %get-tuple-element.45.inner_ref, ...), custom_call_target="tpu_custom_call" | custom-call | tf_op jit(solution)/shard_map/other_groups/pallas_call | solution.py:566
  7.0 2.7 %collective-permute-start.1 = (bf16[96,512]{1,0:T(8,128)(2,1)S(1)}, bf16[96,512]{1,0:T(8,128)(2,1)S(1)}, u32[]{:S(2)}, u32[]{:S(2)}) collective-permute-start(bf16[96,512]{1,0:T(8,128)(2,1)S(1)} %get-tuple-element.54), channel_id=1, source_target_pairs={{0,2},{1,5},{2,0},{3,7},{4,6},{5,1},{6,4},{7,3},{8,10},{9,13},{10,... | collective-permute-start | bytes 294920 | tf_op jit(solution)/shard_map/ppermute | solution.py:533
  9.7 1.5 %collective-permute-start.2 = (bf16[96,512]{1,0:T(8,128)(2,1)S(1)}, bf16[96,512]{1,0:T(8,128)(2,1)S(1)}, u32[]{:S(2)}, u32[]{:S(2)}) collective-permute-start(bf16[96,512]{1,0:T(8,128)(2,1)S(1)} %get-tuple-element.55), channel_id=1, source_target_pairs={{0,4},{1,3},{2,6},{3,1},{4,0},{5,7},{6,2},{7,5},{8,12},{9,11},{10,... | collective-permute-start | bytes 294920 | tf_op jit(solution)/shard_map/ppermute | solution.py:533
  11.2 0.0 collective-permute-start.3
  11.2 0.0 copy-done
  11.2 0.0 copy-done.1
  11.2 3.6 %response.2.refs_3_ = bf16[9,256,256]{2,1,0:T(8,128)(2,1)S(1)} custom-call(bf16[10,1664,128]{2,1,0:T(8,128)(2,1)S(1)} %get-tuple-element.69.early_ref, bf16[2,1664,128]{2,1,0:T(8,128)(2,1)S(1)} %get-tuple-element.70.late_ref, f32[1664,128]{1,0:T(8,128)S(1)} %copy-done, bf16[256,256]{1,0:T(8,128)(2,1)S(1)} %copy-done.1), custom_call_target="tpu_custom_call" | custom-call | flops 1472200704 | bytes 3833856 | tf_op jit(solution)/shard_map/response/pallas_call | solution.py:592
  14.9 0.0 copy-start.2
  14.9 0.0 collective-permute-done.1.refs_0_
  14.9 0.1 collective-permute-done.2.refs_1_
  15.0 1.7 %collective-permute-done.3.refs_2_ = bf16[96,512]{1,0:T(8,128)(2,1)S(1)} collective-permute-done((bf16[96,512]{1,0:T(8,128)(2,1)S(1)}, bf16[96,512]{1,0:T(8,128)(2,1)S(1)}, u32[]{:S(2)}, u32[]{:S(2)}) %collective-permute-start.3) | collective-permute-done | bytes 98336 | tf_op jit(solution)/shard_map/ppermute | solution.py:533
  16.7 0.1 merge.1
  16.8 0.0 copy-start.3
  16.8 3.7 %collective-permute-start.4 = (bf16[24,512]{1,0:T(8,128)(2,1)S(1)}, bf16[24,512]{1,0:T(8,128)(2,1)S(1)}, u32[]{:S(2)}, u32[]{:S(2)}) collective-permute-start(bf16[24,512]{1,0:T(8,128)(2,1)S(1)} %get-tuple-element.66), channel_id=1, source_target_pairs={{0,24},{1,25},{2,26},{3,27},{4,28},{5,29},{6,30},{7,31},{8,16},{9,... | collective-permute-start | bytes 73736 | tf_op jit(solution)/shard_map/ppermute | solution.py:533
  20.4 0.0 collective-permute-start.5
  20.4 0.8 %collective-permute-start.6 = (bf16[24,512]{1,0:T(8,128)(2,1)S(1)}, bf16[24,512]{1,0:T(8,128)(2,1)S(1)}, u32[]{:S(2)}, u32[]{:S(2)}) collective-permute-start(bf16[24,512]{1,0:T(8,128)(2,1)S(1)} %get-tuple-element.68), channel_id=1, source_target_pairs={{0,8},{1,9},{2,10},{3,11},{4,12},{5,13},{6,14},{7,15},{8,0},{9,1},... | collective-permute-start | bytes 73736 | tf_op jit(solution)/shard_map/ppermute | solution.py:533
  21.2 1.3 %response.3.refs_4_ = bf16[3,256,256]{2,1,0:T(8,128)(2,1)S(1)} custom-call(bf16[10,1664,128]{2,1,0:T(8,128)(2,1)S(1)} %get-tuple-element.69.early_ref, bf16[2,1664,128]{2,1,0:T(8,128)(2,1)S(1)} %get-tuple-element.70.late_ref, f32[1664,128]{1,0:T(8,128)S(1)} %copy-done, bf16[256,256]{1,0:T(8,128)(2,1)S(1)} %copy-done.1), custom_call_target="tpu_custom_call" | custom-call | flops 490733568 | bytes 1277952 | tf_op jit(solution)/shard_map/response/pallas_call | solution.py:592
  22.5 0.0 collective-permute-done.4.refs_0_
  22.5 2.6 %collective-permute-done.5.refs_1_ = bf16[24,512]{1,0:T(8,128)(2,1)S(1)} collective-permute-done((bf16[24,512]{1,0:T(8,128)(2,1)S(1)}, bf16[24,512]{1,0:T(8,128)(2,1)S(1)}, u32[]{:S(2)}, u32[]{:S(2)}) %collective-permute-start.5) | collective-permute-done | bytes 24608 | tf_op jit(solution)/shard_map/ppermute | solution.py:533
  25.2 0.0 collective-permute-done.6.refs_2_
  25.2 0.0 copy-done.2
  25.2 1.1 %synthesis.1 = bf16[256,128]{1,0:T(8,128)(2,1)} custom-call(f32[24,512]{1,0:T(8,128)S(1)} %get-tuple-element.62.kept_ref, bf16[24,512]{1,0:T(8,128)(2,1)S(1)} %collective-permute-done.4.refs_0_, bf16[24,512]{1,0:T(8,128)(2,1)S(1)} %collective-permute-done.5.refs_1_, bf16[24,512]{1,0:T(8,128)(2,1)S(1)} %collective-permute-done.6.refs_2_, ...), custom_call_target="tpu_custom_call" | custom-call | tf_op jit(solution)/shard_map/synthesis/pallas_call | solution.py:606
  26.3 3.3 %all-to-all-start = ((bf16[32,8,128]{2,1,0:T(8,128)(2,1)}), bf16[32,8,128]{2,1,0:T(8,128)(2,1)S(1)}, u32[]{:S(2)}, u32[]{:S(2)}) async-start(bf16[32,8,128]{2,1,0:T(8,128)(2,1)} %bitcast.4), calls=%async_computation | async-start | bytes 131072 | tf_op jit(solution)/shard_map/all_to_all | solution.py:616
  29.6 0.0 copy-done.3
  29.6 0.1 reshape.23.slots_ref
  29.7 7.3 %all-to-all-done = bf16[32,8,128]{2,1,0:T(8,128)(2,1)S(1)} async-done(((bf16[32,8,128]{2,1,0:T(8,128)(2,1)}), bf16[32,8,128]{2,1,0:T(8,128)(2,1)S(1)}, u32[]{:S(2)}, u32[]{:S(2)}) %all-to-all-start) | async-done | bytes 65568 | tf_op jit(solution)/shard_map/all_to_all | solution.py:616
  37.0 2.6 %inverse.1 = (f32[4,4,4096]{2,1,0:T(4,128)}, f32[4,4,4096]{2,1,0:T(4,128)}) custom-call(bf16[256,128]{1,0:T(8,128)(2,1)S(1)} %bitcast.7, s32[32,12]{1,0:T(8,128)S(1)} %reshape.23.slots_ref, bf16[16,512]{1,0:T(8,128)(2,1)} %constant.22.clone.turn_hbm, bf16[1536,512]{1,0:T(8,128)(2,1)} %constant.23.clone.table_hbm), custom_call_target="tpu_custom_call" | custom-call | tf_op jit(solution)/shard_map/inverse/pallas_call | solution.py:625
Async XLA Ops:
  4.3 7.0 %copy-start = (f32[1664,128]{1,0:T(8,128)S(1)}, f32[1664,128]{1,0:T(8,128)}, u32[]{:S(2)}) copy-start(f32[1664,128]{1,0:T(8,128)} %constant.19.clone.gain_ref) | copy-start | bytes 2555908
  4.3 7.0 %copy-start.1 = (bf16[256,256]{1,0:T(8,128)(2,1)S(1)}, bf16[256,256]{1,0:T(8,128)(2,1)}, u32[]{:S(2)}) copy-start(bf16[256,256]{1,0:T(8,128)(2,1)} %constant.20.clone.order_ref) | copy-start | bytes 393220
  4.3 1.8 %collective-permute-start = (bf16[608,128]{1,0:T(8,128)(2,1)S(1)}, bf16[608,128]{1,0:T(8,128)(2,1)S(1)}, u32[]{:S(2)}, u32[]{:S(2)}) collective-permute-start(bf16[608,128]{1,0:T(8,128)(2,1)S(1)} %get-tuple-element.40.groups_ref), channel_id=1, source_target_pairs={{0,1},{1,0},{2,3},{3,2},{4,5},{5,4},{6,7},{7,6},{8,9},{9,8},{10,11... | collective-permute-start | bytes 466952 | tf_op jit(solution)/shard_map/ppermute | solution.py:533
  7.0 7.8 %collective-permute-start.1 = (bf16[96,512]{1,0:T(8,128)(2,1)S(1)}, bf16[96,512]{1,0:T(8,128)(2,1)S(1)}, u32[]{:S(2)}, u32[]{:S(2)}) collective-permute-start(bf16[96,512]{1,0:T(8,128)(2,1)S(1)} %get-tuple-element.54), channel_id=1, source_target_pairs={{0,2},{1,5},{2,0},{3,7},{4,6},{5,1},{6,4},{7,3},{8,10},{9,13},{10,... | collective-permute-start | bytes 294920 | tf_op jit(solution)/shard_map/ppermute | solution.py:533
  9.7 5.3 %collective-permute-start.2 = (bf16[96,512]{1,0:T(8,128)(2,1)S(1)}, bf16[96,512]{1,0:T(8,128)(2,1)S(1)}, u32[]{:S(2)}, u32[]{:S(2)}) collective-permute-start(bf16[96,512]{1,0:T(8,128)(2,1)S(1)} %get-tuple-element.55), channel_id=1, source_target_pairs={{0,4},{1,3},{2,6},{3,1},{4,0},{5,7},{6,2},{7,5},{8,12},{9,11},{10,... | collective-permute-start | bytes 294920 | tf_op jit(solution)/shard_map/ppermute | solution.py:533
  11.2 5.5 %collective-permute-start.3 = (bf16[96,512]{1,0:T(8,128)(2,1)S(1)}, bf16[96,512]{1,0:T(8,128)(2,1)S(1)}, u32[]{:S(2)}, u32[]{:S(2)}) collective-permute-start(bf16[96,512]{1,0:T(8,128)(2,1)S(1)} %get-tuple-element.56), channel_id=1, source_target_pairs={{0,6},{1,7},{2,4},{3,5},{4,2},{5,3},{6,0},{7,1},{8,14},{9,15},{10,... | collective-permute-start | bytes 294920 | tf_op jit(solution)/shard_map/ppermute | solution.py:533
  14.9 10.3 %copy-start.2 = (bf16[96,96]{1,0:T(8,128)(2,1)S(1)}, bf16[96,96]{1,0:T(8,128)(2,1)}, u32[]{:S(2)}) copy-start(bf16[96,96]{1,0:T(8,128)(2,1)} %constant.21.clone.refs_5_) | copy-start | bytes 55300
  16.8 12.9 %copy-start.3 = (s32[384]{0:T(512)S(1)}, s32[384]{0:T(512)}, u32[]{:S(2)}) copy-start(s32[384]{0:T(512)} %table_hbm.2) | copy-start | bytes 4612
  16.8 5.7 %collective-permute-start.4 = (bf16[24,512]{1,0:T(8,128)(2,1)S(1)}, bf16[24,512]{1,0:T(8,128)(2,1)S(1)}, u32[]{:S(2)}, u32[]{:S(2)}) collective-permute-start(bf16[24,512]{1,0:T(8,128)(2,1)S(1)} %get-tuple-element.66), channel_id=1, source_target_pairs={{0,24},{1,25},{2,26},{3,27},{4,28},{5,29},{6,30},{7,31},{8,16},{9,... | collective-permute-start | bytes 73736 | tf_op jit(solution)/shard_map/ppermute | solution.py:533
  20.4 4.7 %collective-permute-start.5 = (bf16[24,512]{1,0:T(8,128)(2,1)S(1)}, bf16[24,512]{1,0:T(8,128)(2,1)S(1)}, u32[]{:S(2)}, u32[]{:S(2)}) collective-permute-start(bf16[24,512]{1,0:T(8,128)(2,1)S(1)} %get-tuple-element.67), channel_id=1, source_target_pairs={{0,16},{1,17},{2,18},{3,19},{4,20},{5,21},{6,22},{7,23},{8,24},{9,... | collective-permute-start | bytes 73736 | tf_op jit(solution)/shard_map/ppermute | solution.py:533
  20.4 4.7 %collective-permute-start.6 = (bf16[24,512]{1,0:T(8,128)(2,1)S(1)}, bf16[24,512]{1,0:T(8,128)(2,1)S(1)}, u32[]{:S(2)}, u32[]{:S(2)}) collective-permute-start(bf16[24,512]{1,0:T(8,128)(2,1)S(1)} %get-tuple-element.68), channel_id=1, source_target_pairs={{0,8},{1,9},{2,10},{3,11},{4,12},{5,13},{6,14},{7,15},{8,0},{9,1},... | collective-permute-start | bytes 73736 | tf_op jit(solution)/shard_map/ppermute | solution.py:533
  26.3 10.7 %all-to-all-start = ((bf16[32,8,128]{2,1,0:T(8,128)(2,1)}), bf16[32,8,128]{2,1,0:T(8,128)(2,1)S(1)}, u32[]{:S(2)}, u32[]{:S(2)}) async-start(bf16[32,8,128]{2,1,0:T(8,128)(2,1)} %bitcast.4), calls=%async_computation | async-start | bytes 131072 | tf_op jit(solution)/shard_map/all_to_all | solution.py:616

commit v5 on v4

--- a/solution.py
+++ b/solution.py
@@ -233,7 +233,7 @@
 
 
 def send_order(ways):
-    return [(1, 2), (2, 1), (3, 3)] if ways == 4 else [(i, i) for i in range(1, ways)]
+    return [(3, 3), (1, 2), (2, 1)] if ways == 4 else [(i, i) for i in range(1, ways)]
 
 
 def other_kernel(bins, groups, cycles, groups_ref, inner_ref, outer_ref, own_ref, keep_ref, *refs):
@@ -273,30 +273,30 @@
     return out.astype(jnp.bfloat16)
 
 
-def respond(basis, gain_ref, order_ref, out_ref, slot):
+def respond(basis, gain_ref, out_ref, slot):
     cycles = basis.shape[1]
     gain = jnp.concatenate([gain_ref[...]] * (cycles // BLOCK), 1)
     gained = (basis.astype(jnp.float32) * gain).astype(jnp.bfloat16)
     high, low = high_low(dot(basis, jnp.concatenate([basis, gained], 1), TN))
-    out_ref[slot, :cycles, :] = dot(high, order_ref[...]).astype(jnp.bfloat16)
-    out_ref[slot, cycles:, :] = dot(low, order_ref[...]).astype(jnp.bfloat16)
-
-
-def staged_response_kernel(start, early_ref, late_ref, gain_ref, order_ref, out_ref):
+    out_ref[slot, :cycles, :] = high
+    out_ref[slot, cycles:, :] = low
+
+
+def staged_response_kernel(start, early_ref, late_ref, gain_ref, out_ref):
     early = early_ref.shape[0]
     for slot in range(out_ref.shape[0]):
         at = start + slot
-        respond(early_ref[at] if at < early else late_ref[at - early], gain_ref, order_ref, out_ref, slot)
-
-
-def response_kernel(start, legendre_hbm, gain_ref, order_ref, out_ref, legendre_ref, sems):
+        respond(early_ref[at] if at < early else late_ref[at - early], gain_ref, out_ref, slot)
+
+
+def response_kernel(start, legendre_hbm, gain_ref, out_ref, legendre_ref, sems):
     count = out_ref.shape[0]
     copies = [pltpu.make_async_copy(legendre_hbm.at[start + i], legendre_ref.at[i], sems.at[i]) for i in range(count)]
     for copy in copies:
         copy.start()
     for slot in range(count):
         copies[slot].wait()
-        respond(legendre_ref[slot], gain_ref, order_ref, out_ref, slot)
+        respond(legendre_ref[slot], gain_ref, out_ref, slot)
 
 
 def slot_order(slots, bins):
@@ -310,7 +310,7 @@
 
 def synthesis_kernel(arrivals, pieces, kept_ref, *refs):
     partials, refs = refs[:arrivals], refs[arrivals:]
-    response_refs, (order_ref, out_ref) = refs[:pieces], refs[pieces:]
+    response_refs, (order_ref, columns_ref, out_ref) = refs[:pieces], refs[pieces:]
     cycles = response_refs[0].shape[1] // 2
     bins = kept_ref.shape[1] // cycles
     slots = kept_ref.shape[0] // 2
@@ -331,6 +331,7 @@
         parts.append(part[:per_slot, :] + part[per_slot:, :])
     parts.append(jnp.zeros((128 - slots * per_slot, 2 * cycles), jnp.float32))
     result = jnp.concatenate(parts, 0)
+    result = dot(result.astype(jnp.bfloat16), columns_ref[...])
     out_ref[...] = jnp.transpose(result).astype(jnp.bfloat16)
 
 
@@ -578,7 +579,7 @@
             arrived = [swap(x, even << bits[0], odd << bits[0]) for x, (even, odd) in zip(sends, order_of)]
         else:
             arrived = [swap(x, (i + 1) << bits[0]) for i, x in reversed(list(enumerate(sends)))]
-        first, last = (min(slots, slots * 2 * k * (2 * stages - k) // (2 * stages * stages)) for k in (stage, stage + 1))
+        first, last = (-(-slots * k * (2 * stages + 1 - k) // (stages * (stages + 1))) for k in (stage, stage + 1))
         count = last - first
         shape = shaped(count, 2 * cycles, 2 * cycles)
         cost = pl.CostEstimate(
@@ -591,26 +592,26 @@
             scratch = [pltpu.VMEM((count, degrees, cycles), jnp.bfloat16), pltpu.SemaphoreType.DMA((count,))]
         response = pl.pallas_call(
             kernel,
-            in_specs=[vmem if staged else hbm] * len(basis) + [vmem] * 2,
+            in_specs=[vmem if staged else hbm] * len(basis) + [vmem],
             out_specs=vmem,
             out_shape=shape,
             scratch_shapes=scratch,
             compiler_params=limits,
             cost_estimate=cost,
             name="response",
-        )(*basis if staged else [in_hbm(x) for x in basis], gain, order)
+        )(*basis if staged else [in_hbm(x) for x in basis], gain)
         *arrived, response = lax.optimization_barrier((*arrived, response))
         responses.append(response)
         kernel, inputs, scratch = functools.partial(merge_kernel, len(arrived)), (kept, *arrived), []
 
     outgoing = pl.pallas_call(
         functools.partial(synthesis_kernel, len(inputs) - 1, len(responses)),
-        in_specs=[vmem] * (len(inputs) + len(responses) + 1),
+        in_specs=[vmem] * (len(inputs) + len(responses) + 2),
         out_specs=vmem,
         out_shape=shaped(2 * cycles, 128),
         compiler_params=limits,
         name="synthesis",
-    )(*inputs, *responses, slot_order(slots, bins))
+    )(*inputs, *responses, slot_order(slots, bins), order)
     outgoing = outgoing.reshape(devices, 2 * cycles_here, 128)
     outgoing, held = lax.optimization_barrier((outgoing, m_table))
     arrived = lax.all_to_all(outgoing, axes, split_axis=0, concat_axis=0, tiled=True)

time: 39.9 us -> 40.6 us (1.018)
  Pallas kernels: 14.5 us -> 11.7 us
  waiting for transfers between devices: 11.8 us -> 14.4 us
  starting transfers between devices: 12.5 us -> 13.4 us
    pallas_call x2, Pallas kernels: 4.9 us -> 1.93 us  [per_device(): pl.pallas_call(kernel, in_specs=[vmem if staged else hbm] * len(basis) +...]
    ppermute x7, waiting for transfers between devices: 4.46 us -> 7.08 us  [swap(): lax.ppermute(x, axes, [(i, i ^ masks[i % 2]) for i in range(devices)])]
    all_to_all x1, starting transfers between devices: 3.3 us -> 4.17 us  [per_device(): lax.all_to_all(outgoing, axes, split_axis=0, concat_axis=0, tiled=True)]
  transfers between devices with their start and end apart: 8 -> 8, of which waited for: 4 -> 6; matrix products, arithmetic and copies ran while one was open for 0% -> 0% of each run, Pallas kernels for 16% -> 8%
where the time goes in v5:
time: 40.6 us; the launch traced here: 40.3 us
  waiting for transfers between devices  14.4 us (35%)
  starting transfers between devices  13.4 us (33%)
  Pallas kernels  11.7 us (29%)
  between operations  0.74 us (2%)
    ppermute x7, starting transfers between devices, swap(): lax.ppermute(x, axes, [(i, i ^ masks[i % 2]) for i in range(devices)])  9.2 us
    all_to_all x1, waiting for transfers between devices, per_device(): lax.all_to_all(outgoing, axes, split_axis=0, concat_axis=0, tiled=True)  7.3 us
    ppermute x7, waiting for transfers between devices, swap(): lax.ppermute(x, axes, [(i, i ^ masks[i % 2]) for i in range(devices)])  7.08 us
    all_to_all x1, starting transfers between devices, per_device(): lax.all_to_all(outgoing, axes, split_axis=0, concat_axis=0, tiled=True)  4.17 us
    pallas_call x1, Pallas kernels, per_device(): pl.pallas_call(functools.partial(first_kernel, slots, cycles_here * SEGME...  3.62 us
    pallas_call x1, Pallas kernels, per_device(): pl.pallas_call(inverse_kernel, in_specs=[vmem] * 2 + [hbm] * 2, out_specs...  2.61 us
    pallas_call x2, Pallas kernels, per_device(): pl.pallas_call(kernel, in_specs=[vmem if staged else hbm] * len(basis) +...  1.93 us
    pallas_call x1, Pallas kernels, per_device(): pl.pallas_call(functools.partial(synthesis_kernel, len(inputs) - 1, len(r...  1.29 us
  transfers between devices with their start and end apart: 8, of which 6 were waited for; matrix products, arithmetic and copies ran while one was open for 0% of the time, Pallas kernels for 8%

profile of v5, /device:TPU:0, one launch (start us, length us, event | category | flops | bytes accessed | tf_op | source)
XLA Modules:
  0.0 40.3 jit_solution(17448036071333271259)
XLA Ops:
  0.6 3.6 %deposit.1 = (bf16[608,128]{1,0:T(8,128)(2,1)S(1)}, s32[1,384]{1,0:T(1,128)S(1)}, bf16[192,384]{1,0:T(8,128)(2,1)S(1)}, bf16[384,512]{1,0:T(8,128)(2,1)S(1)}, bf...) custom-call(bf16[1024,128]{1,0:T(8,128)(2,1)} %bitcast.8, s32[256,128]{1,0:T(8,128)} %bitcast.9, ...), custom_call_target="tpu_custom_call" | custom-call | tf_op jit(solution)/shard_map/deposit/pallas_call | solution.py:511
  4.3 0.0 copy-start
  4.3 0.5 %collective-permute-start = (bf16[608,128]{1,0:T(8,128)(2,1)S(1)}, bf16[608,128]{1,0:T(8,128)(2,1)S(1)}, u32[]{:S(2)}, u32[]{:S(2)}) collective-permute-start(bf16[608,128]{1,0:T(8,128)(2,1)S(1)} %get-tuple-element.40.groups_ref), channel_id=1, source_target_pairs={{0,1},{1,0},{2,3},{3,2},{4,5},{5,4},{6,7},{7,6},{8,9},{9,8},{10,11... | collective-permute-start | bytes 466952 | tf_op jit(solution)/shard_map/ppermute | solution.py:534
  4.8 1.3 %own_groups.1 = (f32[4,384,128]{2,1,0:T(8,128)S(1)}, bf16[384,256]{1,0:T(8,128)(2,1)S(1)}, bf16[384,128]{1,0:T(8,128)(2,1)S(1)}, bf16[2,1664,128]{2,1,0:T(8,128)(2,1)S(1)}) custom-call(bf16[608,128]{1,0:T(8,128)(2,1)S(1)} %get-tuple-element.40.groups_ref, s32[1,384]{1,0:T(1,128)S(1)} %get-tuple-element.41.table_ref, ...), custom_call_target="tpu_custom_call" | custom-call | flops 452984832 | bytes 786432 | tf_op jit(solution)/shard_map/own_groups/pallas_call | solution.py:539
  6.1 0.0 collective-permute-done.groups_ref
  6.1 0.9 %other_groups.1 = (f32[96,512]{1,0:T(8,128)S(1)}, bf16[96,512]{1,0:T(8,128)(2,1)S(1)}, bf16[96,512]{1,0:T(8,128)(2,1)S(1)}, bf16[96,512]{1,0:T(8,128)(2,1)S(1)}) custom-call(bf16[608,128]{1,0:T(8,128)(2,1)S(1)} %collective-permute-done.groups_ref, bf16[384,256]{1,0:T(8,128)(2,1)S(1)} %get-tuple-element.45.inner_ref, ...), custom_call_target="tpu_custom_call" | custom-call | tf_op jit(solution)/shard_map/other_groups/pallas_call | solution.py:567
  7.0 3.6 %collective-permute-start.1 = (bf16[96,512]{1,0:T(8,128)(2,1)S(1)}, bf16[96,512]{1,0:T(8,128)(2,1)S(1)}, u32[]{:S(2)}, u32[]{:S(2)}) collective-permute-start(bf16[96,512]{1,0:T(8,128)(2,1)S(1)} %get-tuple-element.54), channel_id=1, source_target_pairs={{0,6},{1,7},{2,4},{3,5},{4,2},{5,3},{6,0},{7,1},{8,14},{9,15},{10,... | collective-permute-start | bytes 294920 | tf_op jit(solution)/shard_map/ppermute | solution.py:534
  10.6 0.5 %collective-permute-start.2 = (bf16[96,512]{1,0:T(8,128)(2,1)S(1)}, bf16[96,512]{1,0:T(8,128)(2,1)S(1)}, u32[]{:S(2)}, u32[]{:S(2)}) collective-permute-start(bf16[96,512]{1,0:T(8,128)(2,1)S(1)} %get-tuple-element.55), channel_id=1, source_target_pairs={{0,2},{1,5},{2,0},{3,7},{4,6},{5,1},{6,4},{7,3},{8,10},{9,13},{10,... | collective-permute-start | bytes 294920 | tf_op jit(solution)/shard_map/ppermute | solution.py:534
  11.1 0.1 collective-permute-start.3
  11.3 0.0 copy-done
  11.3 1.2 %response.2.refs_3_ = bf16[8,256,256]{2,1,0:T(8,128)(2,1)S(1)} custom-call(bf16[10,1664,128]{2,1,0:T(8,128)(2,1)S(1)} %get-tuple-element.69.early_ref, bf16[2,1664,128]{2,1,0:T(8,128)(2,1)S(1)} %get-tuple-element.70.late_ref, f32[1664,128]{1,0:T(8,128)S(1)} %copy-done), custom_call_target="tpu_custom_call" | custom-call | flops 1308622848 | bytes 3407872 | tf_op jit(solution)/shard_map/response/pallas_call | solution.py:593
  12.5 0.0 copy-start.1
  12.5 0.0 copy-start.2
  12.5 1.7 %collective-permute-done.1.refs_0_ = bf16[96,512]{1,0:T(8,128)(2,1)S(1)} collective-permute-done((bf16[96,512]{1,0:T(8,128)(2,1)S(1)}, bf16[96,512]{1,0:T(8,128)(2,1)S(1)}, u32[]{:S(2)}, u32[]{:S(2)}) %collective-permute-start.1) | collective-permute-done | bytes 98336 | tf_op jit(solution)/shard_map/ppermute | solution.py:534
  14.3 1.9 %collective-permute-done.2.refs_1_ = bf16[96,512]{1,0:T(8,128)(2,1)S(1)} collective-permute-done((bf16[96,512]{1,0:T(8,128)(2,1)S(1)}, bf16[96,512]{1,0:T(8,128)(2,1)S(1)}, u32[]{:S(2)}, u32[]{:S(2)}) %collective-permute-start.2) | collective-permute-done | bytes 98336 | tf_op jit(solution)/shard_map/ppermute | solution.py:534
  16.1 0.3 collective-permute-done.3.refs_2_
  16.4 0.1 merge.1
  16.4 0.0 copy-start.3
  16.4 3.7 %collective-permute-start.4 = (bf16[24,512]{1,0:T(8,128)(2,1)S(1)}, bf16[24,512]{1,0:T(8,128)(2,1)S(1)}, u32[]{:S(2)}, u32[]{:S(2)}) collective-permute-start(bf16[24,512]{1,0:T(8,128)(2,1)S(1)} %get-tuple-element.66), channel_id=1, source_target_pairs={{0,24},{1,25},{2,26},{3,27},{4,28},{5,29},{6,30},{7,31},{8,16},{9,... | collective-permute-start | bytes 73736 | tf_op jit(solution)/shard_map/ppermute | solution.py:534
  20.1 0.0 collective-permute-start.5
  20.1 0.8 %collective-permute-start.6 = (bf16[24,512]{1,0:T(8,128)(2,1)S(1)}, bf16[24,512]{1,0:T(8,128)(2,1)S(1)}, u32[]{:S(2)}, u32[]{:S(2)}) collective-permute-start(bf16[24,512]{1,0:T(8,128)(2,1)S(1)} %get-tuple-element.68), channel_id=1, source_target_pairs={{0,8},{1,9},{2,10},{3,11},{4,12},{5,13},{6,14},{7,15},{8,0},{9,1},... | collective-permute-start | bytes 73736 | tf_op jit(solution)/shard_map/ppermute | solution.py:534
  20.9 0.7 %response.3.refs_4_ = bf16[4,256,256]{2,1,0:T(8,128)(2,1)S(1)} custom-call(bf16[10,1664,128]{2,1,0:T(8,128)(2,1)S(1)} %get-tuple-element.69.early_ref, bf16[2,1664,128]{2,1,0:T(8,128)(2,1)S(1)} %get-tuple-element.70.late_ref, f32[1664,128]{1,0:T(8,128)S(1)} %copy-done), custom_call_target="tpu_custom_call" | custom-call | flops 654311424 | bytes 1703936 | tf_op jit(solution)/shard_map/response/pallas_call | solution.py:593
  21.6 0.5 %collective-permute-done.4.refs_0_ = bf16[24,512]{1,0:T(8,128)(2,1)S(1)} collective-permute-done((bf16[24,512]{1,0:T(8,128)(2,1)S(1)}, bf16[24,512]{1,0:T(8,128)(2,1)S(1)}, u32[]{:S(2)}, u32[]{:S(2)}) %collective-permute-start.4) | collective-permute-done | bytes 24608 | tf_op jit(solution)/shard_map/ppermute | solution.py:534
  22.1 2.7 %collective-permute-done.5.refs_1_ = bf16[24,512]{1,0:T(8,128)(2,1)S(1)} collective-permute-done((bf16[24,512]{1,0:T(8,128)(2,1)S(1)}, bf16[24,512]{1,0:T(8,128)(2,1)S(1)}, u32[]{:S(2)}, u32[]{:S(2)}) %collective-permute-start.5) | collective-permute-done | bytes 24608 | tf_op jit(solution)/shard_map/ppermute | solution.py:534
  24.8 0.0 collective-permute-done.6.refs_2_
  24.8 0.0 copy-done.1
  24.8 0.0 copy-done.2
  24.8 1.3 %synthesis.1 = bf16[256,128]{1,0:T(8,128)(2,1)} custom-call(f32[24,512]{1,0:T(8,128)S(1)} %get-tuple-element.62.kept_ref, bf16[24,512]{1,0:T(8,128)(2,1)S(1)} %collective-permute-done.4.refs_0_, bf16[24,512]{1,0:T(8,128)(2,1)S(1)} %collective-permute-done.5.refs_1_, bf16[24,512]{1,0:T(8,128)(2,1)S(1)} %collective-permute-done.6.refs_2_, ...), custom_call_target="tpu_custom_call" | custom-call | tf_op jit(solution)/shard_map/synthesis/pallas_call | solution.py:607
  26.1 4.2 %all-to-all-start = ((bf16[32,8,128]{2,1,0:T(8,128)(2,1)}), bf16[32,8,128]{2,1,0:T(8,128)(2,1)S(1)}, u32[]{:S(2)}, u32[]{:S(2)}) async-start(bf16[32,8,128]{2,1,0:T(8,128)(2,1)} %bitcast.4), calls=%async_computation | async-start | bytes 131072 | tf_op jit(solution)/shard_map/all_to_all | solution.py:617
  30.3 0.0 copy-done.3
  30.3 0.1 reshape.23.slots_ref
  30.4 7.3 %all-to-all-done = bf16[32,8,128]{2,1,0:T(8,128)(2,1)S(1)} async-done(((bf16[32,8,128]{2,1,0:T(8,128)(2,1)}), bf16[32,8,128]{2,1,0:T(8,128)(2,1)S(1)}, u32[]{:S(2)}, u32[]{:S(2)}) %all-to-all-start) | async-done | bytes 65568 | tf_op jit(solution)/shard_map/all_to_all | solution.py:617
  37.7 2.6 %inverse.1 = (f32[4,4,4096]{2,1,0:T(4,128)}, f32[4,4,4096]{2,1,0:T(4,128)}) custom-call(bf16[256,128]{1,0:T(8,128)(2,1)S(1)} %bitcast.7, s32[32,12]{1,0:T(8,128)S(1)} %reshape.23.slots_ref, bf16[16,512]{1,0:T(8,128)(2,1)} %constant.22.clone.turn_hbm, bf16[1536,512]{1,0:T(8,128)(2,1)} %constant.23.clone.table_hbm), custom_call_target="tpu_custom_call" | custom-call | tf_op jit(solution)/shard_map/inverse/pallas_call | solution.py:626
Async XLA Ops:
  4.3 7.0 %copy-start = (f32[1664,128]{1,0:T(8,128)S(1)}, f32[1664,128]{1,0:T(8,128)}, u32[]{:S(2)}) copy-start(f32[1664,128]{1,0:T(8,128)} %constant.19.clone.gain_ref) | copy-start | bytes 2555908
  4.3 1.8 %collective-permute-start = (bf16[608,128]{1,0:T(8,128)(2,1)S(1)}, bf16[608,128]{1,0:T(8,128)(2,1)S(1)}, u32[]{:S(2)}, u32[]{:S(2)}) collective-permute-start(bf16[608,128]{1,0:T(8,128)(2,1)S(1)} %get-tuple-element.40.groups_ref), channel_id=1, source_target_pairs={{0,1},{1,0},{2,3},{3,2},{4,5},{5,4},{6,7},{7,6},{8,9},{9,8},{10,11... | collective-permute-start | bytes 466952 | tf_op jit(solution)/shard_map/ppermute | solution.py:534
  7.0 7.2 %collective-permute-start.1 = (bf16[96,512]{1,0:T(8,128)(2,1)S(1)}, bf16[96,512]{1,0:T(8,128)(2,1)S(1)}, u32[]{:S(2)}, u32[]{:S(2)}) collective-permute-start(bf16[96,512]{1,0:T(8,128)(2,1)S(1)} %get-tuple-element.54), channel_id=1, source_target_pairs={{0,6},{1,7},{2,4},{3,5},{4,2},{5,3},{6,0},{7,1},{8,14},{9,15},{10,... | collective-permute-start | bytes 294920 | tf_op jit(solution)/shard_map/ppermute | solution.py:534
  10.6 5.5 %collective-permute-start.2 = (bf16[96,512]{1,0:T(8,128)(2,1)S(1)}, bf16[96,512]{1,0:T(8,128)(2,1)S(1)}, u32[]{:S(2)}, u32[]{:S(2)}) collective-permute-start(bf16[96,512]{1,0:T(8,128)(2,1)S(1)} %get-tuple-element.55), channel_id=1, source_target_pairs={{0,2},{1,5},{2,0},{3,7},{4,6},{5,1},{6,4},{7,3},{8,10},{9,13},{10,... | collective-permute-start | bytes 294920 | tf_op jit(solution)/shard_map/ppermute | solution.py:534
  11.1 5.3 %collective-permute-start.3 = (bf16[96,512]{1,0:T(8,128)(2,1)S(1)}, bf16[96,512]{1,0:T(8,128)(2,1)S(1)}, u32[]{:S(2)}, u32[]{:S(2)}) collective-permute-start(bf16[96,512]{1,0:T(8,128)(2,1)S(1)} %get-tuple-element.56), channel_id=1, source_target_pairs={{0,4},{1,3},{2,6},{3,1},{4,0},{5,7},{6,2},{7,5},{8,12},{9,11},{10,... | collective-permute-start | bytes 294920 | tf_op jit(solution)/shard_map/ppermute | solution.py:534
  12.5 12.3 %copy-start.1 = (bf16[256,256]{1,0:T(8,128)(2,1)S(1)}, bf16[256,256]{1,0:T(8,128)(2,1)}, u32[]{:S(2)}) copy-start(bf16[256,256]{1,0:T(8,128)(2,1)} %constant.21.clone.refs_6_) | copy-start | bytes 393220
  12.5 12.3 %copy-start.2 = (bf16[96,96]{1,0:T(8,128)(2,1)S(1)}, bf16[96,96]{1,0:T(8,128)(2,1)}, u32[]{:S(2)}) copy-start(bf16[96,96]{1,0:T(8,128)(2,1)} %constant.20.clone.refs_5_) | copy-start | bytes 55300
  16.4 13.9 %copy-start.3 = (s32[384]{0:T(512)S(1)}, s32[384]{0:T(512)}, u32[]{:S(2)}) copy-start(s32[384]{0:T(512)} %table_hbm.2) | copy-start | bytes 4612
  16.4 5.7 %collective-permute-start.4 = (bf16[24,512]{1,0:T(8,128)(2,1)S(1)}, bf16[24,512]{1,0:T(8,128)(2,1)S(1)}, u32[]{:S(2)}, u32[]{:S(2)}) collective-permute-start(bf16[24,512]{1,0:T(8,128)(2,1)S(1)} %get-tuple-element.66), channel_id=1, source_target_pairs={{0,24},{1,25},{2,26},{3,27},{4,28},{5,29},{6,30},{7,31},{8,16},{9,... | collective-permute-start | bytes 73736 | tf_op jit(solution)/shard_map/ppermute | solution.py:534
  20.1 4.7 %collective-permute-start.5 = (bf16[24,512]{1,0:T(8,128)(2,1)S(1)}, bf16[24,512]{1,0:T(8,128)(2,1)S(1)}, u32[]{:S(2)}, u32[]{:S(2)}) collective-permute-start(bf16[24,512]{1,0:T(8,128)(2,1)S(1)} %get-tuple-element.67), channel_id=1, source_target_pairs={{0,16},{1,17},{2,18},{3,19},{4,20},{5,21},{6,22},{7,23},{8,24},{9,... | collective-permute-start | bytes 73736 | tf_op jit(solution)/shard_map/ppermute | solution.py:534
  20.1 4.7 %collective-permute-start.6 = (bf16[24,512]{1,0:T(8,128)(2,1)S(1)}, bf16[24,512]{1,0:T(8,128)(2,1)S(1)}, u32[]{:S(2)}, u32[]{:S(2)}) collective-permute-start(bf16[24,512]{1,0:T(8,128)(2,1)S(1)} %get-tuple-element.68), channel_id=1, source_target_pairs={{0,8},{1,9},{2,10},{3,11},{4,12},{5,13},{6,14},{7,15},{8,0},{9,1},... | collective-permute-start | bytes 73736 | tf_op jit(solution)/shard_map/ppermute | solution.py:534
  26.1 11.6 %all-to-all-start = ((bf16[32,8,128]{2,1,0:T(8,128)(2,1)}), bf16[32,8,128]{2,1,0:T(8,128)(2,1)S(1)}, u32[]{:S(2)}, u32[]{:S(2)}) async-start(bf16[32,8,128]{2,1,0:T(8,128)(2,1)} %bitcast.4), calls=%async_computation | async-start | bytes 131072 | tf_op jit(solution)/shard_map/all_to_all | solution.py:617

commit v6 on v4

--- a/solution.py
+++ b/solution.py
@@ -278,8 +278,7 @@
     gain = jnp.concatenate([gain_ref[...]] * (cycles // BLOCK), 1)
     gained = (basis.astype(jnp.float32) * gain).astype(jnp.bfloat16)
     high, low = high_low(dot(basis, jnp.concatenate([basis, gained], 1), TN))
-    out_ref[slot, :cycles, :] = dot(high, order_ref[...]).astype(jnp.bfloat16)
-    out_ref[slot, cycles:, :] = dot(low, order_ref[...]).astype(jnp.bfloat16)
+    out_ref[slot] = dot(jnp.concatenate([high, low], 0), order_ref[...]).astype(jnp.bfloat16)
 
 
 def staged_response_kernel(start, early_ref, late_ref, gain_ref, order_ref, out_ref):
@@ -577,7 +576,8 @@
             order_of = send_order(ways)
             arrived = [swap(x, even << bits[0], odd << bits[0]) for x, (even, odd) in zip(sends, order_of)]
         else:
-            arrived = [swap(x, (i + 1) << bits[0]) for i, x in reversed(list(enumerate(sends)))]
+            line = [2, 3, 1] if ways == 4 else range(ways - 1, 0, -1)
+            arrived = [swap(sends[i - 1], i << bits[0]) for i in line]
         first, last = (min(slots, slots * 2 * k * (2 * stages - k) // (2 * stages * stages)) for k in (stage, stage + 1))
         count = last - first
         shape = shaped(count, 2 * cycles, 2 * cycles)

time: 39.9 us -> 39.8 us (level)
  waiting for transfers between devices: 11.8 us -> 12.5 us
  Pallas kernels: 14.5 us -> 13.9 us
    ppermute x7, waiting for transfers between devices: 4.46 us -> 5.15 us  [swap(): lax.ppermute(x, axes, [(i, i ^ masks[i % 2]) for i in range(devices)])]
    pallas_call x2, Pallas kernels: 4.9 us -> 4.31 us  [per_device(): pl.pallas_call(kernel, in_specs=[vmem if staged else hbm] * len(basis) +...]
  transfers between devices with their start and end apart: 8 -> 8, of which waited for: 4 -> 4; matrix products, arithmetic and copies ran while one was open for 0% -> 0% of each run, Pallas kernels for 16% -> 14%
where the time goes in v6:
time: 39.8 us; the launch traced here: 39.5 us
  Pallas kernels  13.9 us (35%)
  waiting for transfers between devices  12.5 us (31%)
  starting transfers between devices  12.2 us (31%)
  between operations  0.75 us (2%)
    ppermute x7, starting transfers between devices, swap(): lax.ppermute(x, axes, [(i, i ^ masks[i % 2]) for i in range(devices)])  8.95 us
    all_to_all x1, waiting for transfers between devices, per_device(): lax.all_to_all(outgoing, axes, split_axis=0, concat_axis=0, tiled=True)  7.3 us
    ppermute x7, waiting for transfers between devices, swap(): lax.ppermute(x, axes, [(i, i ^ masks[i % 2]) for i in range(devices)])  5.15 us
    pallas_call x2, Pallas kernels, per_device(): pl.pallas_call(kernel, in_specs=[vmem if staged else hbm] * len(basis) +...  4.31 us
    pallas_call x1, Pallas kernels, per_device(): pl.pallas_call(functools.partial(first_kernel, slots, cycles_here * SEGME...  3.62 us
    all_to_all x1, starting transfers between devices, per_device(): lax.all_to_all(outgoing, axes, split_axis=0, concat_axis=0, tiled=True)  3.3 us
    pallas_call x1, Pallas kernels, per_device(): pl.pallas_call(inverse_kernel, in_specs=[vmem] * 2 + [hbm] * 2, out_specs...  2.61 us
    pallas_call x1, Pallas kernels, per_device(): pl.pallas_call(functools.partial(own_kernel, bins, live, cycles, ahead),...  1.29 us
  transfers between devices with their start and end apart: 8, of which 4 were waited for; matrix products, arithmetic and copies ran while one was open for 0% of the time, Pallas kernels for 14%

profile of v6, /device:TPU:0, one launch (start us, length us, event | category | flops | bytes accessed | tf_op | source)
XLA Modules:
  0.0 39.5 jit_solution(3969195567062823910)
XLA Ops:
  0.6 3.6 %deposit.1 = (bf16[608,128]{1,0:T(8,128)(2,1)S(1)}, s32[1,384]{1,0:T(1,128)S(1)}, bf16[192,384]{1,0:T(8,128)(2,1)S(1)}, bf16[384,512]{1,0:T(8,128)(2,1)S(1)}, bf...) custom-call(bf16[1024,128]{1,0:T(8,128)(2,1)} %bitcast.8, s32[256,128]{1,0:T(8,128)} %bitcast.9, ...), custom_call_target="tpu_custom_call" | custom-call | tf_op jit(solution)/shard_map/deposit/pallas_call | solution.py:509
  4.3 0.0 copy-start
  4.3 0.0 copy-start.1
  4.3 0.5 %collective-permute-start = (bf16[608,128]{1,0:T(8,128)(2,1)S(1)}, bf16[608,128]{1,0:T(8,128)(2,1)S(1)}, u32[]{:S(2)}, u32[]{:S(2)}) collective-permute-start(bf16[608,128]{1,0:T(8,128)(2,1)S(1)} %get-tuple-element.40.groups_ref), channel_id=1, source_target_pairs={{0,1},{1,0},{2,3},{3,2},{4,5},{5,4},{6,7},{7,6},{8,9},{9,8},{10,11... | collective-permute-start | bytes 466952 | tf_op jit(solution)/shard_map/ppermute | solution.py:532
  4.8 1.3 %own_groups.1 = (f32[4,384,128]{2,1,0:T(8,128)S(1)}, bf16[384,256]{1,0:T(8,128)(2,1)S(1)}, bf16[384,128]{1,0:T(8,128)(2,1)S(1)}, bf16[2,1664,128]{2,1,0:T(8,128)(2,1)S(1)}) custom-call(bf16[608,128]{1,0:T(8,128)(2,1)S(1)} %get-tuple-element.40.groups_ref, s32[1,384]{1,0:T(1,128)S(1)} %get-tuple-element.41.table_ref, ...), custom_call_target="tpu_custom_call" | custom-call | flops 452984832 | bytes 786432 | tf_op jit(solution)/shard_map/own_groups/pallas_call | solution.py:537
  6.1 0.0 collective-permute-done.groups_ref
  6.1 0.9 %other_groups.1 = (f32[96,512]{1,0:T(8,128)S(1)}, bf16[96,512]{1,0:T(8,128)(2,1)S(1)}, bf16[96,512]{1,0:T(8,128)(2,1)S(1)}, bf16[96,512]{1,0:T(8,128)(2,1)S(1)}) custom-call(bf16[608,128]{1,0:T(8,128)(2,1)S(1)} %collective-permute-done.groups_ref, bf16[384,256]{1,0:T(8,128)(2,1)S(1)} %get-tuple-element.45.inner_ref, ...), custom_call_target="tpu_custom_call" | custom-call | tf_op jit(solution)/shard_map/other_groups/pallas_call | solution.py:565
  7.0 2.7 %collective-permute-start.1 = (bf16[96,512]{1,0:T(8,128)(2,1)S(1)}, bf16[96,512]{1,0:T(8,128)(2,1)S(1)}, u32[]{:S(2)}, u32[]{:S(2)}) collective-permute-start(bf16[96,512]{1,0:T(8,128)(2,1)S(1)} %get-tuple-element.54), channel_id=1, source_target_pairs={{0,2},{1,5},{2,0},{3,7},{4,6},{5,1},{6,4},{7,3},{8,10},{9,13},{10,... | collective-permute-start | bytes 294920 | tf_op jit(solution)/shard_map/ppermute | solution.py:532
  9.7 1.5 %collective-permute-start.2 = (bf16[96,512]{1,0:T(8,128)(2,1)S(1)}, bf16[96,512]{1,0:T(8,128)(2,1)S(1)}, u32[]{:S(2)}, u32[]{:S(2)}) collective-permute-start(bf16[96,512]{1,0:T(8,128)(2,1)S(1)} %get-tuple-element.55), channel_id=1, source_target_pairs={{0,4},{1,3},{2,6},{3,1},{4,0},{5,7},{6,2},{7,5},{8,12},{9,11},{10,... | collective-permute-start | bytes 294920 | tf_op jit(solution)/shard_map/ppermute | solution.py:532
  11.2 0.0 collective-permute-start.3
  11.2 0.0 copy-done
  11.2 0.0 copy-done.1
  11.2 3.3 %response.2.refs_3_ = bf16[9,256,256]{2,1,0:T(8,128)(2,1)S(1)} custom-call(bf16[10,1664,128]{2,1,0:T(8,128)(2,1)S(1)} %get-tuple-element.69.early_ref, bf16[2,1664,128]{2,1,0:T(8,128)(2,1)S(1)} %get-tuple-element.70.late_ref, f32[1664,128]{1,0:T(8,128)S(1)} %copy-done, bf16[256,256]{1,0:T(8,128)(2,1)S(1)} %copy-done.1), custom_call_target="tpu_custom_call" | custom-call | flops 1472200704 | bytes 3833856 | tf_op jit(solution)/shard_map/response/pallas_call | solution.py:592
  14.6 0.0 copy-start.2
  14.6 0.0 collective-permute-done.1.refs_0_
  14.6 0.4 %collective-permute-done.2.refs_1_ = bf16[96,512]{1,0:T(8,128)(2,1)S(1)} collective-permute-done((bf16[96,512]{1,0:T(8,128)(2,1)S(1)}, bf16[96,512]{1,0:T(8,128)(2,1)S(1)}, u32[]{:S(2)}, u32[]{:S(2)}) %collective-permute-start.2) | collective-permute-done | bytes 98336 | tf_op jit(solution)/shard_map/ppermute | solution.py:532
  15.0 1.7 %collective-permute-done.3.refs_2_ = bf16[96,512]{1,0:T(8,128)(2,1)S(1)} collective-permute-done((bf16[96,512]{1,0:T(8,128)(2,1)S(1)}, bf16[96,512]{1,0:T(8,128)(2,1)S(1)}, u32[]{:S(2)}, u32[]{:S(2)}) %collective-permute-start.3) | collective-permute-done | bytes 98336 | tf_op jit(solution)/shard_map/ppermute | solution.py:532
  16.7 0.1 merge.1
  16.8 0.0 copy-start.3
  16.8 2.7 %collective-permute-start.4 = (bf16[24,512]{1,0:T(8,128)(2,1)S(1)}, bf16[24,512]{1,0:T(8,128)(2,1)S(1)}, u32[]{:S(2)}, u32[]{:S(2)}) collective-permute-start(bf16[24,512]{1,0:T(8,128)(2,1)S(1)} %get-tuple-element.66), channel_id=1, source_target_pairs={{0,16},{1,17},{2,18},{3,19},{4,20},{5,21},{6,22},{7,23},{8,24},{9,... | collective-permute-start | bytes 73736 | tf_op jit(solution)/shard_map/ppermute | solution.py:532
  19.4 1.3 %collective-permute-start.5 = (bf16[24,512]{1,0:T(8,128)(2,1)S(1)}, bf16[24,512]{1,0:T(8,128)(2,1)S(1)}, u32[]{:S(2)}, u32[]{:S(2)}) collective-permute-start(bf16[24,512]{1,0:T(8,128)(2,1)S(1)} %get-tuple-element.67), channel_id=1, source_target_pairs={{0,24},{1,25},{2,26},{3,27},{4,28},{5,29},{6,30},{7,31},{8,16},{9,... | collective-permute-start | bytes 73736 | tf_op jit(solution)/shard_map/ppermute | solution.py:532
  20.8 0.2 collective-permute-start.6
  21.0 1.0 %response.3.refs_4_ = bf16[3,256,256]{2,1,0:T(8,128)(2,1)S(1)} custom-call(bf16[10,1664,128]{2,1,0:T(8,128)(2,1)S(1)} %get-tuple-element.69.early_ref, bf16[2,1664,128]{2,1,0:T(8,128)(2,1)S(1)} %get-tuple-element.70.late_ref, f32[1664,128]{1,0:T(8,128)S(1)} %copy-done, bf16[256,256]{1,0:T(8,128)(2,1)S(1)} %copy-done.1), custom_call_target="tpu_custom_call" | custom-call | flops 490733568 | bytes 1277952 | tf_op jit(solution)/shard_map/response/pallas_call | solution.py:592
  22.0 0.0 collective-permute-done.4.refs_0_
  22.0 3.0 %collective-permute-done.5.refs_1_ = bf16[24,512]{1,0:T(8,128)(2,1)S(1)} collective-permute-done((bf16[24,512]{1,0:T(8,128)(2,1)S(1)}, bf16[24,512]{1,0:T(8,128)(2,1)S(1)}, u32[]{:S(2)}, u32[]{:S(2)}) %collective-permute-start.5) | collective-permute-done | bytes 24608 | tf_op jit(solution)/shard_map/ppermute | solution.py:532
  25.0 0.0 collective-permute-done.6.refs_2_
  25.0 0.0 copy-done.2
  25.1 1.1 %synthesis.1 = bf16[256,128]{1,0:T(8,128)(2,1)} custom-call(f32[24,512]{1,0:T(8,128)S(1)} %get-tuple-element.62.kept_ref, bf16[24,512]{1,0:T(8,128)(2,1)S(1)} %collective-permute-done.4.refs_0_, bf16[24,512]{1,0:T(8,128)(2,1)S(1)} %collective-permute-done.5.refs_1_, bf16[24,512]{1,0:T(8,128)(2,1)S(1)} %collective-permute-done.6.refs_2_, ...), custom_call_target="tpu_custom_call" | custom-call | tf_op jit(solution)/shard_map/synthesis/pallas_call | solution.py:606
  26.2 3.3 %all-to-all-start = ((bf16[32,8,128]{2,1,0:T(8,128)(2,1)}), bf16[32,8,128]{2,1,0:T(8,128)(2,1)S(1)}, u32[]{:S(2)}, u32[]{:S(2)}) async-start(bf16[32,8,128]{2,1,0:T(8,128)(2,1)} %bitcast.4), calls=%async_computation | async-start | bytes 131072 | tf_op jit(solution)/shard_map/all_to_all | solution.py:616
  29.5 0.0 copy-done.3
  29.5 0.1 reshape.23.slots_ref
  29.6 7.3 %all-to-all-done = bf16[32,8,128]{2,1,0:T(8,128)(2,1)S(1)} async-done(((bf16[32,8,128]{2,1,0:T(8,128)(2,1)}), bf16[32,8,128]{2,1,0:T(8,128)(2,1)S(1)}, u32[]{:S(2)}, u32[]{:S(2)}) %all-to-all-start) | async-done | bytes 65568 | tf_op jit(solution)/shard_map/all_to_all | solution.py:616
  36.9 2.6 %inverse.1 = (f32[4,4,4096]{2,1,0:T(4,128)}, f32[4,4,4096]{2,1,0:T(4,128)}) custom-call(bf16[256,128]{1,0:T(8,128)(2,1)S(1)} %bitcast.7, s32[32,12]{1,0:T(8,128)S(1)} %reshape.23.slots_ref, bf16[16,512]{1,0:T(8,128)(2,1)} %constant.22.clone.turn_hbm, bf16[1536,512]{1,0:T(8,128)(2,1)} %constant.23.clone.table_hbm), custom_call_target="tpu_custom_call" | custom-call | tf_op jit(solution)/shard_map/inverse/pallas_call | solution.py:625
Async XLA Ops:
  4.3 7.0 %copy-start = (f32[1664,128]{1,0:T(8,128)S(1)}, f32[1664,128]{1,0:T(8,128)}, u32[]{:S(2)}) copy-start(f32[1664,128]{1,0:T(8,128)} %constant.19.clone.gain_ref) | copy-start | bytes 2555908
  4.3 7.0 %copy-start.1 = (bf16[256,256]{1,0:T(8,128)(2,1)S(1)}, bf16[256,256]{1,0:T(8,128)(2,1)}, u32[]{:S(2)}) copy-start(bf16[256,256]{1,0:T(8,128)(2,1)} %constant.20.clone.order_ref) | copy-start | bytes 393220
  4.3 1.8 %collective-permute-start = (bf16[608,128]{1,0:T(8,128)(2,1)S(1)}, bf16[608,128]{1,0:T(8,128)(2,1)S(1)}, u32[]{:S(2)}, u32[]{:S(2)}) collective-permute-start(bf16[608,128]{1,0:T(8,128)(2,1)S(1)} %get-tuple-element.40.groups_ref), channel_id=1, source_target_pairs={{0,1},{1,0},{2,3},{3,2},{4,5},{5,4},{6,7},{7,6},{8,9},{9,8},{10,11... | collective-permute-start | bytes 466952 | tf_op jit(solution)/shard_map/ppermute | solution.py:532
  7.0 7.6 %collective-permute-start.1 = (bf16[96,512]{1,0:T(8,128)(2,1)S(1)}, bf16[96,512]{1,0:T(8,128)(2,1)S(1)}, u32[]{:S(2)}, u32[]{:S(2)}) collective-permute-start(bf16[96,512]{1,0:T(8,128)(2,1)S(1)} %get-tuple-element.54), channel_id=1, source_target_pairs={{0,2},{1,5},{2,0},{3,7},{4,6},{5,1},{6,4},{7,3},{8,10},{9,13},{10,... | collective-permute-start | bytes 294920 | tf_op jit(solution)/shard_map/ppermute | solution.py:532
  9.7 5.3 %collective-permute-start.2 = (bf16[96,512]{1,0:T(8,128)(2,1)S(1)}, bf16[96,512]{1,0:T(8,128)(2,1)S(1)}, u32[]{:S(2)}, u32[]{:S(2)}) collective-permute-start(bf16[96,512]{1,0:T(8,128)(2,1)S(1)} %get-tuple-element.55), channel_id=1, source_target_pairs={{0,4},{1,3},{2,6},{3,1},{4,0},{5,7},{6,2},{7,5},{8,12},{9,11},{10,... | collective-permute-start | bytes 294920 | tf_op jit(solution)/shard_map/ppermute | solution.py:532
  11.2 5.5 %collective-permute-start.3 = (bf16[96,512]{1,0:T(8,128)(2,1)S(1)}, bf16[96,512]{1,0:T(8,128)(2,1)S(1)}, u32[]{:S(2)}, u32[]{:S(2)}) collective-permute-start(bf16[96,512]{1,0:T(8,128)(2,1)S(1)} %get-tuple-element.56), channel_id=1, source_target_pairs={{0,6},{1,7},{2,4},{3,5},{4,2},{5,3},{6,0},{7,1},{8,14},{9,15},{10,... | collective-permute-start | bytes 294920 | tf_op jit(solution)/shard_map/ppermute | solution.py:532
  14.6 10.5 %copy-start.2 = (bf16[96,96]{1,0:T(8,128)(2,1)S(1)}, bf16[96,96]{1,0:T(8,128)(2,1)}, u32[]{:S(2)}) copy-start(bf16[96,96]{1,0:T(8,128)(2,1)} %constant.21.clone.refs_5_) | copy-start | bytes 55300
  16.8 12.7 %copy-start.3 = (s32[384]{0:T(512)S(1)}, s32[384]{0:T(512)}, u32[]{:S(2)}) copy-start(s32[384]{0:T(512)} %table_hbm.2) | copy-start | bytes 4612
  16.8 5.2 %collective-permute-start.4 = (bf16[24,512]{1,0:T(8,128)(2,1)S(1)}, bf16[24,512]{1,0:T(8,128)(2,1)S(1)}, u32[]{:S(2)}, u32[]{:S(2)}) collective-permute-start(bf16[24,512]{1,0:T(8,128)(2,1)S(1)} %get-tuple-element.66), channel_id=1, source_target_pairs={{0,16},{1,17},{2,18},{3,19},{4,20},{5,21},{6,22},{7,23},{8,24},{9,... | collective-permute-start | bytes 73736 | tf_op jit(solution)/shard_map/ppermute | solution.py:532
  19.4 5.6 %collective-permute-start.5 = (bf16[24,512]{1,0:T(8,128)(2,1)S(1)}, bf16[24,512]{1,0:T(8,128)(2,1)S(1)}, u32[]{:S(2)}, u32[]{:S(2)}) collective-permute-start(bf16[24,512]{1,0:T(8,128)(2,1)S(1)} %get-tuple-element.67), channel_id=1, source_target_pairs={{0,24},{1,25},{2,26},{3,27},{4,28},{5,29},{6,30},{7,31},{8,16},{9,... | collective-permute-start | bytes 73736 | tf_op jit(solution)/shard_map/ppermute | solution.py:532
  20.8 4.3 %collective-permute-start.6 = (bf16[24,512]{1,0:T(8,128)(2,1)S(1)}, bf16[24,512]{1,0:T(8,128)(2,1)S(1)}, u32[]{:S(2)}, u32[]{:S(2)}) collective-permute-start(bf16[24,512]{1,0:T(8,128)(2,1)S(1)} %get-tuple-element.68), channel_id=1, source_target_pairs={{0,8},{1,9},{2,10},{3,11},{4,12},{5,13},{6,14},{7,15},{8,0},{9,1},... | collective-permute-start | bytes 73736 | tf_op jit(solution)/shard_map/ppermute | solution.py:532
  26.2 10.7 %all-to-all-start = ((bf16[32,8,128]{2,1,0:T(8,128)(2,1)}), bf16[32,8,128]{2,1,0:T(8,128)(2,1)S(1)}, u32[]{:S(2)}, u32[]{:S(2)}) async-start(bf16[32,8,128]{2,1,0:T(8,128)(2,1)} %bitcast.4), calls=%async_computation | async-start | bytes 131072 | tf_op jit(solution)/shard_map/all_to_all | solution.py:616

commit v7 on v6

--- a/solution.py
+++ b/solution.py
@@ -172,7 +172,7 @@
         copy.wait()
 
 
-def add_modes(bins, groups, cycles, groups_ref, inner_ref, outer_ref, add):
+def add_modes(bins, groups, cycles, groups_ref, pieces, add):
     pack = 16
     keys = groups_ref[bins * groups :, :].astype(jnp.float32)
     keys = jnp.concatenate([keys[i * pack : (i + 1) * pack, :] for i in range(keys.shape[0] // pack)], 1)
@@ -182,20 +182,39 @@
     half_hot = hot(lax.broadcasted_iota(jnp.int32, (2 * SEGMENTS, groups), 0) == phase)
     phase_hot = jnp.concatenate([half_hot, half_hot], 0)
     deposits = [twice(groups_ref[b * groups : (b + 1) * groups, :]) for b in range(bins)]
-    for start in range(0, inner_ref.shape[0], 2 * CHUNK):
-        rows = slice(start, start + 2 * CHUNK)
-        outer = dot(outer_ref[rows, :], phase_hot)
-        outer_cos, outer_sin = outer[:CHUNK, :], outer[CHUNK:, :]
+    for start, inner_rows, outer_rows in pieces:
+        count = inner_rows.shape[0] // 2
+        outer = dot(outer_rows, phase_hot)
+        outer_cos, outer_sin = outer[:count, :], outer[count:, :]
         for b, deposit in enumerate(deposits):
-            inner = dot(inner_ref[rows, :], deposit, NT)
-            inner_cos, inner_sin = inner[:CHUNK, :], inner[CHUNK:, :]
+            inner = dot(inner_rows, deposit, NT)
+            inner_cos, inner_sin = inner[:count, :], inner[count:, :]
             real = inner_cos * outer_cos - inner_sin * outer_sin
             imag = inner_cos * outer_sin + inner_sin * outer_cos
             both = dot(jnp.concatenate([real, imag], 0).astype(jnp.bfloat16), cycle_hot, NT)
             for part in range(2):
-                value = both[part * CHUNK : (part + 1) * CHUNK, :]
+                value = both[part * count : (part + 1) * count, :]
                 for tile in range(cycles // LANES):
                     add(b * (cycles // LANES) + tile, start + part, value[:, tile * LANES : (tile + 1) * LANES])
+
+
+def all_pieces(inner_ref, outer_ref):
+    for start in range(0, inner_ref.shape[0], 2 * CHUNK):
+        yield start, inner_ref[start : start + 2 * CHUNK, :], outer_ref[start : start + 2 * CHUNK, :]
+
+
+def block_piece(inner_ref, outer_ref, ways, even, odd):
+    count = inner_ref.shape[0] // 2 // ways
+    core = lax.axis_index("core")
+    starts = [block * count // CHUNK * 2 * CHUNK + block * count % CHUNK for block in (even, odd)]
+    tables = []
+    for ref in (inner_ref, outer_ref):
+        parts = []
+        for shift in (0, CHUNK):
+            first = pl.multiple_of(starts[0] + shift + core * (starts[1] - starts[0]), 16)
+            parts.append(ref[pl.ds(first, count), :])
+        tables.append(jnp.concatenate(parts, 0))
+    return [(0, *tables)]
 
 
 def own_kernel(bins, groups, cycles, staged, groups_ref, table_ref, rows_ref, inner_ref, outer_ref, *refs):
@@ -219,7 +238,7 @@
     def add(tile, first, value):
         out_ref.at[tile][pl.ds(first, value.shape[0], stride=2), :] = value
 
-    add_modes(bins, groups, cycles, groups_ref, inner_out, outer_out, add)
+    add_modes(bins, groups, cycles, groups_ref, all_pieces(inner_out, outer_out), add)
     if staged:
         late.wait()
 
@@ -236,21 +255,33 @@
     return [(1, 2), (2, 1), (3, 3)] if ways == 4 else [(i, i) for i in range(1, ways)]
 
 
-def other_kernel(bins, groups, cycles, groups_ref, inner_ref, outer_ref, own_ref, keep_ref, *refs):
-    *send_refs, other_ref = refs
-
+def sum_block(own_ref, other_ref, other_rows, blocks, out_ref):
+    rows = out_ref.shape[0]
+    even, odd = blocks
+    first = even * rows if even == odd else pl.multiple_of((even + lax.axis_index("core") * (odd - even)) * rows, rows)
+    for tile in range(own_ref.shape[0]):
+        value = own_ref[tile, pl.ds(first, rows), :] + other_ref[tile, other_rows or pl.ds(first, rows), :]
+        out_ref[:, tile * LANES : (tile + 1) * LANES] = value.astype(out_ref.dtype)
+
+
+def first_block_kernel(bins, groups, cycles, ways, groups_ref, inner_ref, outer_ref, own_ref, send_ref, other_ref):
     def add(tile, first, value):
         other_ref.at[tile][pl.ds(first, value.shape[0], stride=2), :] = value
 
-    add_modes(bins, groups, cycles, groups_ref, inner_ref, outer_ref, add)
-    rows = keep_ref.shape[0]
-    core = lax.axis_index("core")
-    blocks = [(0, 0)] + send_order(len(send_refs) + 1)
-    for (even, odd), out_ref in zip(blocks, (keep_ref, *send_refs)):
-        first = even * rows if even == odd else pl.multiple_of((even + core * (odd - even)) * rows, rows)
-        for tile in range(own_ref.shape[0]):
-            value = own_ref[tile, pl.ds(first, rows), :] + other_ref[tile, pl.ds(first, rows), :]
-            out_ref[:, tile * LANES : (tile + 1) * LANES] = value.astype(out_ref.dtype)
+    blocks = send_order(ways)[0]
+    add_modes(bins, groups, cycles, groups_ref, block_piece(inner_ref, outer_ref, ways, *blocks), add)
+    sum_block(own_ref, other_ref, slice(0, send_ref.shape[0]), blocks, send_ref)
+
+
+def other_kernel(bins, groups, cycles, ways, groups_ref, inner_ref, outer_ref, own_ref, keep_ref, *refs):
+    *send_refs, other_ref = refs
+
+    def add(tile, first, value):
+        other_ref.at[tile][pl.ds(first, value.shape[0], stride=2), :] = value
+
+    add_modes(bins, groups, cycles, groups_ref, all_pieces(inner_ref, outer_ref), add)
+    for blocks, out_ref in zip([(0, 0)] + send_order(ways)[1:], (keep_ref, *send_refs)):
+        sum_block(own_ref, other_ref, None, blocks, out_ref)
 
 
 def merge_kernel(count, kept_ref, *refs):
@@ -532,7 +563,7 @@
         return lax.ppermute(x, axes, [(i, i ^ masks[i % 2]) for i in range(devices)])
 
     other = swap(deposits, 1)
-    cost = pl.CostEstimate(flops=8 * orders * 256 * bins * live, bytes_accessed=4 * orders * width, transcendentals=0)
+    modes_cost = pl.CostEstimate(flops=8 * orders * 256 * bins * live, bytes_accessed=4 * orders * width, transcendentals=0)
     modes_shape = (width // LANES, orders, LANES)
     own, own_inner, own_outer, *late = pl.pallas_call(
         functools.partial(own_kernel, bins, live, cycles, ahead),
@@ -545,7 +576,7 @@
         ) + (shaped(slots - ahead, degrees, cycles),) * staged,
         scratch_shapes=[pltpu.SemaphoreType.DMA] * staged,
         compiler_params=limits,
-        cost_estimate=cost,
+        cost_estimate=modes_cost,
         name="own_groups",
     )(deposits, *shared, *[in_hbm(legendre)] * staged)
 
@@ -555,7 +586,22 @@
     stages = len(groups_of_bits)
     gain, order = gain_column(degrees), interleave(cycles, cycles_here)
     blocks = devices // 2
-    kernel, inputs = functools.partial(other_kernel, bins, live, cycles), (other, own_inner, own_outer, own)
+    ways = 1 << len(groups_of_bits[0])
+    block_rows = orders // ways
+    first_send = pl.pallas_call(
+        functools.partial(first_block_kernel, bins, live, cycles, ways),
+        in_specs=[vmem] * 4,
+        out_specs=vmem,
+        out_shape=shaped(block_rows, width),
+        scratch_shapes=[pltpu.VMEM((width // LANES, block_rows, LANES), jnp.float32)],
+        compiler_params=limits,
+        name="first_block",
+    )(other, own_inner, own_outer, own)
+    first_send, other = lax.optimization_barrier((first_send, other))
+    even, odd = send_order(ways)[0]
+    low_bit = groups_of_bits[0][0]
+    first_arrived = swap(first_send, even << low_bit, odd << low_bit)
+    kernel, inputs = functools.partial(other_kernel, bins, live, cycles, ways), (other, own_inner, own_outer, own)
     scratch = [pltpu.VMEM(modes_shape, jnp.float32)]
     responses = []
     for stage, bits in enumerate(groups_of_bits):
@@ -565,16 +611,18 @@
         kept, *sends = pl.pallas_call(
             kernel,
             in_specs=[vmem] * len(inputs),
-            out_specs=(vmem,) * ways,
-            out_shape=(shaped(rows_here, width, dtype=jnp.float32),) + (shaped(rows_here, width),) * (ways - 1),
+            out_specs=(vmem,) * (ways if stage else ways - 1),
+            out_shape=(shaped(rows_here, width, dtype=jnp.float32),) + (shaped(rows_here, width),) * (ways - 1 if stage else ways - 2),
             scratch_shapes=scratch,
             compiler_params=limits,
+            cost_estimate=None if stage else modes_cost,
             name="merge" if stage else "other_groups",
         )(*inputs)
         sends, basis = lax.optimization_barrier((sends, basis))
         if stage == 0:
-            order_of = send_order(ways)
-            arrived = [swap(x, even << bits[0], odd << bits[0]) for x, (even, odd) in zip(sends, order_of)]
+            order_of = send_order(ways)[1:]
+            arrived = [first_arrived] + [swap(x, even << bits[0], odd << bits[0]) for x, (even, odd) in zip(sends, order_of)]
+            basis, arrived[0] = lax.optimization_barrier((basis, arrived[0]))
         else:
             line = [2, 3, 1] if ways == 4 else range(ways - 1, 0, -1)
             arrived = [swap(sends[i - 1], i << bits[0]) for i in line]
@@ -582,7 +630,9 @@
         count = last - first
         shape = shaped(count, 2 * cycles, 2 * cycles)
         cost = pl.CostEstimate(
-            flops=6 * count * degrees * cycles * cycles, bytes_accessed=2 * count * degrees * cycles, transcendentals=0
+            flops=6 * count * degrees * cycles if stage == 0 else 6 * count * degrees * cycles * cycles,
+            bytes_accessed=0 if stage == 0 else 2 * count * degrees * cycles,
+            transcendentals=0,
         )
         if staged:
             kernel, scratch = functools.partial(staged_response_kernel, first), []

time: 39.8 us -> 40.6 us (1.020)
  Pallas kernels: 13.9 us -> 14.7 us
    pallas_call x0 -> x1, Pallas kernels: none -> 0.44 us  [per_device(): pl.pallas_call(functools.partial(first_block_kernel, bins, live, cycles,...]
  transfers between devices with their start and end apart: 8 -> 8, of which waited for: 4 -> 5; matrix products, arithmetic and copies ran while one was open for 0% -> 0% of each run, Pallas kernels for 14% -> 17%
where the time goes in v7:
time: 40.6 us; the launch traced here: 40.3 us
  Pallas kernels  14.7 us (36%)
  waiting for transfers between devices  12.5 us (31%)
  starting transfers between devices  12.3 us (30%)
  between operations  0.74 us (2%)
    ppermute x7, starting transfers between devices, swap(): lax.ppermute(x, axes, [(i, i ^ masks[i % 2]) for i in range(devices)])  8.95 us
    all_to_all x1, waiting for transfers between devices, per_device(): lax.all_to_all(outgoing, axes, split_axis=0, concat_axis=0, tiled=True)  7.3 us
    ppermute x7, waiting for transfers between devices, swap(): lax.ppermute(x, axes, [(i, i ^ masks[i % 2]) for i in range(devices)])  5.19 us
    pallas_call x2, Pallas kernels, per_device(): pl.pallas_call(kernel, in_specs=[vmem if staged else hbm] * len(basis) +...  4.31 us
    pallas_call x1, Pallas kernels, per_device(): pl.pallas_call(functools.partial(first_kernel, slots, cycles_here * SEGME...  3.62 us
    all_to_all x1, starting transfers between devices, per_device(): lax.all_to_all(outgoing, axes, split_axis=0, concat_axis=0, tiled=True)  3.35 us
    pallas_call x1, Pallas kernels, per_device(): pl.pallas_call(inverse_kernel, in_specs=[vmem] * 2 + [hbm] * 2, out_specs...  2.61 us
    pallas_call x1, Pallas kernels, per_device(): pl.pallas_call(functools.partial(own_kernel, bins, live, cycles, ahead),...  1.65 us
  transfers between devices with their start and end apart: 8, of which 5 were waited for; matrix products, arithmetic and copies ran while one was open for 0% of the time, Pallas kernels for 17%

profile of v7, /device:TPU:0, one launch (start us, length us, event | category | flops | bytes accessed | tf_op | source)
XLA Modules:
  0.0 40.3 jit_solution(11080069731240039839)
XLA Ops:
  0.6 3.6 %deposit.1 = (bf16[608,128]{1,0:T(8,128)(2,1)S(1)}, s32[1,384]{1,0:T(1,128)S(1)}, bf16[192,384]{1,0:T(8,128)(2,1)S(1)}, bf16[384,512]{1,0:T(8,128)(2,1)S(1)}, bf...) custom-call(bf16[1024,128]{1,0:T(8,128)(2,1)} %bitcast.8, s32[256,128]{1,0:T(8,128)} %bitcast.9, ...), custom_call_target="tpu_custom_call" | custom-call | tf_op jit(solution)/shard_map/deposit/pallas_call | solution.py:540
  4.3 0.5 %collective-permute-start = (bf16[608,128]{1,0:T(8,128)(2,1)S(1)}, bf16[608,128]{1,0:T(8,128)(2,1)S(1)}, u32[]{:S(2)}, u32[]{:S(2)}) collective-permute-start(bf16[608,128]{1,0:T(8,128)(2,1)S(1)} %get-tuple-element.43.groups_ref), channel_id=1, source_target_pairs={{0,1},{1,0},{2,3},{3,2},{4,5},{5,4},{6,7},{7,6},{8,9},{9,8},{10,11... | collective-permute-start | bytes 466952 | tf_op jit(solution)/shard_map/ppermute | solution.py:563
  4.8 0.0 copy-start
  4.8 0.0 copy-start.1
  4.8 1.6 %own_groups.1 = (f32[4,384,128]{2,1,0:T(8,128)S(1)}, bf16[384,256]{1,0:T(8,128)(2,1)S(1)}, bf16[384,128]{1,0:T(8,128)(2,1)S(1)}, bf16[2,1664,128]{2,1,0:T(8,128)(2,1)S(1)}) custom-call(bf16[608,128]{1,0:T(8,128)(2,1)S(1)} %get-tuple-element.43.groups_ref, s32[1,384]{1,0:T(1,128)S(1)} %get-tuple-element.44.table_ref, ...), custom_call_target="tpu_custom_call" | custom-call | flops 452984832 | bytes 786432 | tf_op jit(solution)/shard_map/own_groups/pallas_call | solution.py:568
  6.4 0.0 collective-permute-done.groups_ref
  6.4 0.4 %first_block.1 = bf16[96,512]{1,0:T(8,128)(2,1)S(1)} custom-call(bf16[608,128]{1,0:T(8,128)(2,1)S(1)} %collective-permute-done.groups_ref, bf16[384,256]{1,0:T(8,128)(2,1)S(1)} %get-tuple-element.48.inner_ref, bf16[384,128]{1,0:T(8,128)(2,1)S(1)} %get-tuple-element.49.outer_ref, f32[4,384,128]{2,1,0:T(8,128)S(1)} %get-tuple-element.50.own_ref), custom_call_target="tpu_custom_call" | custom-call | tf_op jit(solution)/shard_map/first_block/pallas_call | solution.py:591
  6.9 2.6 %collective-permute-start.1 = (bf16[96,512]{1,0:T(8,128)(2,1)S(1)}, bf16[96,512]{1,0:T(8,128)(2,1)S(1)}, u32[]{:S(2)}, u32[]{:S(2)}) collective-permute-start(bf16[96,512]{1,0:T(8,128)(2,1)S(1)} %first_block.1), channel_id=1, source_target_pairs={{0,2},{1,5},{2,0},{3,7},{4,6},{5,1},{6,4},{7,3},{8,10},{9,13},{10,... | collective-permute-start | bytes 294920 | tf_op jit(solution)/shard_map/ppermute | solution.py:563
  9.5 0.9 %other_groups.1 = (f32[96,512]{1,0:T(8,128)S(1)}, bf16[96,512]{1,0:T(8,128)(2,1)S(1)}, bf16[96,512]{1,0:T(8,128)(2,1)S(1)}) custom-call(bf16[608,128]{1,0:T(8,128)(2,1)S(1)} %collective-permute-done.groups_ref, bf16[384,256]{1,0:T(8,128)(2,1)S(1)} %get-tuple-element.48.inner_ref, bf16[384,128]{1,0:T(8,128)(2,1)S(1)} %get-tuple-element.49.outer_ref, ...), custom_call_target="tpu_custom_call" | custom-call | flops 452984832 | bytes 786432 | tf_op jit(solution)/shard_map/other_groups/pallas_call | solution.py:611
  10.4 1.6 %collective-permute-start.2 = (bf16[96,512]{1,0:T(8,128)(2,1)S(1)}, bf16[96,512]{1,0:T(8,128)(2,1)S(1)}, u32[]{:S(2)}, u32[]{:S(2)}) collective-permute-start(bf16[96,512]{1,0:T(8,128)(2,1)S(1)} %get-tuple-element.61), channel_id=1, source_target_pairs={{0,4},{1,3},{2,6},{3,1},{4,0},{5,7},{6,2},{7,5},{8,12},{9,11},{10,... | collective-permute-start | bytes 294920 | tf_op jit(solution)/shard_map/ppermute | solution.py:563
  11.9 0.0 collective-permute-start.3
  12.0 0.1 collective-permute-done.1.refs_0_
  12.1 0.0 copy-done
  12.1 0.0 copy-done.1
  12.1 3.3 %response.2.refs_3_ = bf16[9,256,256]{2,1,0:T(8,128)(2,1)S(1)} custom-call(bf16[10,1664,128]{2,1,0:T(8,128)(2,1)S(1)} %get-tuple-element.75.early_ref, bf16[2,1664,128]{2,1,0:T(8,128)(2,1)S(1)} %get-tuple-element.76.late_ref, f32[1664,128]{1,0:T(8,128)S(1)} %copy-done, bf16[256,256]{1,0:T(8,128)(2,1)S(1)} %copy-done.1), custom_call_target="tpu_custom_call" | custom-call | flops 11501568 | tf_op jit(solution)/shard_map/response/pallas_call | solution.py:642
  15.5 0.0 copy-start.2
  15.5 0.4 collective-permute-done.2.refs_1_
  15.8 1.6 %collective-permute-done.3.refs_2_ = bf16[96,512]{1,0:T(8,128)(2,1)S(1)} collective-permute-done((bf16[96,512]{1,0:T(8,128)(2,1)S(1)}, bf16[96,512]{1,0:T(8,128)(2,1)S(1)}, u32[]{:S(2)}, u32[]{:S(2)}) %collective-permute-start.3) | collective-permute-done | bytes 98336 | tf_op jit(solution)/shard_map/ppermute | solution.py:563
  17.5 0.1 merge.1
  17.5 0.0 copy-start.3
  17.5 2.7 %collective-permute-start.4 = (bf16[24,512]{1,0:T(8,128)(2,1)S(1)}, bf16[24,512]{1,0:T(8,128)(2,1)S(1)}, u32[]{:S(2)}, u32[]{:S(2)}) collective-permute-start(bf16[24,512]{1,0:T(8,128)(2,1)S(1)} %get-tuple-element.72), channel_id=1, source_target_pairs={{0,16},{1,17},{2,18},{3,19},{4,20},{5,21},{6,22},{7,23},{8,24},{9,... | collective-permute-start | bytes 73736 | tf_op jit(solution)/shard_map/ppermute | solution.py:563
  20.2 1.3 %collective-permute-start.5 = (bf16[24,512]{1,0:T(8,128)(2,1)S(1)}, bf16[24,512]{1,0:T(8,128)(2,1)S(1)}, u32[]{:S(2)}, u32[]{:S(2)}) collective-permute-start(bf16[24,512]{1,0:T(8,128)(2,1)S(1)} %get-tuple-element.73), channel_id=1, source_target_pairs={{0,24},{1,25},{2,26},{3,27},{4,28},{5,29},{6,30},{7,31},{8,16},{9,... | collective-permute-start | bytes 73736 | tf_op jit(solution)/shard_map/ppermute | solution.py:563
  21.5 0.2 collective-permute-start.6
  21.8 1.0 %response.3.refs_4_ = bf16[3,256,256]{2,1,0:T(8,128)(2,1)S(1)} custom-call(bf16[10,1664,128]{2,1,0:T(8,128)(2,1)S(1)} %get-tuple-element.75.early_ref, bf16[2,1664,128]{2,1,0:T(8,128)(2,1)S(1)} %get-tuple-element.76.late_ref, f32[1664,128]{1,0:T(8,128)S(1)} %copy-done, bf16[256,256]{1,0:T(8,128)(2,1)S(1)} %copy-done.1), custom_call_target="tpu_custom_call" | custom-call | flops 490733568 | bytes 1277952 | tf_op jit(solution)/shard_map/response/pallas_call | solution.py:642
  22.8 0.0 collective-permute-done.4.refs_0_
  22.8 3.0 %collective-permute-done.5.refs_1_ = bf16[24,512]{1,0:T(8,128)(2,1)S(1)} collective-permute-done((bf16[24,512]{1,0:T(8,128)(2,1)S(1)}, bf16[24,512]{1,0:T(8,128)(2,1)S(1)}, u32[]{:S(2)}, u32[]{:S(2)}) %collective-permute-start.5) | collective-permute-done | bytes 24608 | tf_op jit(solution)/shard_map/ppermute | solution.py:563
  25.8 0.0 collective-permute-done.6.refs_2_
  25.8 0.0 copy-done.2
  25.8 1.1 %synthesis.1 = bf16[256,128]{1,0:T(8,128)(2,1)} custom-call(f32[24,512]{1,0:T(8,128)S(1)} %get-tuple-element.68.kept_ref, bf16[24,512]{1,0:T(8,128)(2,1)S(1)} %collective-permute-done.4.refs_0_, bf16[24,512]{1,0:T(8,128)(2,1)S(1)} %collective-permute-done.5.refs_1_, bf16[24,512]{1,0:T(8,128)(2,1)S(1)} %collective-permute-done.6.refs_2_, ...), custom_call_target="tpu_custom_call" | custom-call | tf_op jit(solution)/shard_map/synthesis/pallas_call | solution.py:656
  27.0 3.3 %all-to-all-start = ((bf16[32,8,128]{2,1,0:T(8,128)(2,1)}), bf16[32,8,128]{2,1,0:T(8,128)(2,1)S(1)}, u32[]{:S(2)}, u32[]{:S(2)}) async-start(bf16[32,8,128]{2,1,0:T(8,128)(2,1)} %bitcast.4), calls=%async_computation | async-start | bytes 131072 | tf_op jit(solution)/shard_map/all_to_all | solution.py:666
  30.3 0.0 copy-done.3
  30.3 0.1 reshape.23.slots_ref
  30.4 7.3 %all-to-all-done = bf16[32,8,128]{2,1,0:T(8,128)(2,1)S(1)} async-done(((bf16[32,8,128]{2,1,0:T(8,128)(2,1)}), bf16[32,8,128]{2,1,0:T(8,128)(2,1)S(1)}, u32[]{:S(2)}, u32[]{:S(2)}) %all-to-all-start) | async-done | bytes 65568 | tf_op jit(solution)/shard_map/all_to_all | solution.py:666
  37.7 2.6 %inverse.1 = (f32[4,4,4096]{2,1,0:T(4,128)}, f32[4,4,4096]{2,1,0:T(4,128)}) custom-call(bf16[256,128]{1,0:T(8,128)(2,1)S(1)} %bitcast.7, s32[32,12]{1,0:T(8,128)S(1)} %reshape.23.slots_ref, bf16[16,512]{1,0:T(8,128)(2,1)} %constant.22.clone.turn_hbm, bf16[1536,512]{1,0:T(8,128)(2,1)} %constant.23.clone.table_hbm), custom_call_target="tpu_custom_call" | custom-call | tf_op jit(solution)/shard_map/inverse/pallas_call | solution.py:675
Async XLA Ops:
  4.3 2.2 %collective-permute-start = (bf16[608,128]{1,0:T(8,128)(2,1)S(1)}, bf16[608,128]{1,0:T(8,128)(2,1)S(1)}, u32[]{:S(2)}, u32[]{:S(2)}) collective-permute-start(bf16[608,128]{1,0:T(8,128)(2,1)S(1)} %get-tuple-element.43.groups_ref), channel_id=1, source_target_pairs={{0,1},{1,0},{2,3},{3,2},{4,5},{5,4},{6,7},{7,6},{8,9},{9,8},{10,11... | collective-permute-start | bytes 466952 | tf_op jit(solution)/shard_map/ppermute | solution.py:563
  4.8 7.3 %copy-start = (f32[1664,128]{1,0:T(8,128)S(1)}, f32[1664,128]{1,0:T(8,128)}, u32[]{:S(2)}) copy-start(f32[1664,128]{1,0:T(8,128)} %constant.19.clone.gain_ref) | copy-start | bytes 2555908
  4.8 7.3 %copy-start.1 = (bf16[256,256]{1,0:T(8,128)(2,1)S(1)}, bf16[256,256]{1,0:T(8,128)(2,1)}, u32[]{:S(2)}) copy-start(bf16[256,256]{1,0:T(8,128)(2,1)} %constant.20.clone.order_ref) | copy-start | bytes 393220
  6.9 5.2 %collective-permute-start.1 = (bf16[96,512]{1,0:T(8,128)(2,1)S(1)}, bf16[96,512]{1,0:T(8,128)(2,1)S(1)}, u32[]{:S(2)}, u32[]{:S(2)}) collective-permute-start(bf16[96,512]{1,0:T(8,128)(2,1)S(1)} %first_block.1), channel_id=1, source_target_pairs={{0,2},{1,5},{2,0},{3,7},{4,6},{5,1},{6,4},{7,3},{8,10},{9,13},{10,... | collective-permute-start | bytes 294920 | tf_op jit(solution)/shard_map/ppermute | solution.py:563
  10.4 5.5 %collective-permute-start.2 = (bf16[96,512]{1,0:T(8,128)(2,1)S(1)}, bf16[96,512]{1,0:T(8,128)(2,1)S(1)}, u32[]{:S(2)}, u32[]{:S(2)}) collective-permute-start(bf16[96,512]{1,0:T(8,128)(2,1)S(1)} %get-tuple-element.61), channel_id=1, source_target_pairs={{0,4},{1,3},{2,6},{3,1},{4,0},{5,7},{6,2},{7,5},{8,12},{9,11},{10,... | collective-permute-start | bytes 294920 | tf_op jit(solution)/shard_map/ppermute | solution.py:563
  11.9 5.5 %collective-permute-start.3 = (bf16[96,512]{1,0:T(8,128)(2,1)S(1)}, bf16[96,512]{1,0:T(8,128)(2,1)S(1)}, u32[]{:S(2)}, u32[]{:S(2)}) collective-permute-start(bf16[96,512]{1,0:T(8,128)(2,1)S(1)} %get-tuple-element.62), channel_id=1, source_target_pairs={{0,6},{1,7},{2,4},{3,5},{4,2},{5,3},{6,0},{7,1},{8,14},{9,15},{10,... | collective-permute-start | bytes 294920 | tf_op jit(solution)/shard_map/ppermute | solution.py:563
  15.5 10.4 %copy-start.2 = (bf16[96,96]{1,0:T(8,128)(2,1)S(1)}, bf16[96,96]{1,0:T(8,128)(2,1)}, u32[]{:S(2)}) copy-start(bf16[96,96]{1,0:T(8,128)(2,1)} %constant.21.clone.refs_5_) | copy-start | bytes 55300
  17.5 12.8 %copy-start.3 = (s32[384]{0:T(512)S(1)}, s32[384]{0:T(512)}, u32[]{:S(2)}) copy-start(s32[384]{0:T(512)} %table_hbm.2) | copy-start | bytes 4612
  17.5 5.2 %collective-permute-start.4 = (bf16[24,512]{1,0:T(8,128)(2,1)S(1)}, bf16[24,512]{1,0:T(8,128)(2,1)S(1)}, u32[]{:S(2)}, u32[]{:S(2)}) collective-permute-start(bf16[24,512]{1,0:T(8,128)(2,1)S(1)} %get-tuple-element.72), channel_id=1, source_target_pairs={{0,16},{1,17},{2,18},{3,19},{4,20},{5,21},{6,22},{7,23},{8,24},{9,... | collective-permute-start | bytes 73736 | tf_op jit(solution)/shard_map/ppermute | solution.py:563
  20.2 5.6 %collective-permute-start.5 = (bf16[24,512]{1,0:T(8,128)(2,1)S(1)}, bf16[24,512]{1,0:T(8,128)(2,1)S(1)}, u32[]{:S(2)}, u32[]{:S(2)}) collective-permute-start(bf16[24,512]{1,0:T(8,128)(2,1)S(1)} %get-tuple-element.73), channel_id=1, source_target_pairs={{0,24},{1,25},{2,26},{3,27},{4,28},{5,29},{6,30},{7,31},{8,16},{9,... | collective-permute-start | bytes 73736 | tf_op jit(solution)/shard_map/ppermute | solution.py:563
  21.5 4.3 %collective-permute-start.6 = (bf16[24,512]{1,0:T(8,128)(2,1)S(1)}, bf16[24,512]{1,0:T(8,128)(2,1)S(1)}, u32[]{:S(2)}, u32[]{:S(2)}) collective-permute-start(bf16[24,512]{1,0:T(8,128)(2,1)S(1)} %get-tuple-element.74), channel_id=1, source_target_pairs={{0,8},{1,9},{2,10},{3,11},{4,12},{5,13},{6,14},{7,15},{8,0},{9,1},... | collective-permute-start | bytes 73736 | tf_op jit(solution)/shard_map/ppermute | solution.py:563
  27.0 10.8 %all-to-all-start = ((bf16[32,8,128]{2,1,0:T(8,128)(2,1)}), bf16[32,8,128]{2,1,0:T(8,128)(2,1)S(1)}, u32[]{:S(2)}, u32[]{:S(2)}) async-start(bf16[32,8,128]{2,1,0:T(8,128)(2,1)} %bitcast.4), calls=%async_computation | async-start | bytes 131072 | tf_op jit(solution)/shard_map/all_to_all | solution.py:666

commit v8 on v6

--- a/solution.py
+++ b/solution.py
@@ -233,7 +233,7 @@
 
 
 def send_order(ways):
-    return [(1, 2), (2, 1), (3, 3)] if ways == 4 else [(i, i) for i in range(1, ways)]
+    return [(1, 2), (3, 3), (2, 1)] if ways == 4 else [(i, i) for i in range(1, ways)]
 
 
 def other_kernel(bins, groups, cycles, groups_ref, inner_ref, outer_ref, own_ref, keep_ref, *refs):
@@ -578,7 +578,7 @@
         else:
             line = [2, 3, 1] if ways == 4 else range(ways - 1, 0, -1)
             arrived = [swap(sends[i - 1], i << bits[0]) for i in line]
-        first, last = (min(slots, slots * 2 * k * (2 * stages - k) // (2 * stages * stages)) for k in (stage, stage + 1))
+        first, last = (-(-slots * k * (2 * stages + 1 - k) // (stages * (stages + 1))) for k in (stage, stage + 1))
         count = last - first
         shape = shaped(count, 2 * cycles, 2 * cycles)
         cost = pl.CostEstimate(

time: 39.8 us -> 39.5 us (level)
  waiting for transfers between devices: 12.5 us -> 11 us
  Pallas kernels: 13.9 us -> 14.6 us
  starting transfers between devices: 12.2 us -> 12.7 us
    ppermute x7, waiting for transfers between devices: 5.15 us -> 3.72 us  [swap(): lax.ppermute(x, axes, [(i, i ^ masks[i % 2]) for i in range(devices)])]
    pallas_call x2, Pallas kernels: 4.31 us -> 5.02 us  [per_device(): pl.pallas_call(kernel, in_specs=[vmem if staged else hbm] * len(basis) +...]
    ppermute x7, starting transfers between devices: 8.95 us -> 9.39 us  [swap(): lax.ppermute(x, axes, [(i, i ^ masks[i % 2]) for i in range(devices)])]
  transfers between devices with their start and end apart: 8 -> 8, of which waited for: 4 -> 4; matrix products, arithmetic and copies ran while one was open for 0% -> 0% of each run, Pallas kernels for 14% -> 16%
where the time goes in v8:
time: 39.5 us; the launch traced here: 39.2 us
  Pallas kernels  14.6 us (37%)
  starting transfers between devices  12.7 us (32%)
  waiting for transfers between devices  11 us (28%)
  between operations  0.75 us (2%)
    ppermute x7, starting transfers between devices, swap(): lax.ppermute(x, axes, [(i, i ^ masks[i % 2]) for i in range(devices)])  9.39 us
    all_to_all x1, waiting for transfers between devices, per_device(): lax.all_to_all(outgoing, axes, split_axis=0, concat_axis=0, tiled=True)  7.3 us
    pallas_call x2, Pallas kernels, per_device(): pl.pallas_call(kernel, in_specs=[vmem if staged else hbm] * len(basis) +...  5.02 us
    ppermute x7, waiting for transfers between devices, swap(): lax.ppermute(x, axes, [(i, i ^ masks[i % 2]) for i in range(devices)])  3.72 us
    pallas_call x1, Pallas kernels, per_device(): pl.pallas_call(functools.partial(first_kernel, slots, cycles_here * SEGME...  3.62 us
    all_to_all x1, starting transfers between devices, per_device(): lax.all_to_all(outgoing, axes, split_axis=0, concat_axis=0, tiled=True)  3.28 us
    pallas_call x1, Pallas kernels, per_device(): pl.pallas_call(inverse_kernel, in_specs=[vmem] * 2 + [hbm] * 2, out_specs...  2.61 us
    pallas_call x1, Pallas kernels, per_device(): pl.pallas_call(functools.partial(own_kernel, bins, live, cycles, ahead),...  1.27 us
  transfers between devices with their start and end apart: 8, of which 4 were waited for; matrix products, arithmetic and copies ran while one was open for 0% of the time, Pallas kernels for 16%

profile of v8, /device:TPU:0, one launch (start us, length us, event | category | flops | bytes accessed | tf_op | source)
XLA Modules:
  0.0 39.2 jit_solution(8203130711145817246)
XLA Ops:
  0.6 3.6 %deposit.1 = (bf16[608,128]{1,0:T(8,128)(2,1)S(1)}, s32[1,384]{1,0:T(1,128)S(1)}, bf16[192,384]{1,0:T(8,128)(2,1)S(1)}, bf16[384,512]{1,0:T(8,128)(2,1)S(1)}, bf...) custom-call(bf16[1024,128]{1,0:T(8,128)(2,1)} %bitcast.8, s32[256,128]{1,0:T(8,128)} %bitcast.9, ...), custom_call_target="tpu_custom_call" | custom-call | tf_op jit(solution)/shard_map/deposit/pallas_call | solution.py:509
  4.3 0.0 copy-start
  4.3 0.0 copy-start.1
  4.3 0.5 %collective-permute-start = (bf16[608,128]{1,0:T(8,128)(2,1)S(1)}, bf16[608,128]{1,0:T(8,128)(2,1)S(1)}, u32[]{:S(2)}, u32[]{:S(2)}) collective-permute-start(bf16[608,128]{1,0:T(8,128)(2,1)S(1)} %get-tuple-element.40.groups_ref), channel_id=1, source_target_pairs={{0,1},{1,0},{2,3},{3,2},{4,5},{5,4},{6,7},{7,6},{8,9},{9,8},{10,11... | collective-permute-start | bytes 466952 | tf_op jit(solution)/shard_map/ppermute | solution.py:532
  4.8 1.3 %own_groups.1 = (f32[4,384,128]{2,1,0:T(8,128)S(1)}, bf16[384,256]{1,0:T(8,128)(2,1)S(1)}, bf16[384,128]{1,0:T(8,128)(2,1)S(1)}, bf16[2,1664,128]{2,1,0:T(8,128)(2,1)S(1)}) custom-call(bf16[608,128]{1,0:T(8,128)(2,1)S(1)} %get-tuple-element.40.groups_ref, s32[1,384]{1,0:T(1,128)S(1)} %get-tuple-element.41.table_ref, ...), custom_call_target="tpu_custom_call" | custom-call | flops 452984832 | bytes 786432 | tf_op jit(solution)/shard_map/own_groups/pallas_call | solution.py:537
  6.1 0.0 collective-permute-done.groups_ref
  6.1 0.9 %other_groups.1 = (f32[96,512]{1,0:T(8,128)S(1)}, bf16[96,512]{1,0:T(8,128)(2,1)S(1)}, bf16[96,512]{1,0:T(8,128)(2,1)S(1)}, bf16[96,512]{1,0:T(8,128)(2,1)S(1)}) custom-call(bf16[608,128]{1,0:T(8,128)(2,1)S(1)} %collective-permute-done.groups_ref, bf16[384,256]{1,0:T(8,128)(2,1)S(1)} %get-tuple-element.45.inner_ref, ...), custom_call_target="tpu_custom_call" | custom-call | tf_op jit(solution)/shard_map/other_groups/pallas_call | solution.py:565
  7.0 2.7 %collective-permute-start.1 = (bf16[96,512]{1,0:T(8,128)(2,1)S(1)}, bf16[96,512]{1,0:T(8,128)(2,1)S(1)}, u32[]{:S(2)}, u32[]{:S(2)}) collective-permute-start(bf16[96,512]{1,0:T(8,128)(2,1)S(1)} %get-tuple-element.54), channel_id=1, source_target_pairs={{0,2},{1,5},{2,0},{3,7},{4,6},{5,1},{6,4},{7,3},{8,10},{9,13},{10,... | collective-permute-start | bytes 294920 | tf_op jit(solution)/shard_map/ppermute | solution.py:532
  9.7 1.4 %collective-permute-start.2 = (bf16[96,512]{1,0:T(8,128)(2,1)S(1)}, bf16[96,512]{1,0:T(8,128)(2,1)S(1)}, u32[]{:S(2)}, u32[]{:S(2)}) collective-permute-start(bf16[96,512]{1,0:T(8,128)(2,1)S(1)} %get-tuple-element.55), channel_id=1, source_target_pairs={{0,6},{1,7},{2,4},{3,5},{4,2},{5,3},{6,0},{7,1},{8,14},{9,15},{10,... | collective-permute-start | bytes 294920 | tf_op jit(solution)/shard_map/ppermute | solution.py:532
  11.1 0.1 collective-permute-start.3
  11.2 0.0 copy-done
  11.2 0.0 copy-done.1
  11.2 3.3 %response.2.refs_3_ = bf16[8,256,256]{2,1,0:T(8,128)(2,1)S(1)} custom-call(bf16[10,1664,128]{2,1,0:T(8,128)(2,1)S(1)} %get-tuple-element.69.early_ref, bf16[2,1664,128]{2,1,0:T(8,128)(2,1)S(1)} %get-tuple-element.70.late_ref, f32[1664,128]{1,0:T(8,128)S(1)} %copy-done, bf16[256,256]{1,0:T(8,128)(2,1)S(1)} %copy-done.1), custom_call_target="tpu_custom_call" | custom-call | flops 1308622848 | bytes 3407872 | tf_op jit(solution)/shard_map/response/pallas_call | solution.py:592
  14.5 0.0 copy-start.2
  14.5 0.0 collective-permute-done.1.refs_0_
  14.6 0.9 %collective-permute-done.2.refs_1_ = bf16[96,512]{1,0:T(8,128)(2,1)S(1)} collective-permute-done((bf16[96,512]{1,0:T(8,128)(2,1)S(1)}, bf16[96,512]{1,0:T(8,128)(2,1)S(1)}, u32[]{:S(2)}, u32[]{:S(2)}) %collective-permute-start.2) | collective-permute-done | bytes 98336 | tf_op jit(solution)/shard_map/ppermute | solution.py:532
  15.5 0.5 %collective-permute-done.3.refs_2_ = bf16[96,512]{1,0:T(8,128)(2,1)S(1)} collective-permute-done((bf16[96,512]{1,0:T(8,128)(2,1)S(1)}, bf16[96,512]{1,0:T(8,128)(2,1)S(1)}, u32[]{:S(2)}, u32[]{:S(2)}) %collective-permute-start.3) | collective-permute-done | bytes 98336 | tf_op jit(solution)/shard_map/ppermute | solution.py:532
  16.0 0.1 merge.1
  16.0 0.0 copy-start.3
  16.0 3.1 %collective-permute-start.4 = (bf16[24,512]{1,0:T(8,128)(2,1)S(1)}, bf16[24,512]{1,0:T(8,128)(2,1)S(1)}, u32[]{:S(2)}, u32[]{:S(2)}) collective-permute-start(bf16[24,512]{1,0:T(8,128)(2,1)S(1)} %get-tuple-element.66), channel_id=1, source_target_pairs={{0,16},{1,17},{2,18},{3,19},{4,20},{5,21},{6,22},{7,23},{8,24},{9,... | collective-permute-start | bytes 73736 | tf_op jit(solution)/shard_map/ppermute | solution.py:532
  19.1 1.3 %collective-permute-start.5 = (bf16[24,512]{1,0:T(8,128)(2,1)S(1)}, bf16[24,512]{1,0:T(8,128)(2,1)S(1)}, u32[]{:S(2)}, u32[]{:S(2)}) collective-permute-start(bf16[24,512]{1,0:T(8,128)(2,1)S(1)} %get-tuple-element.67), channel_id=1, source_target_pairs={{0,24},{1,25},{2,26},{3,27},{4,28},{5,29},{6,30},{7,31},{8,16},{9,... | collective-permute-start | bytes 73736 | tf_op jit(solution)/shard_map/ppermute | solution.py:532
  20.5 0.2 collective-permute-start.6
  20.7 1.7 %response.3.refs_4_ = bf16[4,256,256]{2,1,0:T(8,128)(2,1)S(1)} custom-call(bf16[10,1664,128]{2,1,0:T(8,128)(2,1)S(1)} %get-tuple-element.69.early_ref, bf16[2,1664,128]{2,1,0:T(8,128)(2,1)S(1)} %get-tuple-element.70.late_ref, f32[1664,128]{1,0:T(8,128)S(1)} %copy-done, bf16[256,256]{1,0:T(8,128)(2,1)S(1)} %copy-done.1), custom_call_target="tpu_custom_call" | custom-call | flops 654311424 | bytes 1703936 | tf_op jit(solution)/shard_map/response/pallas_call | solution.py:592
  22.4 0.0 collective-permute-done.4.refs_0_
  22.4 2.3 %collective-permute-done.5.refs_1_ = bf16[24,512]{1,0:T(8,128)(2,1)S(1)} collective-permute-done((bf16[24,512]{1,0:T(8,128)(2,1)S(1)}, bf16[24,512]{1,0:T(8,128)(2,1)S(1)}, u32[]{:S(2)}, u32[]{:S(2)}) %collective-permute-start.5) | collective-permute-done | bytes 24608 | tf_op jit(solution)/shard_map/ppermute | solution.py:532
  24.7 0.0 collective-permute-done.6.refs_2_
  24.7 0.0 copy-done.2
  24.7 1.1 %synthesis.1 = bf16[256,128]{1,0:T(8,128)(2,1)} custom-call(f32[24,512]{1,0:T(8,128)S(1)} %get-tuple-element.62.kept_ref, bf16[24,512]{1,0:T(8,128)(2,1)S(1)} %collective-permute-done.4.refs_0_, bf16[24,512]{1,0:T(8,128)(2,1)S(1)} %collective-permute-done.5.refs_1_, bf16[24,512]{1,0:T(8,128)(2,1)S(1)} %collective-permute-done.6.refs_2_, ...), custom_call_target="tpu_custom_call" | custom-call | tf_op jit(solution)/shard_map/synthesis/pallas_call | solution.py:606
  25.9 3.3 %all-to-all-start = ((bf16[32,8,128]{2,1,0:T(8,128)(2,1)}), bf16[32,8,128]{2,1,0:T(8,128)(2,1)S(1)}, u32[]{:S(2)}, u32[]{:S(2)}) async-start(bf16[32,8,128]{2,1,0:T(8,128)(2,1)} %bitcast.4), calls=%async_computation | async-start | bytes 131072 | tf_op jit(solution)/shard_map/all_to_all | solution.py:616
  29.2 0.0 copy-done.3
  29.2 0.1 reshape.23.slots_ref
  29.3 7.3 %all-to-all-done = bf16[32,8,128]{2,1,0:T(8,128)(2,1)S(1)} async-done(((bf16[32,8,128]{2,1,0:T(8,128)(2,1)}), bf16[32,8,128]{2,1,0:T(8,128)(2,1)S(1)}, u32[]{:S(2)}, u32[]{:S(2)}) %all-to-all-start) | async-done | bytes 65568 | tf_op jit(solution)/shard_map/all_to_all | solution.py:616
  36.6 2.6 %inverse.1 = (f32[4,4,4096]{2,1,0:T(4,128)}, f32[4,4,4096]{2,1,0:T(4,128)}) custom-call(bf16[256,128]{1,0:T(8,128)(2,1)S(1)} %bitcast.7, s32[32,12]{1,0:T(8,128)S(1)} %reshape.23.slots_ref, bf16[16,512]{1,0:T(8,128)(2,1)} %constant.22.clone.turn_hbm, bf16[1536,512]{1,0:T(8,128)(2,1)} %constant.23.clone.table_hbm), custom_call_target="tpu_custom_call" | custom-call | tf_op jit(solution)/shard_map/inverse/pallas_call | solution.py:625
Async XLA Ops:
  4.3 7.0 %copy-start = (f32[1664,128]{1,0:T(8,128)S(1)}, f32[1664,128]{1,0:T(8,128)}, u32[]{:S(2)}) copy-start(f32[1664,128]{1,0:T(8,128)} %constant.19.clone.gain_ref) | copy-start | bytes 2555908
  4.3 7.0 %copy-start.1 = (bf16[256,256]{1,0:T(8,128)(2,1)S(1)}, bf16[256,256]{1,0:T(8,128)(2,1)}, u32[]{:S(2)}) copy-start(bf16[256,256]{1,0:T(8,128)(2,1)} %constant.20.clone.order_ref) | copy-start | bytes 393220
  4.3 1.8 %collective-permute-start = (bf16[608,128]{1,0:T(8,128)(2,1)S(1)}, bf16[608,128]{1,0:T(8,128)(2,1)S(1)}, u32[]{:S(2)}, u32[]{:S(2)}) collective-permute-start(bf16[608,128]{1,0:T(8,128)(2,1)S(1)} %get-tuple-element.40.groups_ref), channel_id=1, source_target_pairs={{0,1},{1,0},{2,3},{3,2},{4,5},{5,4},{6,7},{7,6},{8,9},{9,8},{10,11... | collective-permute-start | bytes 466952 | tf_op jit(solution)/shard_map/ppermute | solution.py:532
  7.0 7.5 %collective-permute-start.1 = (bf16[96,512]{1,0:T(8,128)(2,1)S(1)}, bf16[96,512]{1,0:T(8,128)(2,1)S(1)}, u32[]{:S(2)}, u32[]{:S(2)}) collective-permute-start(bf16[96,512]{1,0:T(8,128)(2,1)S(1)} %get-tuple-element.54), channel_id=1, source_target_pairs={{0,2},{1,5},{2,0},{3,7},{4,6},{5,1},{6,4},{7,3},{8,10},{9,13},{10,... | collective-permute-start | bytes 294920 | tf_op jit(solution)/shard_map/ppermute | solution.py:532
  9.7 5.8 %collective-permute-start.2 = (bf16[96,512]{1,0:T(8,128)(2,1)S(1)}, bf16[96,512]{1,0:T(8,128)(2,1)S(1)}, u32[]{:S(2)}, u32[]{:S(2)}) collective-permute-start(bf16[96,512]{1,0:T(8,128)(2,1)S(1)} %get-tuple-element.55), channel_id=1, source_target_pairs={{0,6},{1,7},{2,4},{3,5},{4,2},{5,3},{6,0},{7,1},{8,14},{9,15},{10,... | collective-permute-start | bytes 294920 | tf_op jit(solution)/shard_map/ppermute | solution.py:532
  11.1 4.9 %collective-permute-start.3 = (bf16[96,512]{1,0:T(8,128)(2,1)S(1)}, bf16[96,512]{1,0:T(8,128)(2,1)S(1)}, u32[]{:S(2)}, u32[]{:S(2)}) collective-permute-start(bf16[96,512]{1,0:T(8,128)(2,1)S(1)} %get-tuple-element.56), channel_id=1, source_target_pairs={{0,4},{1,3},{2,6},{3,1},{4,0},{5,7},{6,2},{7,5},{8,12},{9,11},{10,... | collective-permute-start | bytes 294920 | tf_op jit(solution)/shard_map/ppermute | solution.py:532
  14.5 10.2 %copy-start.2 = (bf16[96,96]{1,0:T(8,128)(2,1)S(1)}, bf16[96,96]{1,0:T(8,128)(2,1)}, u32[]{:S(2)}) copy-start(bf16[96,96]{1,0:T(8,128)(2,1)} %constant.21.clone.refs_5_) | copy-start | bytes 55300
  16.0 13.2 %copy-start.3 = (s32[384]{0:T(512)S(1)}, s32[384]{0:T(512)}, u32[]{:S(2)}) copy-start(s32[384]{0:T(512)} %table_hbm.2) | copy-start | bytes 4612
  16.0 6.4 %collective-permute-start.4 = (bf16[24,512]{1,0:T(8,128)(2,1)S(1)}, bf16[24,512]{1,0:T(8,128)(2,1)S(1)}, u32[]{:S(2)}, u32[]{:S(2)}) collective-permute-start(bf16[24,512]{1,0:T(8,128)(2,1)S(1)} %get-tuple-element.66), channel_id=1, source_target_pairs={{0,16},{1,17},{2,18},{3,19},{4,20},{5,21},{6,22},{7,23},{8,24},{9,... | collective-permute-start | bytes 73736 | tf_op jit(solution)/shard_map/ppermute | solution.py:532
  19.1 5.6 %collective-permute-start.5 = (bf16[24,512]{1,0:T(8,128)(2,1)S(1)}, bf16[24,512]{1,0:T(8,128)(2,1)S(1)}, u32[]{:S(2)}, u32[]{:S(2)}) collective-permute-start(bf16[24,512]{1,0:T(8,128)(2,1)S(1)} %get-tuple-element.67), channel_id=1, source_target_pairs={{0,24},{1,25},{2,26},{3,27},{4,28},{5,29},{6,30},{7,31},{8,16},{9,... | collective-permute-start | bytes 73736 | tf_op jit(solution)/shard_map/ppermute | solution.py:532
  20.5 4.3 %collective-permute-start.6 = (bf16[24,512]{1,0:T(8,128)(2,1)S(1)}, bf16[24,512]{1,0:T(8,128)(2,1)S(1)}, u32[]{:S(2)}, u32[]{:S(2)}) collective-permute-start(bf16[24,512]{1,0:T(8,128)(2,1)S(1)} %get-tuple-element.68), channel_id=1, source_target_pairs={{0,8},{1,9},{2,10},{3,11},{4,12},{5,13},{6,14},{7,15},{8,0},{9,1},... | collective-permute-start | bytes 73736 | tf_op jit(solution)/shard_map/ppermute | solution.py:532
  25.9 10.7 %all-to-all-start = ((bf16[32,8,128]{2,1,0:T(8,128)(2,1)}), bf16[32,8,128]{2,1,0:T(8,128)(2,1)S(1)}, u32[]{:S(2)}, u32[]{:S(2)}) async-start(bf16[32,8,128]{2,1,0:T(8,128)(2,1)} %bitcast.4), calls=%async_computation | async-start | bytes 131072 | tf_op jit(solution)/shard_map/all_to_all | solution.py:616

commit v9 on v8

--- a/solution.py
+++ b/solution.py
@@ -576,7 +576,7 @@
             order_of = send_order(ways)
             arrived = [swap(x, even << bits[0], odd << bits[0]) for x, (even, odd) in zip(sends, order_of)]
         else:
-            line = [2, 3, 1] if ways == 4 else range(ways - 1, 0, -1)
+            line = range(ways - 1, 0, -1)
             arrived = [swap(sends[i - 1], i << bits[0]) for i in line]
         first, last = (-(-slots * k * (2 * stages + 1 - k) // (stages * (stages + 1))) for k in (stage, stage + 1))
         count = last - first

time: 39.5 us -> 39.6 us (level)
  no operation moved by 1% of the time
where the time goes in v9:
time: 39.6 us; the launch traced here: 39.3 us
  Pallas kernels  14.6 us (37%)
  starting transfers between devices  12.7 us (32%)
  waiting for transfers between devices  11.1 us (28%)
  between operations  0.75 us (2%)
    ppermute x7, starting transfers between devices, swap(): lax.ppermute(x, axes, [(i, i ^ masks[i % 2]) for i in range(devices)])  9.47 us
    all_to_all x1, waiting for transfers between devices, per_device(): lax.all_to_all(outgoing, axes, split_axis=0, concat_axis=0, tiled=True)  7.3 us
    pallas_call x2, Pallas kernels, per_device(): pl.pallas_call(kernel, in_specs=[vmem if staged else hbm] * len(basis) +...  5.02 us
    ppermute x7, waiting for transfers between devices, swap(): lax.ppermute(x, axes, [(i, i ^ masks[i % 2]) for i in range(devices)])  3.76 us
    pallas_call x1, Pallas kernels, per_device(): pl.pallas_call(functools.partial(first_kernel, slots, cycles_here * SEGME...  3.62 us
    all_to_all x1, starting transfers between devices, per_device(): lax.all_to_all(outgoing, axes, split_axis=0, concat_axis=0, tiled=True)  3.28 us
    pallas_call x1, Pallas kernels, per_device(): pl.pallas_call(inverse_kernel, in_specs=[vmem] * 2 + [hbm] * 2, out_specs...  2.61 us
    pallas_call x1, Pallas kernels, per_device(): pl.pallas_call(functools.partial(own_kernel, bins, live, cycles, ahead),...  1.27 us
  transfers between devices with their start and end apart: 8, of which 4 were waited for; matrix products, arithmetic and copies ran while one was open for 0% of the time, Pallas kernels for 16%

profile of v9, /device:TPU:0, one launch (start us, length us, event | category | flops | bytes accessed | tf_op | source)
XLA Modules:
  0.0 39.3 jit_solution(17973231619253391209)
XLA Ops:
  0.6 3.6 %deposit.1 = (bf16[608,128]{1,0:T(8,128)(2,1)S(1)}, s32[1,384]{1,0:T(1,128)S(1)}, bf16[192,384]{1,0:T(8,128)(2,1)S(1)}, bf16[384,512]{1,0:T(8,128)(2,1)S(1)}, bf...) custom-call(bf16[1024,128]{1,0:T(8,128)(2,1)} %bitcast.8, s32[256,128]{1,0:T(8,128)} %bitcast.9, ...), custom_call_target="tpu_custom_call" | custom-call | tf_op jit(solution)/shard_map/deposit/pallas_call | solution.py:509
  4.3 0.0 copy-start
  4.3 0.0 copy-start.1
  4.3 0.5 %collective-permute-start = (bf16[608,128]{1,0:T(8,128)(2,1)S(1)}, bf16[608,128]{1,0:T(8,128)(2,1)S(1)}, u32[]{:S(2)}, u32[]{:S(2)}) collective-permute-start(bf16[608,128]{1,0:T(8,128)(2,1)S(1)} %get-tuple-element.40.groups_ref), channel_id=1, source_target_pairs={{0,1},{1,0},{2,3},{3,2},{4,5},{5,4},{6,7},{7,6},{8,9},{9,8},{10,11... | collective-permute-start | bytes 466952 | tf_op jit(solution)/shard_map/ppermute | solution.py:532
  4.8 1.3 %own_groups.1 = (f32[4,384,128]{2,1,0:T(8,128)S(1)}, bf16[384,256]{1,0:T(8,128)(2,1)S(1)}, bf16[384,128]{1,0:T(8,128)(2,1)S(1)}, bf16[2,1664,128]{2,1,0:T(8,128)(2,1)S(1)}) custom-call(bf16[608,128]{1,0:T(8,128)(2,1)S(1)} %get-tuple-element.40.groups_ref, s32[1,384]{1,0:T(1,128)S(1)} %get-tuple-element.41.table_ref, ...), custom_call_target="tpu_custom_call" | custom-call | flops 452984832 | bytes 786432 | tf_op jit(solution)/shard_map/own_groups/pallas_call | solution.py:537
  6.1 0.0 collective-permute-done.groups_ref
  6.1 0.9 %other_groups.1 = (f32[96,512]{1,0:T(8,128)S(1)}, bf16[96,512]{1,0:T(8,128)(2,1)S(1)}, bf16[96,512]{1,0:T(8,128)(2,1)S(1)}, bf16[96,512]{1,0:T(8,128)(2,1)S(1)}) custom-call(bf16[608,128]{1,0:T(8,128)(2,1)S(1)} %collective-permute-done.groups_ref, bf16[384,256]{1,0:T(8,128)(2,1)S(1)} %get-tuple-element.45.inner_ref, ...), custom_call_target="tpu_custom_call" | custom-call | tf_op jit(solution)/shard_map/other_groups/pallas_call | solution.py:565
  7.0 2.7 %collective-permute-start.1 = (bf16[96,512]{1,0:T(8,128)(2,1)S(1)}, bf16[96,512]{1,0:T(8,128)(2,1)S(1)}, u32[]{:S(2)}, u32[]{:S(2)}) collective-permute-start(bf16[96,512]{1,0:T(8,128)(2,1)S(1)} %get-tuple-element.54), channel_id=1, source_target_pairs={{0,2},{1,5},{2,0},{3,7},{4,6},{5,1},{6,4},{7,3},{8,10},{9,13},{10,... | collective-permute-start | bytes 294920 | tf_op jit(solution)/shard_map/ppermute | solution.py:532
  9.7 1.4 %collective-permute-start.2 = (bf16[96,512]{1,0:T(8,128)(2,1)S(1)}, bf16[96,512]{1,0:T(8,128)(2,1)S(1)}, u32[]{:S(2)}, u32[]{:S(2)}) collective-permute-start(bf16[96,512]{1,0:T(8,128)(2,1)S(1)} %get-tuple-element.55), channel_id=1, source_target_pairs={{0,6},{1,7},{2,4},{3,5},{4,2},{5,3},{6,0},{7,1},{8,14},{9,15},{10,... | collective-permute-start | bytes 294920 | tf_op jit(solution)/shard_map/ppermute | solution.py:532
  11.1 0.1 collective-permute-start.3
  11.2 0.0 copy-done
  11.2 0.0 copy-done.1
  11.2 3.3 %response.2.refs_3_ = bf16[8,256,256]{2,1,0:T(8,128)(2,1)S(1)} custom-call(bf16[10,1664,128]{2,1,0:T(8,128)(2,1)S(1)} %get-tuple-element.69.early_ref, bf16[2,1664,128]{2,1,0:T(8,128)(2,1)S(1)} %get-tuple-element.70.late_ref, f32[1664,128]{1,0:T(8,128)S(1)} %copy-done, bf16[256,256]{1,0:T(8,128)(2,1)S(1)} %copy-done.1), custom_call_target="tpu_custom_call" | custom-call | flops 1308622848 | bytes 3407872 | tf_op jit(solution)/shard_map/response/pallas_call | solution.py:592
  14.5 0.0 copy-start.2
  14.5 0.0 collective-permute-done.1.refs_0_
  14.6 0.9 %collective-permute-done.2.refs_1_ = bf16[96,512]{1,0:T(8,128)(2,1)S(1)} collective-permute-done((bf16[96,512]{1,0:T(8,128)(2,1)S(1)}, bf16[96,512]{1,0:T(8,128)(2,1)S(1)}, u32[]{:S(2)}, u32[]{:S(2)}) %collective-permute-start.2) | collective-permute-done | bytes 98336 | tf_op jit(solution)/shard_map/ppermute | solution.py:532
  15.5 0.5 %collective-permute-done.3.refs_2_ = bf16[96,512]{1,0:T(8,128)(2,1)S(1)} collective-permute-done((bf16[96,512]{1,0:T(8,128)(2,1)S(1)}, bf16[96,512]{1,0:T(8,128)(2,1)S(1)}, u32[]{:S(2)}, u32[]{:S(2)}) %collective-permute-start.3) | collective-permute-done | bytes 98336 | tf_op jit(solution)/shard_map/ppermute | solution.py:532
  16.0 0.1 merge.1
  16.0 0.0 copy-start.3
  16.0 4.1 %collective-permute-start.4 = (bf16[24,512]{1,0:T(8,128)(2,1)S(1)}, bf16[24,512]{1,0:T(8,128)(2,1)S(1)}, u32[]{:S(2)}, u32[]{:S(2)}) collective-permute-start(bf16[24,512]{1,0:T(8,128)(2,1)S(1)} %get-tuple-element.66), channel_id=1, source_target_pairs={{0,24},{1,25},{2,26},{3,27},{4,28},{5,29},{6,30},{7,31},{8,16},{9,... | collective-permute-start | bytes 73736 | tf_op jit(solution)/shard_map/ppermute | solution.py:532
  20.1 0.0 collective-permute-start.5
  20.1 0.6 %collective-permute-start.6 = (bf16[24,512]{1,0:T(8,128)(2,1)S(1)}, bf16[24,512]{1,0:T(8,128)(2,1)S(1)}, u32[]{:S(2)}, u32[]{:S(2)}) collective-permute-start(bf16[24,512]{1,0:T(8,128)(2,1)S(1)} %get-tuple-element.68), channel_id=1, source_target_pairs={{0,8},{1,9},{2,10},{3,11},{4,12},{5,13},{6,14},{7,15},{8,0},{9,1},... | collective-permute-start | bytes 73736 | tf_op jit(solution)/shard_map/ppermute | solution.py:532
  20.8 1.7 %response.3.refs_4_ = bf16[4,256,256]{2,1,0:T(8,128)(2,1)S(1)} custom-call(bf16[10,1664,128]{2,1,0:T(8,128)(2,1)S(1)} %get-tuple-element.69.early_ref, bf16[2,1664,128]{2,1,0:T(8,128)(2,1)S(1)} %get-tuple-element.70.late_ref, f32[1664,128]{1,0:T(8,128)S(1)} %copy-done, bf16[256,256]{1,0:T(8,128)(2,1)S(1)} %copy-done.1), custom_call_target="tpu_custom_call" | custom-call | flops 654311424 | bytes 1703936 | tf_op jit(solution)/shard_map/response/pallas_call | solution.py:592
  22.5 0.0 collective-permute-done.4.refs_0_
  22.5 2.3 %collective-permute-done.5.refs_1_ = bf16[24,512]{1,0:T(8,128)(2,1)S(1)} collective-permute-done((bf16[24,512]{1,0:T(8,128)(2,1)S(1)}, bf16[24,512]{1,0:T(8,128)(2,1)S(1)}, u32[]{:S(2)}, u32[]{:S(2)}) %collective-permute-start.5) | collective-permute-done | bytes 24608 | tf_op jit(solution)/shard_map/ppermute | solution.py:532
  24.9 0.0 collective-permute-done.6.refs_2_
  24.9 0.0 copy-done.2
  24.9 1.1 %synthesis.1 = bf16[256,128]{1,0:T(8,128)(2,1)} custom-call(f32[24,512]{1,0:T(8,128)S(1)} %get-tuple-element.62.kept_ref, bf16[24,512]{1,0:T(8,128)(2,1)S(1)} %collective-permute-done.4.refs_0_, bf16[24,512]{1,0:T(8,128)(2,1)S(1)} %collective-permute-done.5.refs_1_, bf16[24,512]{1,0:T(8,128)(2,1)S(1)} %collective-permute-done.6.refs_2_, ...), custom_call_target="tpu_custom_call" | custom-call | tf_op jit(solution)/shard_map/synthesis/pallas_call | solution.py:606
  26.0 3.3 %all-to-all-start = ((bf16[32,8,128]{2,1,0:T(8,128)(2,1)}), bf16[32,8,128]{2,1,0:T(8,128)(2,1)S(1)}, u32[]{:S(2)}, u32[]{:S(2)}) async-start(bf16[32,8,128]{2,1,0:T(8,128)(2,1)} %bitcast.4), calls=%async_computation | async-start | bytes 131072 | tf_op jit(solution)/shard_map/all_to_all | solution.py:616
  29.3 0.0 copy-done.3
  29.3 0.1 reshape.23.slots_ref
  29.4 7.3 %all-to-all-done = bf16[32,8,128]{2,1,0:T(8,128)(2,1)S(1)} async-done(((bf16[32,8,128]{2,1,0:T(8,128)(2,1)}), bf16[32,8,128]{2,1,0:T(8,128)(2,1)S(1)}, u32[]{:S(2)}, u32[]{:S(2)}) %all-to-all-start) | async-done | bytes 65568 | tf_op jit(solution)/shard_map/all_to_all | solution.py:616
  36.7 2.6 %inverse.1 = (f32[4,4,4096]{2,1,0:T(4,128)}, f32[4,4,4096]{2,1,0:T(4,128)}) custom-call(bf16[256,128]{1,0:T(8,128)(2,1)S(1)} %bitcast.7, s32[32,12]{1,0:T(8,128)S(1)} %reshape.23.slots_ref, bf16[16,512]{1,0:T(8,128)(2,1)} %constant.22.clone.turn_hbm, bf16[1536,512]{1,0:T(8,128)(2,1)} %constant.23.clone.table_hbm), custom_call_target="tpu_custom_call" | custom-call | tf_op jit(solution)/shard_map/inverse/pallas_call | solution.py:625
Async XLA Ops:
  4.3 7.0 %copy-start = (f32[1664,128]{1,0:T(8,128)S(1)}, f32[1664,128]{1,0:T(8,128)}, u32[]{:S(2)}) copy-start(f32[1664,128]{1,0:T(8,128)} %constant.19.clone.gain_ref) | copy-start | bytes 2555908
  4.3 7.0 %copy-start.1 = (bf16[256,256]{1,0:T(8,128)(2,1)S(1)}, bf16[256,256]{1,0:T(8,128)(2,1)}, u32[]{:S(2)}) copy-start(bf16[256,256]{1,0:T(8,128)(2,1)} %constant.20.clone.order_ref) | copy-start | bytes 393220
  4.3 1.8 %collective-permute-start = (bf16[608,128]{1,0:T(8,128)(2,1)S(1)}, bf16[608,128]{1,0:T(8,128)(2,1)S(1)}, u32[]{:S(2)}, u32[]{:S(2)}) collective-permute-start(bf16[608,128]{1,0:T(8,128)(2,1)S(1)} %get-tuple-element.40.groups_ref), channel_id=1, source_target_pairs={{0,1},{1,0},{2,3},{3,2},{4,5},{5,4},{6,7},{7,6},{8,9},{9,8},{10,11... | collective-permute-start | bytes 466952 | tf_op jit(solution)/shard_map/ppermute | solution.py:532
  7.0 7.5 %collective-permute-start.1 = (bf16[96,512]{1,0:T(8,128)(2,1)S(1)}, bf16[96,512]{1,0:T(8,128)(2,1)S(1)}, u32[]{:S(2)}, u32[]{:S(2)}) collective-permute-start(bf16[96,512]{1,0:T(8,128)(2,1)S(1)} %get-tuple-element.54), channel_id=1, source_target_pairs={{0,2},{1,5},{2,0},{3,7},{4,6},{5,1},{6,4},{7,3},{8,10},{9,13},{10,... | collective-permute-start | bytes 294920 | tf_op jit(solution)/shard_map/ppermute | solution.py:532
  9.7 5.8 %collective-permute-start.2 = (bf16[96,512]{1,0:T(8,128)(2,1)S(1)}, bf16[96,512]{1,0:T(8,128)(2,1)S(1)}, u32[]{:S(2)}, u32[]{:S(2)}) collective-permute-start(bf16[96,512]{1,0:T(8,128)(2,1)S(1)} %get-tuple-element.55), channel_id=1, source_target_pairs={{0,6},{1,7},{2,4},{3,5},{4,2},{5,3},{6,0},{7,1},{8,14},{9,15},{10,... | collective-permute-start | bytes 294920 | tf_op jit(solution)/shard_map/ppermute | solution.py:532
  11.1 4.9 %collective-permute-start.3 = (bf16[96,512]{1,0:T(8,128)(2,1)S(1)}, bf16[96,512]{1,0:T(8,128)(2,1)S(1)}, u32[]{:S(2)}, u32[]{:S(2)}) collective-permute-start(bf16[96,512]{1,0:T(8,128)(2,1)S(1)} %get-tuple-element.56), channel_id=1, source_target_pairs={{0,4},{1,3},{2,6},{3,1},{4,0},{5,7},{6,2},{7,5},{8,12},{9,11},{10,... | collective-permute-start | bytes 294920 | tf_op jit(solution)/shard_map/ppermute | solution.py:532
  14.5 10.3 %copy-start.2 = (bf16[96,96]{1,0:T(8,128)(2,1)S(1)}, bf16[96,96]{1,0:T(8,128)(2,1)}, u32[]{:S(2)}) copy-start(bf16[96,96]{1,0:T(8,128)(2,1)} %constant.21.clone.refs_5_) | copy-start | bytes 55300
  16.0 13.3 %copy-start.3 = (s32[384]{0:T(512)S(1)}, s32[384]{0:T(512)}, u32[]{:S(2)}) copy-start(s32[384]{0:T(512)} %table_hbm.2) | copy-start | bytes 4612
  16.0 6.5 %collective-permute-start.4 = (bf16[24,512]{1,0:T(8,128)(2,1)S(1)}, bf16[24,512]{1,0:T(8,128)(2,1)S(1)}, u32[]{:S(2)}, u32[]{:S(2)}) collective-permute-start(bf16[24,512]{1,0:T(8,128)(2,1)S(1)} %get-tuple-element.66), channel_id=1, source_target_pairs={{0,24},{1,25},{2,26},{3,27},{4,28},{5,29},{6,30},{7,31},{8,16},{9,... | collective-permute-start | bytes 73736 | tf_op jit(solution)/shard_map/ppermute | solution.py:532
  20.1 4.7 %collective-permute-start.5 = (bf16[24,512]{1,0:T(8,128)(2,1)S(1)}, bf16[24,512]{1,0:T(8,128)(2,1)S(1)}, u32[]{:S(2)}, u32[]{:S(2)}) collective-permute-start(bf16[24,512]{1,0:T(8,128)(2,1)S(1)} %get-tuple-element.67), channel_id=1, source_target_pairs={{0,16},{1,17},{2,18},{3,19},{4,20},{5,21},{6,22},{7,23},{8,24},{9,... | collective-permute-start | bytes 73736 | tf_op jit(solution)/shard_map/ppermute | solution.py:532
  20.1 4.7 %collective-permute-start.6 = (bf16[24,512]{1,0:T(8,128)(2,1)S(1)}, bf16[24,512]{1,0:T(8,128)(2,1)S(1)}, u32[]{:S(2)}, u32[]{:S(2)}) collective-permute-start(bf16[24,512]{1,0:T(8,128)(2,1)S(1)} %get-tuple-element.68), channel_id=1, source_target_pairs={{0,8},{1,9},{2,10},{3,11},{4,12},{5,13},{6,14},{7,15},{8,0},{9,1},... | collective-permute-start | bytes 73736 | tf_op jit(solution)/shard_map/ppermute | solution.py:532
  26.0 10.7 %all-to-all-start = ((bf16[32,8,128]{2,1,0:T(8,128)(2,1)}), bf16[32,8,128]{2,1,0:T(8,128)(2,1)S(1)}, u32[]{:S(2)}, u32[]{:S(2)}) async-start(bf16[32,8,128]{2,1,0:T(8,128)(2,1)} %bitcast.4), calls=%async_computation | async-start | bytes 131072 | tf_op jit(solution)/shard_map/all_to_all | solution.py:616

commit v10 on v8

--- a/solution.py
+++ b/solution.py
@@ -578,7 +578,7 @@
         else:
             line = [2, 3, 1] if ways == 4 else range(ways - 1, 0, -1)
             arrived = [swap(sends[i - 1], i << bits[0]) for i in line]
-        first, last = (-(-slots * k * (2 * stages + 1 - k) // (stages * (stages + 1))) for k in (stage, stage + 1))
+        first, last = (slots * k * (4 * stages - k) // (stages * (3 * stages)) for k in (stage, stage + 1))
         count = last - first
         shape = shaped(count, 2 * cycles, 2 * cycles)
         cost = pl.CostEstimate(

time: 39.5 us -> 39.5 us (level)
  waiting for transfers between devices: 11 us -> 11.6 us
  Pallas kernels: 14.6 us -> 14.1 us
    ppermute x7, waiting for transfers between devices: 3.72 us -> 4.26 us  [swap(): lax.ppermute(x, axes, [(i, i ^ masks[i % 2]) for i in range(devices)])]
    pallas_call x2, Pallas kernels: 5.02 us -> 4.49 us  [per_device(): pl.pallas_call(kernel, in_specs=[vmem if staged else hbm] * len(basis) +...]
  transfers between devices with their start and end apart: 8 -> 8, of which waited for: 4 -> 5; matrix products, arithmetic and copies ran while one was open for 0% -> 0% of each run, Pallas kernels for 16% -> 15%
where the time goes in v10:
time: 39.5 us; the launch traced here: 39.2 us
  Pallas kernels  14.1 us (36%)
  starting transfers between devices  12.7 us (32%)
  waiting for transfers between devices  11.6 us (29%)
  between operations  0.75 us (2%)
    ppermute x7, starting transfers between devices, swap(): lax.ppermute(x, axes, [(i, i ^ masks[i % 2]) for i in range(devices)])  9.39 us
    all_to_all x1, waiting for transfers between devices, per_device(): lax.all_to_all(outgoing, axes, split_axis=0, concat_axis=0, tiled=True)  7.3 us
    pallas_call x2, Pallas kernels, per_device(): pl.pallas_call(kernel, in_specs=[vmem if staged else hbm] * len(basis) +...  4.49 us
    ppermute x7, waiting for transfers between devices, swap(): lax.ppermute(x, axes, [(i, i ^ masks[i % 2]) for i in range(devices)])  4.26 us
    pallas_call x1, Pallas kernels, per_device(): pl.pallas_call(functools.partial(first_kernel, slots, cycles_here * SEGME...  3.62 us
    all_to_all x1, starting transfers between devices, per_device(): lax.all_to_all(outgoing, axes, split_axis=0, concat_axis=0, tiled=True)  3.29 us
    pallas_call x1, Pallas kernels, per_device(): pl.pallas_call(inverse_kernel, in_specs=[vmem] * 2 + [hbm] * 2, out_specs...  2.61 us
    pallas_call x1, Pallas kernels, per_device(): pl.pallas_call(functools.partial(own_kernel, bins, live, cycles, ahead),...  1.27 us
  transfers between devices with their start and end apart: 8, of which 5 were waited for; matrix products, arithmetic and copies ran while one was open for 0% of the time, Pallas kernels for 15%

profile of v10, /device:TPU:0, one launch (start us, length us, event | category | flops | bytes accessed | tf_op | source)
XLA Modules:
  0.0 39.2 jit_solution(3239835477981108136)
XLA Ops:
  0.6 3.6 %deposit.1 = (bf16[608,128]{1,0:T(8,128)(2,1)S(1)}, s32[1,384]{1,0:T(1,128)S(1)}, bf16[192,384]{1,0:T(8,128)(2,1)S(1)}, bf16[384,512]{1,0:T(8,128)(2,1)S(1)}, bf...) custom-call(bf16[1024,128]{1,0:T(8,128)(2,1)} %bitcast.8, s32[256,128]{1,0:T(8,128)} %bitcast.9, ...), custom_call_target="tpu_custom_call" | custom-call | tf_op jit(solution)/shard_map/deposit/pallas_call | solution.py:509
  4.3 0.0 copy-start
  4.3 0.0 copy-start.1
  4.3 0.5 %collective-permute-start = (bf16[608,128]{1,0:T(8,128)(2,1)S(1)}, bf16[608,128]{1,0:T(8,128)(2,1)S(1)}, u32[]{:S(2)}, u32[]{:S(2)}) collective-permute-start(bf16[608,128]{1,0:T(8,128)(2,1)S(1)} %get-tuple-element.40.groups_ref), channel_id=1, source_target_pairs={{0,1},{1,0},{2,3},{3,2},{4,5},{5,4},{6,7},{7,6},{8,9},{9,8},{10,11... | collective-permute-start | bytes 466952 | tf_op jit(solution)/shard_map/ppermute | solution.py:532
  4.8 1.3 %own_groups.1 = (f32[4,384,128]{2,1,0:T(8,128)S(1)}, bf16[384,256]{1,0:T(8,128)(2,1)S(1)}, bf16[384,128]{1,0:T(8,128)(2,1)S(1)}, bf16[2,1664,128]{2,1,0:T(8,128)(2,1)S(1)}) custom-call(bf16[608,128]{1,0:T(8,128)(2,1)S(1)} %get-tuple-element.40.groups_ref, s32[1,384]{1,0:T(1,128)S(1)} %get-tuple-element.41.table_ref, ...), custom_call_target="tpu_custom_call" | custom-call | flops 452984832 | bytes 786432 | tf_op jit(solution)/shard_map/own_groups/pallas_call | solution.py:537
  6.1 0.0 collective-permute-done.groups_ref
  6.1 0.9 %other_groups.1 = (f32[96,512]{1,0:T(8,128)S(1)}, bf16[96,512]{1,0:T(8,128)(2,1)S(1)}, bf16[96,512]{1,0:T(8,128)(2,1)S(1)}, bf16[96,512]{1,0:T(8,128)(2,1)S(1)}) custom-call(bf16[608,128]{1,0:T(8,128)(2,1)S(1)} %collective-permute-done.groups_ref, bf16[384,256]{1,0:T(8,128)(2,1)S(1)} %get-tuple-element.45.inner_ref, ...), custom_call_target="tpu_custom_call" | custom-call | tf_op jit(solution)/shard_map/other_groups/pallas_call | solution.py:565
  7.0 2.7 %collective-permute-start.1 = (bf16[96,512]{1,0:T(8,128)(2,1)S(1)}, bf16[96,512]{1,0:T(8,128)(2,1)S(1)}, u32[]{:S(2)}, u32[]{:S(2)}) collective-permute-start(bf16[96,512]{1,0:T(8,128)(2,1)S(1)} %get-tuple-element.54), channel_id=1, source_target_pairs={{0,2},{1,5},{2,0},{3,7},{4,6},{5,1},{6,4},{7,3},{8,10},{9,13},{10,... | collective-permute-start | bytes 294920 | tf_op jit(solution)/shard_map/ppermute | solution.py:532
  9.7 1.4 %collective-permute-start.2 = (bf16[96,512]{1,0:T(8,128)(2,1)S(1)}, bf16[96,512]{1,0:T(8,128)(2,1)S(1)}, u32[]{:S(2)}, u32[]{:S(2)}) collective-permute-start(bf16[96,512]{1,0:T(8,128)(2,1)S(1)} %get-tuple-element.55), channel_id=1, source_target_pairs={{0,6},{1,7},{2,4},{3,5},{4,2},{5,3},{6,0},{7,1},{8,14},{9,15},{10,... | collective-permute-start | bytes 294920 | tf_op jit(solution)/shard_map/ppermute | solution.py:532
  11.1 0.1 collective-permute-start.3
  11.2 0.0 copy-done
  11.2 0.0 copy-done.1
  11.2 2.6 %response.2.refs_3_ = bf16[7,256,256]{2,1,0:T(8,128)(2,1)S(1)} custom-call(bf16[10,1664,128]{2,1,0:T(8,128)(2,1)S(1)} %get-tuple-element.69.early_ref, bf16[2,1664,128]{2,1,0:T(8,128)(2,1)S(1)} %get-tuple-element.70.late_ref, f32[1664,128]{1,0:T(8,128)S(1)} %copy-done, bf16[256,256]{1,0:T(8,128)(2,1)S(1)} %copy-done.1), custom_call_target="tpu_custom_call" | custom-call | flops 1145044992 | bytes 2981888 | tf_op jit(solution)/shard_map/response/pallas_call | solution.py:592
  13.9 0.0 copy-start.2
  13.9 0.2 collective-permute-done.1.refs_0_
  14.1 1.4 %collective-permute-done.2.refs_1_ = bf16[96,512]{1,0:T(8,128)(2,1)S(1)} collective-permute-done((bf16[96,512]{1,0:T(8,128)(2,1)S(1)}, bf16[96,512]{1,0:T(8,128)(2,1)S(1)}, u32[]{:S(2)}, u32[]{:S(2)}) %collective-permute-start.2) | collective-permute-done | bytes 98336 | tf_op jit(solution)/shard_map/ppermute | solution.py:532
  15.5 0.5 %collective-permute-done.3.refs_2_ = bf16[96,512]{1,0:T(8,128)(2,1)S(1)} collective-permute-done((bf16[96,512]{1,0:T(8,128)(2,1)S(1)}, bf16[96,512]{1,0:T(8,128)(2,1)S(1)}, u32[]{:S(2)}, u32[]{:S(2)}) %collective-permute-start.3) | collective-permute-done | bytes 98336 | tf_op jit(solution)/shard_map/ppermute | solution.py:532
  16.0 0.1 merge.1
  16.0 0.0 copy-start.3
  16.0 3.1 %collective-permute-start.4 = (bf16[24,512]{1,0:T(8,128)(2,1)S(1)}, bf16[24,512]{1,0:T(8,128)(2,1)S(1)}, u32[]{:S(2)}, u32[]{:S(2)}) collective-permute-start(bf16[24,512]{1,0:T(8,128)(2,1)S(1)} %get-tuple-element.66), channel_id=1, source_target_pairs={{0,16},{1,17},{2,18},{3,19},{4,20},{5,21},{6,22},{7,23},{8,24},{9,... | collective-permute-start | bytes 73736 | tf_op jit(solution)/shard_map/ppermute | solution.py:532
  19.1 1.3 %collective-permute-start.5 = (bf16[24,512]{1,0:T(8,128)(2,1)S(1)}, bf16[24,512]{1,0:T(8,128)(2,1)S(1)}, u32[]{:S(2)}, u32[]{:S(2)}) collective-permute-start(bf16[24,512]{1,0:T(8,128)(2,1)S(1)} %get-tuple-element.67), channel_id=1, source_target_pairs={{0,24},{1,25},{2,26},{3,27},{4,28},{5,29},{6,30},{7,31},{8,16},{9,... | collective-permute-start | bytes 73736 | tf_op jit(solution)/shard_map/ppermute | solution.py:532
  20.5 0.2 collective-permute-start.6
  20.7 1.8 %response.3.refs_4_ = bf16[5,256,256]{2,1,0:T(8,128)(2,1)S(1)} custom-call(bf16[10,1664,128]{2,1,0:T(8,128)(2,1)S(1)} %get-tuple-element.69.early_ref, bf16[2,1664,128]{2,1,0:T(8,128)(2,1)S(1)} %get-tuple-element.70.late_ref, f32[1664,128]{1,0:T(8,128)S(1)} %copy-done, bf16[256,256]{1,0:T(8,128)(2,1)S(1)} %copy-done.1), custom_call_target="tpu_custom_call" | custom-call | flops 817889280 | bytes 2129920 | tf_op jit(solution)/shard_map/response/pallas_call | solution.py:592
  22.5 0.0 collective-permute-done.4.refs_0_
  22.6 2.2 %collective-permute-done.5.refs_1_ = bf16[24,512]{1,0:T(8,128)(2,1)S(1)} collective-permute-done((bf16[24,512]{1,0:T(8,128)(2,1)S(1)}, bf16[24,512]{1,0:T(8,128)(2,1)S(1)}, u32[]{:S(2)}, u32[]{:S(2)}) %collective-permute-start.5) | collective-permute-done | bytes 24608 | tf_op jit(solution)/shard_map/ppermute | solution.py:532
  24.7 0.0 collective-permute-done.6.refs_2_
  24.7 0.0 copy-done.2
  24.7 1.1 %synthesis.1 = bf16[256,128]{1,0:T(8,128)(2,1)} custom-call(f32[24,512]{1,0:T(8,128)S(1)} %get-tuple-element.62.kept_ref, bf16[24,512]{1,0:T(8,128)(2,1)S(1)} %collective-permute-done.4.refs_0_, bf16[24,512]{1,0:T(8,128)(2,1)S(1)} %collective-permute-done.5.refs_1_, bf16[24,512]{1,0:T(8,128)(2,1)S(1)} %collective-permute-done.6.refs_2_, ...), custom_call_target="tpu_custom_call" | custom-call | tf_op jit(solution)/shard_map/synthesis/pallas_call | solution.py:606
  25.9 3.3 %all-to-all-start = ((bf16[32,8,128]{2,1,0:T(8,128)(2,1)}), bf16[32,8,128]{2,1,0:T(8,128)(2,1)S(1)}, u32[]{:S(2)}, u32[]{:S(2)}) async-start(bf16[32,8,128]{2,1,0:T(8,128)(2,1)} %bitcast.4), calls=%async_computation | async-start | bytes 131072 | tf_op jit(solution)/shard_map/all_to_all | solution.py:616
  29.2 0.0 copy-done.3
  29.2 0.1 reshape.23.slots_ref
  29.3 7.3 %all-to-all-done = bf16[32,8,128]{2,1,0:T(8,128)(2,1)S(1)} async-done(((bf16[32,8,128]{2,1,0:T(8,128)(2,1)}), bf16[32,8,128]{2,1,0:T(8,128)(2,1)S(1)}, u32[]{:S(2)}, u32[]{:S(2)}) %all-to-all-start) | async-done | bytes 65568 | tf_op jit(solution)/shard_map/all_to_all | solution.py:616
  36.6 2.6 %inverse.1 = (f32[4,4,4096]{2,1,0:T(4,128)}, f32[4,4,4096]{2,1,0:T(4,128)}) custom-call(bf16[256,128]{1,0:T(8,128)(2,1)S(1)} %bitcast.7, s32[32,12]{1,0:T(8,128)S(1)} %reshape.23.slots_ref, bf16[16,512]{1,0:T(8,128)(2,1)} %constant.22.clone.turn_hbm, bf16[1536,512]{1,0:T(8,128)(2,1)} %constant.23.clone.table_hbm), custom_call_target="tpu_custom_call" | custom-call | tf_op jit(solution)/shard_map/inverse/pallas_call | solution.py:625
Async XLA Ops:
  4.3 7.0 %copy-start = (f32[1664,128]{1,0:T(8,128)S(1)}, f32[1664,128]{1,0:T(8,128)}, u32[]{:S(2)}) copy-start(f32[1664,128]{1,0:T(8,128)} %constant.19.clone.gain_ref) | copy-start | bytes 2555908
  4.3 7.0 %copy-start.1 = (bf16[256,256]{1,0:T(8,128)(2,1)S(1)}, bf16[256,256]{1,0:T(8,128)(2,1)}, u32[]{:S(2)}) copy-start(bf16[256,256]{1,0:T(8,128)(2,1)} %constant.20.clone.order_ref) | copy-start | bytes 393220
  4.3 1.8 %collective-permute-start = (bf16[608,128]{1,0:T(8,128)(2,1)S(1)}, bf16[608,128]{1,0:T(8,128)(2,1)S(1)}, u32[]{:S(2)}, u32[]{:S(2)}) collective-permute-start(bf16[608,128]{1,0:T(8,128)(2,1)S(1)} %get-tuple-element.40.groups_ref), channel_id=1, source_target_pairs={{0,1},{1,0},{2,3},{3,2},{4,5},{5,4},{6,7},{7,6},{8,9},{9,8},{10,11... | collective-permute-start | bytes 466952 | tf_op jit(solution)/shard_map/ppermute | solution.py:532
  7.0 7.1 %collective-permute-start.1 = (bf16[96,512]{1,0:T(8,128)(2,1)S(1)}, bf16[96,512]{1,0:T(8,128)(2,1)S(1)}, u32[]{:S(2)}, u32[]{:S(2)}) collective-permute-start(bf16[96,512]{1,0:T(8,128)(2,1)S(1)} %get-tuple-element.54), channel_id=1, source_target_pairs={{0,2},{1,5},{2,0},{3,7},{4,6},{5,1},{6,4},{7,3},{8,10},{9,13},{10,... | collective-permute-start | bytes 294920 | tf_op jit(solution)/shard_map/ppermute | solution.py:532
  9.7 5.8 %collective-permute-start.2 = (bf16[96,512]{1,0:T(8,128)(2,1)S(1)}, bf16[96,512]{1,0:T(8,128)(2,1)S(1)}, u32[]{:S(2)}, u32[]{:S(2)}) collective-permute-start(bf16[96,512]{1,0:T(8,128)(2,1)S(1)} %get-tuple-element.55), channel_id=1, source_target_pairs={{0,6},{1,7},{2,4},{3,5},{4,2},{5,3},{6,0},{7,1},{8,14},{9,15},{10,... | collective-permute-start | bytes 294920 | tf_op jit(solution)/shard_map/ppermute | solution.py:532
  11.1 4.9 %collective-permute-start.3 = (bf16[96,512]{1,0:T(8,128)(2,1)S(1)}, bf16[96,512]{1,0:T(8,128)(2,1)S(1)}, u32[]{:S(2)}, u32[]{:S(2)}) collective-permute-start(bf16[96,512]{1,0:T(8,128)(2,1)S(1)} %get-tuple-element.56), channel_id=1, source_target_pairs={{0,4},{1,3},{2,6},{3,1},{4,0},{5,7},{6,2},{7,5},{8,12},{9,11},{10,... | collective-permute-start | bytes 294920 | tf_op jit(solution)/shard_map/ppermute | solution.py:532
  13.9 10.9 %copy-start.2 = (bf16[96,96]{1,0:T(8,128)(2,1)S(1)}, bf16[96,96]{1,0:T(8,128)(2,1)}, u32[]{:S(2)}) copy-start(bf16[96,96]{1,0:T(8,128)(2,1)} %constant.21.clone.refs_5_) | copy-start | bytes 55300
  16.0 13.2 %copy-start.3 = (s32[384]{0:T(512)S(1)}, s32[384]{0:T(512)}, u32[]{:S(2)}) copy-start(s32[384]{0:T(512)} %table_hbm.2) | copy-start | bytes 4612
  16.0 6.5 %collective-permute-start.4 = (bf16[24,512]{1,0:T(8,128)(2,1)S(1)}, bf16[24,512]{1,0:T(8,128)(2,1)S(1)}, u32[]{:S(2)}, u32[]{:S(2)}) collective-permute-start(bf16[24,512]{1,0:T(8,128)(2,1)S(1)} %get-tuple-element.66), channel_id=1, source_target_pairs={{0,16},{1,17},{2,18},{3,19},{4,20},{5,21},{6,22},{7,23},{8,24},{9,... | collective-permute-start | bytes 73736 | tf_op jit(solution)/shard_map/ppermute | solution.py:532
  19.1 5.6 %collective-permute-start.5 = (bf16[24,512]{1,0:T(8,128)(2,1)S(1)}, bf16[24,512]{1,0:T(8,128)(2,1)S(1)}, u32[]{:S(2)}, u32[]{:S(2)}) collective-permute-start(bf16[24,512]{1,0:T(8,128)(2,1)S(1)} %get-tuple-element.67), channel_id=1, source_target_pairs={{0,24},{1,25},{2,26},{3,27},{4,28},{5,29},{6,30},{7,31},{8,16},{9,... | collective-permute-start | bytes 73736 | tf_op jit(solution)/shard_map/ppermute | solution.py:532
  20.5 4.3 %collective-permute-start.6 = (bf16[24,512]{1,0:T(8,128)(2,1)S(1)}, bf16[24,512]{1,0:T(8,128)(2,1)S(1)}, u32[]{:S(2)}, u32[]{:S(2)}) collective-permute-start(bf16[24,512]{1,0:T(8,128)(2,1)S(1)} %get-tuple-element.68), channel_id=1, source_target_pairs={{0,8},{1,9},{2,10},{3,11},{4,12},{5,13},{6,14},{7,15},{8,0},{9,1},... | collective-permute-start | bytes 73736 | tf_op jit(solution)/shard_map/ppermute | solution.py:532
  25.9 10.7 %all-to-all-start = ((bf16[32,8,128]{2,1,0:T(8,128)(2,1)}), bf16[32,8,128]{2,1,0:T(8,128)(2,1)S(1)}, u32[]{:S(2)}, u32[]{:S(2)}) async-start(bf16[32,8,128]{2,1,0:T(8,128)(2,1)} %bitcast.4), calls=%async_computation | async-start | bytes 131072 | tf_op jit(solution)/shard_map/all_to_all | solution.py:616
